TPU v7x, 32 devices: a whole 2x2x4 slice. The times are simulated.
32 devices in a mesh: dp: 8 (over y, x, core), mp: 4 (over z).
Axes of the slice: x: 2, y: 2, z: 4, core: 2. Of those that a mesh axis runs over, the one named last changes fastest.
Arguments:
- tokens: bfloat16 [8192, 2304], P(('dp', 'mp')), may hold values from -6 to 6
- attn_gain: float32 [2304], replicated, may hold values from 0.25 to 1.75
- mlp_gain: float32 [2304], replicated, may hold values from 0.25 to 1.75
- w_query: bfloat16 [2304, 2304], P('dp', 'mp'), may hold values from -0.125 to 0.125
- w_key: bfloat16 [2304, 2304], P('dp', 'mp'), may hold values from -0.125 to 0.125
- w_value: bfloat16 [2304, 2304], P('dp', 'mp'), may hold values from -0.125 to 0.125
- w_out: bfloat16 [2304, 2304], P('mp', 'dp'), may hold values from -12 to 12
- w_gate: bfloat16 [2304, 5760], P('dp', 'mp'), may hold values from -0.125 to 0.125
- w_up: bfloat16 [2304, 5760], P('dp', 'mp'), may hold values from -0.125 to 0.125
- w_down: bfloat16 [5760, 2304], P('mp', 'dp'), may hold values from -0.5 to 0.5
- prefix: int32 [8], P('dp'), may hold values from 102 to 512, as said below
- out_grad: bfloat16 [8192, 2304], P(('dp', 'mp')), may hold values from -6 to 6
Outputs:
- block_out: bfloat16 [8192, 2304], P(('dp', 'mp'))
- input_grad: bfloat16 [8192, 2304], P(('dp', 'mp'))
- grad_w_query: float32 [2304, 2304], P('dp', 'mp')
- grad_w_key: float32 [2304, 2304], P('dp', 'mp')
- grad_w_value: float32 [2304, 2304], P('dp', 'mp')
- grad_w_out: float32 [2304, 2304], P('mp', 'dp')
- grad_w_gate: float32 [2304, 5760], P('dp', 'mp')
- grad_w_up: float32 [2304, 5760], P('dp', 'mp')
- grad_w_down: float32 [5760, 2304], P('mp', 'dp')
- grad_attn_gain: float32 [2304], replicated
- grad_mlp_gain: float32 [2304], replicated
Inputs may be any that keep to these rules, and one draw needn't show every extreme that they name: prefix[s] is the number of leading tokens of sequence s that all its tokens attend to; later tokens attend causally. Both ends of the range occur in every draw.
All inputs are finite; a program needn't handle non-finite values.
Results may differ from a plain program's by a relative error of at most 0.019.
Values may be sent and summed in bfloat16 or wider, within the bound.
No kernel may reach another device: no remote copies, remote signals or barrier semaphores. Data moves between devices by JAX's collectives and lax.ppermute only.
A program may use at most 256 MiB of HBM per device.

v0:
```python
from functools import partial

import jax
import jax.numpy as jnp
from jax import lax
from jax.sharding import PartitionSpec as P

HD = 64
LEN = 1024
SEQ_DP = 1


EPSILON = 1e-05
BRANCH = 1.4 / 40**0.5
MASKED = -1e30


def normalize(value, gain):
    factor = lax.rsqrt(jnp.mean(value * value, axis=-1, keepdims=True) + EPSILON)
    return value * factor * gain


def normalize_back(value, gain, incoming):
    factor = lax.rsqrt(jnp.mean(value * value, axis=-1, keepdims=True) + EPSILON)
    normed = value * factor
    scaled = incoming * gain
    inner = jnp.mean(scaled * normed, axis=-1, keepdims=True)
    return (factor * (scaled - normed * inner), jnp.sum(incoming * normed, axis=0))


def angle_tables(length, width):
    half_width = width // 2
    places = jnp.arange(length, dtype=jnp.float32)
    rates = 10000.0 ** (-jnp.arange(half_width, dtype=jnp.float32) * 2.0 / width)
    angles = places[:, None] * rates[None, :]
    cosine = jnp.concatenate([jnp.cos(angles), jnp.cos(angles)], axis=-1)[:, None, :]
    sine = jnp.concatenate([jnp.sin(angles), jnp.sin(angles)], axis=-1)[:, None, :]
    return (cosine, sine)


def turned(value):
    half_width = value.shape[-1] // 2
    return jnp.concatenate([-value[..., half_width:], value[..., :half_width]], axis=-1)


def rotate_flat(flat):
    shaped = flat.reshape(SEQ_DP, LEN, -1, HD)
    cosine, sine = angle_tables(LEN, HD)
    return (shaped * cosine + turned(shaped) * sine).reshape(flat.shape)


def rotate_back_flat(flat):
    shaped = flat.reshape(SEQ_DP, LEN, -1, HD)
    cosine, sine = angle_tables(LEN, HD)
    return (shaped * cosine - turned(shaped * sine)).reshape(flat.shape)


def to_heads(flat):
    return flat.reshape(SEQ_DP, LEN, -1, HD).transpose(0, 2, 1, 3)


def from_heads(split):
    return split.transpose(0, 2, 1, 3).reshape(SEQ_DP * LEN, -1)


def matmul(left, right):
    return jnp.dot(left, right, preferred_element_type=jnp.float32)


def inner_rows(left, right):
    return lax.dot_general(
        left, right, (((0,), (0,)), ((), ())), preferred_element_type=jnp.float32
    )


def outer_cols(left, right):
    return lax.dot_general(
        left, right, (((1,), (1,)), ((), ())), preferred_element_type=jnp.float32
    )


def key_limits(block_rows):
    limits = []
    for block in range(LEN // block_rows):
        limits.append(LEN)
    return limits


def block_scores(query_block, key_rows, offset, limit):
    raw_scores = outer_cols(query_block, key_rows) * HD ** (-0.5)
    row_place = offset + lax.broadcasted_iota(jnp.int32, raw_scores.shape, 0)
    col_place = lax.broadcasted_iota(jnp.int32, raw_scores.shape, 1)
    visible = (col_place < limit) | (col_place <= row_place)
    return jnp.where(visible, raw_scores, MASKED)


def head_forward(limit, inputs):
    queries, key_rows, value_rows = inputs
    block_rows = min(512, LEN)
    outputs = []
    log_totals = []
    for block, reach in enumerate(key_limits(block_rows)):
        offset = block * block_rows
        scores = block_scores(
            queries[offset : offset + block_rows], key_rows[:reach], offset, limit
        )
        maximum = jnp.max(scores, axis=-1, keepdims=True)
        weights = jnp.exp(scores - maximum)
        totals = jnp.sum(weights, axis=-1, keepdims=True)
        chances = (weights / totals).astype(jnp.bfloat16)
        outputs.append(matmul(chances, value_rows[:reach]).astype(jnp.bfloat16))
        log_totals.append((maximum + jnp.log(totals))[:, 0])
    return (jnp.concatenate(outputs, axis=0), jnp.concatenate(log_totals, axis=0))


def head_backward(limit, inputs):
    queries, key_rows, value_rows, grad_out, log_total = inputs
    block_rows = min(512, LEN)
    scale = HD ** (-0.5)
    grad_query_parts = []
    grad_keys = jnp.zeros(key_rows.shape, jnp.float32)
    grad_values = jnp.zeros(value_rows.shape, jnp.float32)
    for block, reach in enumerate(key_limits(block_rows)):
        offset = block * block_rows
        query_block = queries[offset : offset + block_rows]
        grad_block = grad_out[offset : offset + block_rows]
        scores = block_scores(query_block, key_rows[:reach], offset, limit)
        chances = jnp.exp(scores - log_total[offset : offset + block_rows, None])
        rounded = chances.astype(jnp.bfloat16)
        grad_chance = outer_cols(grad_block, value_rows[:reach])
        inner = jnp.sum(chances * grad_chance, axis=-1, keepdims=True)
        grad_scores = (chances * (grad_chance - inner)).astype(jnp.bfloat16)
        grad_query_parts.append(matmul(grad_scores, key_rows[:reach]) * scale)
        grad_keys = grad_keys.at[:reach].add(inner_rows(grad_scores, query_block) * scale)
        grad_values = grad_values.at[:reach].add(inner_rows(rounded, grad_block))
    return (jnp.concatenate(grad_query_parts, axis=0), grad_keys, grad_values)


def attend(queries, key_rows, value_rows, prefix):

    def one_sequence(inputs):
        query_seq, key_seq, value_seq, limit = inputs
        return lax.map(partial(head_forward, limit), (query_seq, key_seq, value_seq))

    return lax.map(one_sequence, (queries, key_rows, value_rows, prefix))


def attend_back(queries, key_rows, value_rows, grad_out, log_total, prefix):

    def one_sequence(inputs):
        query_seq, key_seq, value_seq, grad_seq, total_seq, limit = inputs
        return lax.map(
            partial(head_backward, limit), (query_seq, key_seq, value_seq, grad_seq, total_seq)
        )

    return lax.map(one_sequence, (queries, key_rows, value_rows, grad_out, log_total, prefix))


def gather_rows(value):
    return lax.all_gather(value, "mp", axis=0, tiled=True)


def scatter_rows(value):
    return lax.psum_scatter(value, "mp", scatter_dimension=0, tiled=True)


def gather_grads(value):
    return lax.all_gather(value, "mp", axis=0, tiled=True)


def scatter_grads(value):
    return lax.psum_scatter(value, "mp", scatter_dimension=0, tiled=True)


def body(
    tokens,
    attn_gain,
    mlp_gain,
    w_query,
    w_key,
    w_value,
    w_out,
    w_gate,
    w_up,
    w_down,
    prefix,
    out_grad,
):
    inputs = tokens.astype(jnp.float32)
    normed_one = normalize(inputs, attn_gain).astype(jnp.bfloat16)
    whole_one = gather_rows(normed_one)
    row_count = whole_one.shape[0]
    width = whole_one.shape[1]
    pieces = (
        lax.all_gather(w_query, "dp", axis=0, tiled=True),
        lax.all_gather(w_key, "dp", axis=0, tiled=True),
        lax.all_gather(w_value, "dp", axis=0, tiled=True),
    )
    columns = whole_one
    query_pre = matmul(columns, pieces[0])
    key_pre = matmul(columns, pieces[1])
    value_pre = matmul(columns, pieces[2])
    queries = to_heads(rotate_flat(query_pre).astype(jnp.bfloat16))
    key_rows = to_heads(rotate_flat(key_pre).astype(jnp.bfloat16))
    value_rows = to_heads(value_pre.astype(jnp.bfloat16))
    attended_heads, log_total = attend(queries, key_rows, value_rows, prefix)
    attended = from_heads(attended_heads)
    out_whole = lax.all_gather(w_out, "dp", axis=1, tiled=True)
    attn_sum = scatter_rows(matmul(attended, out_whole))
    middle = inputs + BRANCH * attn_sum
    normed_two = normalize(middle, mlp_gain).astype(jnp.bfloat16)
    whole_two = gather_rows(normed_two)
    zeros_hidden = jnp.zeros((row_count, w_gate.shape[1]), jnp.float32)
    pieces = (
        lax.all_gather(w_gate, "dp", axis=0, tiled=True),
        lax.all_gather(w_up, "dp", axis=0, tiled=True),
    )
    columns = lax.slice_in_dim(whole_two, 0, pieces[0].shape[0], axis=1)
    gate_act = zeros_hidden + matmul(columns, pieces[0])
    up_act = zeros_hidden + matmul(columns, pieces[1])
    sigmoid_gate = jax.nn.sigmoid(gate_act)
    hidden = (gate_act * sigmoid_gate * up_act).astype(jnp.bfloat16)
    down_whole = lax.all_gather(w_down, "dp", axis=1, tiled=True)
    mlp_sum = scatter_rows(matmul(hidden, down_whole))
    block_out = middle + BRANCH * mlp_sum
    grad_result = out_grad.astype(jnp.float32)
    grad_mlp = gather_grads((BRANCH * grad_result).astype(jnp.bfloat16))
    grad_hidden = outer_cols(grad_mlp, down_whole)
    grad_gate = (
        grad_hidden * up_act * sigmoid_gate * (1.0 + gate_act * (1.0 - sigmoid_gate))
    ).astype(jnp.bfloat16)
    grad_up = (grad_hidden * gate_act * sigmoid_gate).astype(jnp.bfloat16)
    left_rows = lax.slice_in_dim(whole_two, 0, w_gate.shape[0] * lax.axis_size("dp"), axis=1)
    grad_rows = grad_mlp
    ffn_shares = lax.psum_scatter(
        jnp.concatenate(
            [
                inner_rows(left_rows, grad_gate),
                inner_rows(left_rows, grad_up),
                inner_rows(grad_rows, hidden),
            ],
            axis=1,
        ).astype(jnp.bfloat16),
        "dp",
        scatter_dimension=0,
        tiled=True,
    ).astype(jnp.float32)
    width_ff = w_gate.shape[1]
    grad_w_gate = ffn_shares[:, :width_ff]
    grad_w_up = ffn_shares[:, width_ff : 2 * width_ff]
    grad_w_down = ffn_shares[:, 2 * width_ff :].T
    canvas = jnp.zeros((row_count, width), jnp.float32)
    pieces = (
        lax.all_gather(w_gate, "dp", axis=0, tiled=True),
        lax.all_gather(w_up, "dp", axis=0, tiled=True),
    )
    term = outer_cols(grad_gate, pieces[0]) + outer_cols(grad_up, pieces[1])
    grad_two = scatter_grads(lax.dynamic_update_slice_in_dim(canvas, term, jnp.int32(0), 1))
    grad_middle_norm, gain_two = normalize_back(middle, mlp_gain, grad_two)
    grad_middle = grad_result + grad_middle_norm
    grad_attn = gather_grads((BRANCH * grad_middle).astype(jnp.bfloat16))
    grad_attended = outer_cols(grad_attn, out_whole).astype(jnp.bfloat16)
    grad_rot_q, grad_rot_k, grad_val = attend_back(
        queries, key_rows, value_rows, to_heads(grad_attended), log_total, prefix
    )
    grad_query = rotate_back_flat(from_heads(grad_rot_q)).astype(jnp.bfloat16)
    grad_key = rotate_back_flat(from_heads(grad_rot_k)).astype(jnp.bfloat16)
    grad_value = from_heads(grad_val).astype(jnp.bfloat16)
    left_rows = whole_one
    grad_rows = lax.slice_in_dim(grad_attn, 0, w_query.shape[0] * lax.axis_size("dp"), axis=1)
    attn_shares = lax.psum_scatter(
        jnp.concatenate(
            [
                inner_rows(left_rows, grad_query),
                inner_rows(left_rows, grad_key),
                inner_rows(left_rows, grad_value),
                inner_rows(grad_rows, attended),
            ],
            axis=1,
        ).astype(jnp.bfloat16),
        "dp",
        scatter_dimension=0,
        tiled=True,
    ).astype(jnp.float32)
    width_heads = w_query.shape[1]
    grad_w_query = attn_shares[:, :width_heads]
    grad_w_key = attn_shares[:, width_heads : 2 * width_heads]
    grad_w_value = attn_shares[:, 2 * width_heads : 3 * width_heads]
    grad_w_out = attn_shares[:, 3 * width_heads :].T
    pieces = (
        lax.all_gather(w_query, "dp", axis=0, tiled=True),
        lax.all_gather(w_key, "dp", axis=0, tiled=True),
        lax.all_gather(w_value, "dp", axis=0, tiled=True),
    )
    term = (
        outer_cols(grad_query, pieces[0])
        + outer_cols(grad_key, pieces[1])
        + outer_cols(grad_value, pieces[2])
    )
    grad_one = scatter_grads(lax.dynamic_update_slice_in_dim(canvas, term, jnp.int32(0), 1))
    grad_input_norm, gain_one = normalize_back(inputs, attn_gain, grad_one)
    input_grad = grad_middle + grad_input_norm
    gain_one, gain_two = lax.psum((gain_one, gain_two), ("dp", "mp"))
    return (
        block_out.astype(jnp.bfloat16),
        input_grad.astype(jnp.bfloat16),
        grad_w_query,
        grad_w_key,
        grad_w_value,
        grad_w_out,
        grad_w_gate,
        grad_w_up,
        grad_w_down,
        gain_one,
        gain_two,
    )


def solution(mesh):
    return jax.shard_map(
        body,
        mesh=mesh,
        in_specs=(
            P(("dp", "mp"), None),
            P(),
            P(),
            P("dp", "mp"),
            P("dp", "mp"),
            P("dp", "mp"),
            P("mp", "dp"),
            P("dp", "mp"),
            P("dp", "mp"),
            P("mp", "dp"),
            P("dp"),
            P(("dp", "mp"), None),
        ),
        out_specs=(
            P(("dp", "mp"), None),
            P(("dp", "mp"), None),
            P("dp", "mp"),
            P("dp", "mp"),
            P("dp", "mp"),
            P("mp", "dp"),
            P("dp", "mp"),
            P("dp", "mp"),
            P("mp", "dp"),
            P(),
            P(),
        ),
        check_vma=False,
    )
```

profile of v0, /device:TPU:0, one launch (start us, length us, event | category | flops | bytes accessed | tf_op | source)
XLA Modules:
  0.0 1743.9 jit_solution(3933953739725701369)
XLA Ops:
  15.6 28.5 %all-gather.18.cloned.1.call-done = bf16[2304,576]{1,0:T(8,128)(2,1)} async-done(((bf16[288,576]{1,0:T(8,128)(2,1)}), bf16[2304,576]{1,0:T(8,128)(2,1)}) %all-gather.18.cloned.1.call-update) | async-done | bytes 2654224 | tf_op jit(solution)/shard_map/all_gather | solution.py:197
  44.1 91.6 %all-gather.12.cloned.1.call-done = bf16[1024,2304]{1,0:T(8,128)(2,1)} async-done(((bf16[256,2304]{1,0:T(8,128)(2,1)}), bf16[1024,2304]{1,0:T(8,128)(2,1)}) %all-gather.12.cloned.1.call-update) | async-done | bytes 4718608 | tf_op jit(solution)/shard_map/all_gather | solution.py:160
  146.2 21.4 %all-gather.14.cloned.1.call-done = bf16[2304,576]{1,0:T(8,128)(2,1)} async-done(((bf16[288,576]{1,0:T(8,128)(2,1)}), bf16[2304,576]{1,0:T(8,128)(2,1)}) %all-gather.14.cloned.1.call-update) | async-done | bytes 2654224 | tf_op jit(solution)/shard_map/all_gather | solution.py:195
  176.3 24.5 %all-gather.16.cloned.1.call-done = bf16[2304,576]{1,0:T(8,128)(2,1)} async-done(((bf16[288,576]{1,0:T(8,128)(2,1)}), bf16[2304,576]{1,0:T(8,128)(2,1)}) %all-gather.16.cloned.1.call-update) | async-done | bytes 2654224 | tf_op jit(solution)/shard_map/all_gather | solution.py:196
  220.5 95.0 %while.57 = (s32[]{:T(128)}, bf16[9,1024,64]{1,2,0:T(8,128)(2,1)}, f32[9,1024]{1,0:T(8,128)}, s32[]{:T(128)}, bf16[9,1024,64]{2,1,0:T(8,128)(2,1)}, /*index=5*/b...) while((s32[]{:T(128)}, bf16[9,1024,64]{1,2,0:T(8,128)(2,1)}, ...), condition=%wide.region_6.7_spmd, body=%wide.region_1.6_spmd.sunk | while | flops 279250432 | bytes 14345869 | solution.py:143
  315.6 10.5 fusion.82
  327.0 160.6 %reduce-scatter.11.cloned.1.call-done = f32[256,2304]{1,0:T(8,128)} async-done(((f32[1024,2304]{1,0:T(8,128)}), f32[256,2304]{1,0:T(8,128)}) %reduce-scatter.11.cloned.1.call-update) | async-done | bytes 2359312 | tf_op jit(solution)/shard_map/reduce_scatter | solution.py:164
  493.9 45.3 %all-gather.26.cloned.1.call-done = bf16[2304,1440]{1,0:T(8,128)(2,1)} async-done(((bf16[288,1440]{1,0:T(8,128)(2,1)}), bf16[2304,1440]{1,0:T(8,128)(2,1)}) %all-gather.26.cloned.1.call-update) | async-done | bytes 6635536 | tf_op jit(solution)/shard_map/all_gather | solution.py:216
  539.2 91.6 %all-gather.22.cloned.1.call-done = bf16[1024,2304]{1,0:T(8,128)(2,1)} async-done(((bf16[256,2304]{1,0:T(8,128)(2,1)}), bf16[1024,2304]{1,0:T(8,128)(2,1)}) %all-gather.22.cloned.1.call-update) | async-done | bytes 4718608 | tf_op jit(solution)/shard_map/all_gather | solution.py:160
  630.8 12.7 fusion.84
  643.5 36.5 %all-gather.24.cloned.1.call-done = bf16[2304,1440]{1,0:T(8,128)(2,1)} async-done(((bf16[288,1440]{1,0:T(8,128)(2,1)}), bf16[2304,1440]{1,0:T(8,128)(2,1)}) %all-gather.24.cloned.1.call-update) | async-done | bytes 6635536 | tf_op jit(solution)/shard_map/all_gather | solution.py:215
  680.0 12.7 fusion.83
  692.8 78.7 %all-gather.30.cloned.1.call-done = bf16[1024,2304]{1,0:T(8,128)(2,1)} async-done(((bf16[256,2304]{1,0:T(8,128)(2,1)}), bf16[1024,2304]{1,0:T(8,128)(2,1)}) %all-gather.30.cloned.1.call-update) | async-done | bytes 4718608 | tf_op jit(solution)/shard_map/all_gather | solution.py:168
  771.5 49.2 %all-gather.28.cloned.1.call-done = bf16[1440,2304]{0,1:T(8,128)(2,1)} async-done(((bf16[1440,288]{0,1:T(8,128)(2,1)}), bf16[1440,2304]{0,1:T(8,128)(2,1)}) %all-gather.28.cloned.1.call-update) | async-done | bytes 6635536 | tf_op jit(solution)/shard_map/all_gather | solution.py:223
  820.7 18.8 %multiply_convert_fusion.2 = (bf16[1024,1440]{0,1:T(8,128)(2,1)}, bf16[1024,1440]{0,1:T(8,128)(2,1)}, bf16[1024,1440]{0,1:T(8,128)(2,1)}) fusion(f32[1024,1440]{0,1:T(8,128)} %fusion.83, f32[1024,1440]{0,1:T(8,128)} %fusion.84, bf16[1024,2304]{1,0:T(8,128)(2,1)} %all-gather.30.cloned.1.call-done, bf16[1440,2304]{0,1:T(8,128)(2,1)} %all-gather.28.cloned.1.call-done), kind=kOutput, calls=%fused_computation.98 | convolution fusion | flops 6818365440 | bytes 31997952 | tf_op jit(solution)/shard_map/dot_general | solution.py:77
  839.6 10.7 fusion.86
  850.3 13.5 convolution_add_fusion.2
  864.0 161.2 %reduce-scatter.15.cloned.1.call-done = f32[256,2304]{1,0:T(8,128)} async-done(((f32[1024,2304]{1,0:T(8,128)}), f32[256,2304]{1,0:T(8,128)}) %reduce-scatter.15.cloned.1.call-update) | async-done | bytes 2359312 | tf_op jit(solution)/shard_map/reduce_scatter | solution.py:172
  1030.7 10.2 convolution_convert_fusion.3
  1040.9 11.7 convolution_convert_fusion.4
  1052.6 8.9 convolution_convert_fusion.2
  1061.6 14.1 pad_maximum_fusion.1
  1075.7 24.9 %copy.47 = bf16[2304,4320]{1,0:T(8,128)(2,1)} copy(bf16[2304,4320]{0,1:T(8,128)(2,1)} %pad_maximum_fusion.1) | data formatting | bytes 39813120
  1100.7 20.3 %all-gather.32.cloned.1.call-done = bf16[1024,2304]{1,0:T(8,128)(2,1)} async-done(((bf16[256,2304]{1,0:T(8,128)(2,1)}), bf16[1024,2304]{1,0:T(8,128)(2,1)}) %all-gather.32.cloned.1.call-update) | async-done | bytes 4718608 | tf_op jit(solution)/shard_map/all_gather | solution.py:168
  1128.7 152.9 %while.58 = (s32[]{:T(128)}, f32[9,1024,64]{1,2,0:T(8,128)}, f32[9,1024,64]{1,2,0:T(8,128)}, bf16[9,1024,64]{1,2,0:T(8,128)(2,1)}, s32[]{:T(128)}, /*index=5*/bf...) while((s32[]{:T(128)}, f32[9,1024,64]{1,2,0:T(8,128)}, ...), condition=%wide.region_15.16_spmd, body=%wide.region_12.15_spmd.sunk | while | flops 682951168 | bytes 36474032 | solution.py:152
  1306.8 15.0 copy.45
  1335.3 10.0 add_add_fusion
  1347.1 13.4 fusion.85
  1379.1 23.8 %reduce-scatter.19.cloned.1.call-done = bf16[288,2304]{1,0:T(8,128)(2,1)} async-done(((bf16[2304,2304]{1,0:T(8,128)(2,1)}), bf16[288,2304]{1,0:T(8,128)(2,1)}) %reduce-scatter.19.cloned.1.call-update) | async-done | bytes 1327120
  1417.3 149.3 %reduce-scatter.17.cloned.1.call-done = f32[256,2304]{1,0:T(8,128)} async-done(((f32[1024,2304]{1,0:T(8,128)}), f32[256,2304]{1,0:T(8,128)}) %reduce-scatter.17.cloned.1.call-update) | async-done | bytes 2359312 | tf_op jit(solution)/shard_map/reduce_scatter | solution.py:172
  1569.5 45.2 %all-reduce = (f32[2304]{0:T(1024)}, f32[2304]{0:T(1024)}) all-reduce(f32[2304]{0:T(1024)} %get-tuple-element.380, f32[2304]{0:T(1024)} %get-tuple-element.378), channel_id=1, replica_groups=mesh['dp'=8,'mp'=4] {'dp','mp'}, use_global_device_ids=true, to_apply=%region_21.22 | all-reduce | flops 4608 | bytes 36864 | tf_op jit(solution)/shard_map/psum | solution.py:303
  1616.0 116.0 %reduce-scatter.13.cloned.1.call-done = f32[256,2304]{1,0:T(8,128)} async-done(((f32[1024,2304]{1,0:T(8,128)}), f32[256,2304]{1,0:T(8,128)}) %reduce-scatter.13.cloned.1.call-update) | async-done | bytes 2359312 | tf_op jit(solution)/shard_map/reduce_scatter | solution.py:164
  (425 shorter events, 397.2 us)
Async XLA Ops:
  7.2 36.9 %all-gather.18.cloned.1.call-start = ((), (), s32[]{:S(2)}) async-start(), calls=%async_computation.9 | async-start | bytes 3317760 | tf_op jit(solution)/shard_map/all_gather | solution.py:197
  7.9 127.8 %all-gather.12.cloned.1.call-start = ((), (), s32[]{:S(2)}) async-start(), calls=%async_computation.6 | async-start | bytes 5898240 | tf_op jit(solution)/shard_map/all_gather | solution.py:160
  12.2 155.3 %all-gather.14.cloned.1.call-start = ((), (), s32[]{:S(2)}) async-start(), calls=%async_computation.7 | async-start | bytes 3317760 | tf_op jit(solution)/shard_map/all_gather | solution.py:195
  13.0 187.9 %all-gather.16.cloned.1.call-start = ((), (), s32[]{:S(2)}) async-start(), calls=%async_computation.8 | async-start | bytes 3317760 | tf_op jit(solution)/shard_map/all_gather | solution.py:196
  13.6 302.1 %all-gather.20.cloned.1.call-start = ((), (), s32[]{:S(2)}) async-start(), calls=%async_computation.10 | async-start | bytes 3317760 | tf_op jit(solution)/shard_map/all_gather | solution.py:208
  14.1 473.5 %reduce-scatter.11.cloned.1.call-start = ((), (), s32[]{:S(2)}) async-start(), calls=%async_computation.11 | async-start | bytes 11796480 | tf_op jit(solution)/shard_map/reduce_scatter | solution.py:164
  315.6 10.6 copy-start.6
  326.2 213.0 %all-gather.26.cloned.1.call-start = ((), (), s32[]{:S(2)}) async-start(), calls=%async_computation.14 | async-start | bytes 7962624 | tf_op jit(solution)/shard_map/all_gather | solution.py:216
  326.9 162.8 %copy-start.20 = (f32[2304]{0:T(1024)S(1)}, f32[2304]{0:T(1024)}, u32[]{:S(2)}) copy-start(f32[2304]{0:T(1024)} %param.34) | copy-start | bytes 27652
  326.9 303.9 %all-gather.22.cloned.1.call-start = ((), (), s32[]{:S(2)}) async-start(), calls=%async_computation.12 | async-start | bytes 5898240 | tf_op jit(solution)/shard_map/all_gather | solution.py:160
  489.7 538.5 %copy-start = (f32[256,2304]{1,0:T(8,128)}, f32[256,2304]{1,0:T(8,128)S(1)}, u32[]{:S(2)}) copy-start(f32[256,2304]{1,0:T(8,128)S(1)} %get-tuple-element.419) | copy-start | bytes 7077892
  489.7 538.5 %copy-start.22 = (f32[256]{0:T(256)}, f32[256]{0:T(256)S(1)}, u32[]{:S(2)}) copy-start(f32[256]{0:T(256)S(1)} %add_rsqrt_fusion) | copy-start | bytes 3076
  491.1 189.0 %all-gather.24.cloned.1.call-start = ((), (), s32[]{:S(2)}) async-start(), calls=%async_computation.13 | async-start | bytes 7962624 | tf_op jit(solution)/shard_map/all_gather | solution.py:215
  491.8 279.7 %all-gather.30.cloned.1.call-start = ((), (), s32[]{:S(2)}) async-start(), calls=%async_computation.17 | async-start | bytes 5898240 | tf_op jit(solution)/shard_map/all_gather | solution.py:168
  493.1 327.6 %all-gather.28.cloned.1.call-start = ((), (), s32[]{:S(2)}) async-start(), calls=%async_computation.15 | async-start | bytes 7962624 | tf_op jit(solution)/shard_map/all_gather | solution.py:223
  493.9 531.3 %reduce-scatter.15.cloned.1.call-start = ((), (), s32[]{:S(2)}) async-start(), calls=%async_computation.18 | async-start | bytes 11796480 | tf_op jit(solution)/shard_map/reduce_scatter | solution.py:172
  863.8 257.3 %all-gather.32.cloned.1.call-start = ((), (), s32[]{:S(2)}) async-start(), calls=%async_computation.19 | async-start | bytes 5898240 | tf_op jit(solution)/shard_map/all_gather | solution.py:168
  1030.6 330.0 %reduce-scatter.21.cloned.1.call-start = ((), (), s32[]{:S(2)}) async-start(), calls=%async_computation.22 | async-start | bytes 22560768
  1030.7 10.2 copy-start.30
  1030.7 21.9 %slice-start.4 = ((s8[4718592]{0:T(1024)(128)(4,1)}), s8[4194304]{0:T(1024)(128)(4,1)S(1)}, s32[]{:S(2)}) async-start(s8[4718592]{0:T(1024)(128)(4,1)} %bitcast.293), calls=%async_computation.27 | async-start | bytes 8388608
  1040.9 11.8 slice-start.5
  1040.9 11.8 copy-start.28
  1100.7 302.2 %reduce-scatter.19.cloned.1.call-start = ((), (), s32[]{:S(2)}) async-start(), calls=%async_computation.21 | async-start | bytes 11943936
  1128.7 152.9 %copy-start.18 = (f32[1024,64]{0,1:T(8,128)S(1)}, f32[1024,64]{0,1:T(8,128)}, u32[]{:S(2)}) copy-start(f32[1024,64]{0,1:T(8,128)} %get-tuple-element.459) | copy-start | bytes 786436
  1321.9 244.6 %reduce-scatter.17.cloned.1.call-start = ((), (), s32[]{:S(2)}) async-start(), calls=%async_computation.20 | async-start | bytes 11796480 | tf_op jit(solution)/shard_map/reduce_scatter | solution.py:172
  1321.9 5.9 copy-start.26
  1327.8 7.5 copy-start.14
  1345.3 386.7 %reduce-scatter.13.cloned.1.call-start = ((), (), s32[]{:S(2)}) async-start(), calls=%async_computation.16 | async-start | bytes 11796480 | tf_op jit(solution)/shard_map/reduce_scatter | solution.py:164
  1411.4 155.1 %copy-start.3 = (bf16[256,2304]{1,0:T(8,128)(2,1)S(1)}, bf16[256,2304]{1,0:T(8,128)(2,1)}, u32[]{:S(2)}) copy-start(bf16[256,2304]{1,0:T(8,128)(2,1)} %param.32) | copy-start | bytes 3538948
  1414.8 317.2 %copy-start.1 = (f32[256,2304]{1,0:T(8,128)S(1)}, f32[256,2304]{1,0:T(8,128)}, u32[]{:S(2)}) copy-start(f32[256,2304]{1,0:T(8,128)} %copy-done) | copy-start | bytes 7077892
  1414.8 317.2 %copy-start.21 = (f32[2304]{0:T(1024)S(1)}, f32[2304]{0:T(1024)}, u32[]{:S(2)}) copy-start(f32[2304]{0:T(1024)} %param.34) | copy-start | bytes 27652
  1414.8 317.2 %copy-start.23 = (f32[256]{0:T(256)S(1)}, f32[256]{0:T(256)}, u32[]{:S(2)}) copy-start(f32[256]{0:T(256)} %copy-done.22) | copy-start | bytes 3076
  (22 other events, 48.0 us)
Sparse Core Ops, SparseCore 0:
  9.9 34.1 all-gather.17
  46.3 89.4 all-gather.11
  137.6 29.9 all-gather.13
  169.3 31.4 all-gather.15
  202.6 31.4 all-gather.19
  326.3 161.2 reduce-scatter.10
  489.5 49.6 all-gather.25
  541.4 89.4 all-gather.21
  632.7 47.2 all-gather.23
  682.0 89.4 all-gather.29
  773.4 47.2 all-gather.27
  863.9 161.2 reduce-scatter.14
  1030.7 90.2 all-gather.31
  1124.6 129.8 reduce-scatter.20
  1322.0 80.8 reduce-scatter.18
  1405.2 161.2 reduce-scatter.16
  1568.8 163.0 reduce-scatter.12
where the time goes:
time: 1750 us; the launch traced here: 1740 us
  waiting for transfers between devices  1100 us (63%)
  matrix products  365 us (21%)
  local copies, waits for them, and re-layouts  110 us (6%)
  other arithmetic  104 us (6%)
  blocking collectives  45.2 us (3%)
    reduce_scatter x2, waiting for transfers between devices, scatter_grads(): return lax.psum_scatter(value, 'mp', scatter_dimension=0, tiled=True)  310 us
    reduce_scatter x2, waiting for transfers between devices, scatter_rows(): return lax.psum_scatter(value, 'mp', scatter_dimension=0, tiled=True)  277 us
    all_gather x2, waiting for transfers between devices, gather_rows(): return lax.all_gather(value, 'mp', axis=0, tiled=True)  183 us
    dot_general x61, matrix products, outer_cols(): lax.dot_general(left, right, (((1,), (1,)), ((), ())), preferred_element_...  164 us
    dot_general x43, matrix products, matmul(): return jnp.dot(left, right, preferred_element_type=jnp.float32)  117 us
    all_gather x2, waiting for transfers between devices, gather_grads(): return lax.all_gather(value, 'mp', axis=0, tiled=True)  99 us
    dot_general x43, matrix products, inner_rows(): lax.dot_general(left, right, (((0,), (0,)), ((), ())), preferred_element_...  84.7 us
    unnamed x85, local copies, waits for them, and re-layouts  70.2 us
  transfers between devices with their start and end apart: 17, of which 15 were waited for; matrix products, arithmetic and copies ran while one was open for 29% of the time, Pallas kernels for 0%

commit v1 on v0

v1 whole, which is shorter than its diff:
```python
import functools

import jax
import jax.numpy as jnp
from jax import lax
from jax.experimental import pallas as pl
from jax.experimental.pallas import tpu as pltpu
from jax.sharding import PartitionSpec as P

HD = 64
LEN = 1024
LANES = 128
EPSILON = 1e-05
BRANCH = 1.4 / 40**0.5
MASKED = -1e30
FF_BLOCK = 256
VMEM_LIMIT = 56 * 1024 * 1024

F32 = jnp.float32
BF16 = jnp.bfloat16


def round_up(value, unit):
    return -(-value // unit) * unit


def matmul(left, right):
    return jnp.dot(left, right, preferred_element_type=F32)


def inner_rows(left, right):
    return lax.dot_general(
        left, right, (((0,), (0,)), ((), ())), preferred_element_type=F32
    )


def outer_cols(left, right):
    return lax.dot_general(
        left, right, (((1,), (1,)), ((), ())), preferred_element_type=F32
    )


def params(limit=VMEM_LIMIT):
    return pltpu.CompilerParams(vmem_limit_bytes=limit)


def ring_up(value):
    n = lax.axis_size("mp")
    return lax.ppermute(value, "mp", [(i, (i + 1) % n) for i in range(n)])


def ring_gather(value):
    pieces = [value]
    for _ in range(lax.axis_size("mp") - 1):
        pieces.append(ring_up(pieces[-1]))
    return pieces


def ring_scatter(part):
    n = lax.axis_size("mp")
    place = lax.axis_index("mp")
    total = part((place + n - 1) % n)
    for step in range(1, n):
        arrived = ring_up(total.astype(BF16))
        total = part((place + 2 * n - 1 - step) % n) + arrived.astype(F32)
    return total


def shift_back(value, count):
    n = lax.axis_size("mp")
    return lax.ppermute(value, "mp", [(i, (i - count) % n) for i in range(n)])


def sum_all(value):
    for axis in ("mp", "dp"):
        n = lax.axis_size(axis)
        bit = 1
        while bit < n:
            value = value + lax.ppermute(value, axis, [(i, i ^ bit) for i in range(n)])
            bit *= 2
    return value


def place_kernel(count, place_ref, *refs):
    pieces, out_ref, sems = refs[:count], refs[count], refs[count + 1]
    rows = pieces[0].shape[0]
    place = place_ref[0]
    copies = []
    for k in range(count):
        start = pl.multiple_of(lax.rem(place + count - k, count) * rows, rows)
        copy = pltpu.make_async_copy(
            pieces[k], out_ref.at[pl.ds(start, rows)], sems.at[k]
        )
        copy.start()
        copies.append(copy)
    for copy in copies:
        copy.wait()


def place_rows(pieces, place):
    count = len(pieces)
    rows, width = pieces[0].shape
    return pl.pallas_call(
        functools.partial(place_kernel, count),
        out_shape=jax.ShapeDtypeStruct((count * rows, width), pieces[0].dtype),
        in_specs=[pl.BlockSpec(memory_space=pltpu.SMEM)]
        + [pl.BlockSpec(memory_space=pl.ANY)] * count,
        out_specs=pl.BlockSpec(memory_space=pl.ANY),
        scratch_shapes=[pltpu.SemaphoreType.DMA((count,))],
        name="place",
    )(place, *pieces)


def angle_tables():
    half = HD // 2
    places = jnp.arange(LEN, dtype=F32)
    rates = 10000.0 ** (-jnp.arange(half, dtype=F32) * 2.0 / HD)
    angles = places[:, None] * rates[None, :]
    cosine, sine = jnp.cos(angles), jnp.sin(angles)
    return (
        jnp.concatenate([cosine] * 4, axis=-1),
        jnp.concatenate([-sine, sine] * 2, axis=-1),
    )


def swap_halves(value):
    lane = lax.broadcasted_iota(jnp.int32, value.shape, 1)
    low = (lane % HD) < HD // 2
    return jnp.where(
        low, pltpu.roll(value, LANES - HD // 2, 1), pltpu.roll(value, HD // 2, 1)
    )


def project_kernel(fresh, where_ref, x_ref, gain_ref, w_ref, cos_ref, sin_ref, *refs):
    qkv_ref, norm_ref, copy_ref, held = refs[-4:]

    @pl.when(pl.program_id(0) == 0)
    def _():
        value = x_ref[...].astype(F32)
        factor = lax.rsqrt(jnp.mean(value * value, axis=-1, keepdims=True) + EPSILON)
        normed = (value * factor * gain_ref[...]).astype(BF16)
        held[...] = normed
        norm_ref[...] = normed
        copy_ref[...] = x_ref[...]

    product = matmul(held[...], w_ref[...])
    cosine, sine = cos_ref[...], sin_ref[...]
    query = product[:, :LANES]
    key = product[:, LANES : 2 * LANES]
    query = (query * cosine + swap_halves(query) * sine).astype(BF16)
    qkv_ref[:, :LANES] = query * HD**-0.5
    qkv_ref[:, LANES : 2 * LANES] = (key * cosine + swap_halves(key) * sine).astype(BF16)
    qkv_ref[:, 2 * LANES :] = product[:, 2 * LANES :].astype(BF16)


def project(where, piece, gain, weights, tables, held):
    rows, width = piece.shape
    columns = weights.shape[1]
    block = 3 * LANES
    fresh = held is None
    outs = (
        jax.ShapeDtypeStruct((LEN, columns), BF16),
        jax.ShapeDtypeStruct((LEN, width), BF16),
        jax.ShapeDtypeStruct((LEN, width), BF16),
    )
    specs = [
        pl.BlockSpec((rows, width), lambda i, w: (0, 0)),
        pl.BlockSpec((1, width), lambda i, w: (0, 0)),
        pl.BlockSpec((width, block), lambda i, w: (0, i)),
        pl.BlockSpec((rows, LANES), lambda i, w: (w[0], 0)),
        pl.BlockSpec((rows, LANES), lambda i, w: (w[0], 0)),
    ]
    args = [piece, gain, weights, *tables]
    aliases = {}
    if not fresh:
        for index, array in enumerate(held):
            aliases[1 + len(args)] = index
            args.append(array)
            specs.append(pl.BlockSpec(memory_space=pl.ANY))
    return pl.pallas_call(
        functools.partial(project_kernel, fresh),
        out_shape=outs,
        grid_spec=pltpu.PrefetchScalarGridSpec(
            num_scalar_prefetch=1,
            grid=(columns // block,),
            in_specs=specs,
            out_specs=(
                pl.BlockSpec((rows, block), lambda i, w: (w[0], i)),
                pl.BlockSpec((rows, width), lambda i, w: (w[0], 0)),
                pl.BlockSpec((rows, width), lambda i, w: (w[0], 0)),
            ),
            scratch_shapes=[pltpu.VMEM((rows, width), BF16)],
        ),
        input_output_aliases=aliases,
        compiler_params=params(),
        cost_estimate=pl.CostEstimate(
            flops=2 * rows * width * columns,
            bytes_accessed=2 * width * columns + 6 * rows * width,
            transcendentals=0,
        ),
        name="project",
    )(where, *args)


PARTS = (
    (0, 512, ((0, 512, True),)),
    (512, 256, ((0, 512, False), (512, 256, True))),
    (768, 256, ((0, 768, False), (768, 256, True))),
)


def visible(shape, first_key, first_query, limit):
    key = first_key + lax.broadcasted_iota(jnp.int32, shape, 0)
    query = first_query + lax.broadcasted_iota(jnp.int32, shape, 1)
    return (key < limit) | (key <= query)


def head_only(value, head):
    lane = lax.broadcasted_iota(jnp.int32, value.shape, 1)
    return jnp.where((lane >= HD) == (head == 1), value, jnp.zeros_like(value))


def attend_kernel(heads, prefix_ref, qkv_ref, out_ref, log_ref, turned):
    limit = prefix_ref[0]
    pair = pl.program_id(0)
    values_across = qkv_ref[:, 2 * LANES :].T
    for head in (0, 1):

        @pl.when(2 * pair + head < heads)
        def _():
            queries = head_only(qkv_ref[:, :LANES], head)
            for first, count, spans in PARTS:
                mine = queries[first : first + count]
                scores = []
                for start, keys, masked in spans:
                    raw = outer_cols(qkv_ref[start : start + keys, LANES : 2 * LANES], mine)
                    if masked:
                        raw = jnp.where(visible(raw.shape, start, first, limit), raw, MASKED)
                    scores.append(raw)
                top = functools.reduce(
                    jnp.maximum, [jnp.max(s, axis=0, keepdims=True) for s in scores]
                )
                total = jnp.zeros_like(top)
                summed = jnp.zeros((HD, count), F32)
                for (start, keys, _), raw in zip(spans, scores):
                    weight = jnp.exp(raw - top)
                    total = total + jnp.sum(weight, axis=0, keepdims=True)
                    summed = summed + matmul(
                        values_across[head * HD : (head + 1) * HD, start : start + keys],
                        weight.astype(BF16),
                    )
                turned[head * HD : (head + 1) * HD, first : first + count] = summed / total
                log_ref[0, head : head + 1, first : first + count] = top + jnp.log(total)

        @pl.when(2 * pair + head >= heads)
        def _():
            turned[head * HD : (head + 1) * HD, :] = jnp.zeros((HD, LEN), F32)
            log_ref[0, head : head + 1, :] = jnp.zeros((1, LEN), F32)

    out_ref[...] = turned[...].T.astype(BF16)


def attend(qkv, prefix, heads):
    pairs = qkv.shape[1] // (3 * LANES)
    return pl.pallas_call(
        functools.partial(attend_kernel, heads),
        out_shape=(
            jax.ShapeDtypeStruct((LEN, pairs * LANES), BF16),
            jax.ShapeDtypeStruct((pairs, 2, LEN), F32),
        ),
        grid_spec=pltpu.PrefetchScalarGridSpec(
            num_scalar_prefetch=1,
            grid=(pairs,),
            in_specs=[pl.BlockSpec((LEN, 3 * LANES), lambda i, s: (0, i))],
            out_specs=(
                pl.BlockSpec((LEN, LANES), lambda i, s: (0, i)),
                pl.BlockSpec((1, 2, LEN), lambda i, s: (i, 0, 0)),
            ),
            scratch_shapes=[pltpu.VMEM((LANES, LEN), F32)],
        ),
        compiler_params=params(),
        cost_estimate=pl.CostEstimate(
            flops=16 * LEN * LEN * LANES * heads,
            bytes_accessed=8 * LEN * LANES * pairs,
            transcendentals=LEN * LEN * heads,
        ),
        name="attend",
    )(prefix, qkv)


def attend_back_kernel(
    heads, prefix_ref, qkv_ref, out_ref, grad_ref, log_ref, cos_ref, sin_ref, back_ref,
    turned, grad_key, grad_value,
):
    limit = prefix_ref[0]
    pair = pl.program_id(0)
    keys_across = qkv_ref[:, LANES : 2 * LANES].T
    inner = (out_ref[...].astype(F32) * grad_ref[...].astype(F32)).T
    grad_key[...] = jnp.zeros_like(grad_key)
    grad_value[...] = jnp.zeros_like(grad_value)
    for head in (0, 1):
        band = slice(head * HD, (head + 1) * HD)

        @pl.when(2 * pair + head < heads)
        def _():
            queries = head_only(qkv_ref[:, :LANES], head)
            grads = head_only(grad_ref[...], head)
            inner_row = jnp.sum(inner[band], axis=0, keepdims=True)
            for first, count, spans in PARTS:
                here = slice(first, first + count)
                mine, grad_mine = queries[here], grads[here]
                log_mine = log_ref[0, head : head + 1, here]
                inner_mine = inner_row[:, here]
                summed = jnp.zeros((HD, count), F32)
                for start, keys, masked in spans:
                    there = slice(start, start + keys)
                    raw = outer_cols(qkv_ref[there, LANES : 2 * LANES], mine)
                    chance = jnp.exp(raw - log_mine)
                    if masked:
                        chance = jnp.where(
                            visible(raw.shape, start, first, limit), chance, 0.0
                        )
                    grad_chance = outer_cols(qkv_ref[there, 2 * LANES :], grad_mine)
                    grad_score = (chance * (grad_chance - inner_mine)).astype(BF16)
                    grad_key[there, :] += matmul(grad_score, mine)
                    grad_value[there, :] += matmul(chance.astype(BF16), grad_mine)
                    summed = summed + matmul(keys_across[band, there], grad_score)
                turned[band, here] = summed

        @pl.when(2 * pair + head >= heads)
        def _():
            turned[band, :] = jnp.zeros((HD, LEN), F32)

    cosine, sine = cos_ref[...], sin_ref[...]
    grad_query = turned[...].T * HD**-0.5
    back_ref[:, :LANES] = (grad_query * cosine - swap_halves(grad_query) * sine).astype(BF16)
    back = grad_key[...]
    back_ref[:, LANES : 2 * LANES] = (back * cosine - swap_halves(back) * sine).astype(BF16)
    back_ref[:, 2 * LANES :] = grad_value[...].astype(BF16)


def attend_back(qkv, attended, grad, log_total, tables, prefix, heads):
    pairs = qkv.shape[1] // (3 * LANES)
    return pl.pallas_call(
        functools.partial(attend_back_kernel, heads),
        out_shape=jax.ShapeDtypeStruct(qkv.shape, BF16),
        grid_spec=pltpu.PrefetchScalarGridSpec(
            num_scalar_prefetch=1,
            grid=(pairs,),
            in_specs=[
                pl.BlockSpec((LEN, 3 * LANES), lambda i, s: (0, i)),
                pl.BlockSpec((LEN, LANES), lambda i, s: (0, i)),
                pl.BlockSpec((LEN, LANES), lambda i, s: (0, i)),
                pl.BlockSpec((1, 2, LEN), lambda i, s: (i, 0, 0)),
                pl.BlockSpec((LEN, LANES), lambda i, s: (0, 0)),
                pl.BlockSpec((LEN, LANES), lambda i, s: (0, 0)),
            ],
            out_specs=pl.BlockSpec((LEN, 3 * LANES), lambda i, s: (0, i)),
            scratch_shapes=[
                pltpu.VMEM((LANES, LEN), F32),
                pltpu.VMEM((LEN, LANES), F32),
                pltpu.VMEM((LEN, LANES), F32),
            ],
        ),
        compiler_params=params(),
        cost_estimate=pl.CostEstimate(
            flops=40 * LEN * LEN * LANES * heads,
            bytes_accessed=16 * LEN * LANES * pairs,
            transcendentals=LEN * LEN * heads,
        ),
        name="attend_back",
    )(prefix, qkv, attended, grad, log_total, *tables)


def mlp_kernel(normed_ref, grad_ref, gate_up_ref, down_ref, both_ref, hidden_ref):
    rows = 256
    for start in range(0, LEN, rows):
        here = slice(start, start + rows)
        product = matmul(normed_ref[here], gate_up_ref[...])
        gate, up = product[:, :FF_BLOCK], product[:, FF_BLOCK:]
        grad = matmul(grad_ref[here], down_ref[...])
        sigmoid = jax.nn.sigmoid(gate)
        silu = gate * sigmoid
        hidden_ref[here, :] = (silu * up).astype(BF16)
        both_ref[here, :FF_BLOCK] = (
            grad * up * (sigmoid + silu * (1.0 - sigmoid))
        ).astype(BF16)
        both_ref[here, FF_BLOCK:] = (grad * silu).astype(BF16)


def mlp(normed, grad, gate_up, down):
    width = normed.shape[1]
    hidden = down.shape[1]
    return pl.pallas_call(
        mlp_kernel,
        out_shape=(
            jax.ShapeDtypeStruct((LEN, 2 * hidden), BF16),
            jax.ShapeDtypeStruct((LEN, hidden), BF16),
        ),
        grid=(hidden // FF_BLOCK,),
        in_specs=[
            pl.BlockSpec((LEN, width), lambda i: (0, 0)),
            pl.BlockSpec((LEN, width), lambda i: (0, 0)),
            pl.BlockSpec((width, 2 * FF_BLOCK), lambda i: (0, i)),
            pl.BlockSpec((width, FF_BLOCK), lambda i: (0, i)),
        ],
        out_specs=(
            pl.BlockSpec((LEN, 2 * FF_BLOCK), lambda i: (0, i)),
            pl.BlockSpec((LEN, FF_BLOCK), lambda i: (0, i)),
        ),
        compiler_params=params(),
        cost_estimate=pl.CostEstimate(
            flops=6 * LEN * width * hidden,
            bytes_accessed=4 * LEN * width + 6 * width * hidden + 6 * LEN * hidden,
            transcendentals=LEN * hidden,
        ),
        name="mlp",
    )(normed, grad, gate_up, down)


def widen(value, width):
    return jnp.pad(value, ((0, 0), (0, width - value.shape[1])))


def interleave(values, width, block):
    rows = values[0].shape[0]
    shaped = [widen(v, width).reshape(rows, width // block, block) for v in values]
    return jnp.stack(shaped, axis=2).reshape(rows, len(values) * width)


def separate(value, count, block, width):
    rows = value.shape[0]
    shaped = value.reshape(rows, -1, count, block)
    return [shaped[:, :, i].reshape(rows, -1)[:, :width] for i in range(count)]


def dp_gather(value):
    return lax.all_gather(value, "dp", axis=0, tiled=True)


def dp_scatter(value):
    return lax.psum_scatter(value, "dp", scatter_dimension=0, tiled=True)


def normalize_back(value, gain, incoming):
    factor = lax.rsqrt(jnp.mean(value * value, axis=-1, keepdims=True) + EPSILON)
    normed = value * factor
    scaled = incoming * gain
    inner = jnp.mean(scaled * normed, axis=-1, keepdims=True)
    return (factor * (scaled - normed * inner), jnp.sum(incoming * normed, axis=0))


def body(
    tokens,
    attn_gain,
    mlp_gain,
    w_query,
    w_key,
    w_value,
    w_out,
    w_gate,
    w_up,
    w_down,
    prefix,
    out_grad,
):
    mp = lax.axis_size("mp")
    place = lax.axis_index("mp")
    rows = tokens.shape[0]
    width_heads = w_query.shape[1]
    heads = width_heads // HD
    padded_heads = round_up(width_heads, LANES)
    width_ff = w_gate.shape[1]
    padded_ff = round_up(width_ff, FF_BLOCK)
    own = place * rows

    def row_block(value, index):
        return lax.dynamic_slice_in_dim(value, index * rows, rows, 0)

    tables = angle_tables()
    attn_weights = dp_gather(interleave([w_query, w_key, w_value], padded_heads, LANES))
    out_weights = dp_gather(
        jnp.concatenate(ring_gather(widen(w_out.T, padded_heads)), axis=1)
    )
    gate_up = dp_gather(interleave([w_gate, w_up], padded_ff, FF_BLOCK))
    down = dp_gather(widen(w_down.T, padded_ff))

    held = None
    token_pieces = ring_gather(tokens)
    for k, piece in enumerate(token_pieces):
        where = jnp.reshape((place + mp - k) % mp, (1,))
        held = project(where, piece, attn_gain[None], attn_weights, tables, held)
    qkv, normed_one, whole_tokens = held

    attended, log_total = attend(qkv, prefix, heads)
    attended_pieces = ring_gather(attended)
    attn_sum = jnp.zeros((LEN, out_weights.shape[0]), F32)
    for k, piece in enumerate(attended_pieces):
        attn_sum = attn_sum + outer_cols(
            piece, out_weights[:, k * padded_heads : (k + 1) * padded_heads]
        )
    middle_all = whole_tokens.astype(F32) + BRANCH * attn_sum
    normed_two = (
        middle_all
        * lax.rsqrt(jnp.mean(middle_all * middle_all, axis=-1, keepdims=True) + EPSILON)
        * mlp_gain
    ).astype(BF16)
    middle = row_block(middle_all, place)

    grad_result = out_grad.astype(F32)
    grad_pieces = ring_gather((BRANCH * grad_result).astype(BF16))
    grad_mlp = place_rows(grad_pieces, jnp.reshape(place, (1,)))

    grad_both, hidden = mlp(normed_two, grad_mlp, gate_up, down)

    grad_two = ring_scatter(lambda c: outer_cols(row_block(grad_both, c), gate_up))
    grad_middle_norm, gain_two = normalize_back(middle, mlp_gain, grad_two)
    grad_middle = grad_result + grad_middle_norm
    grad_attn = (BRANCH * grad_middle).astype(BF16)
    grad_attended = matmul(grad_attn, out_weights).astype(BF16)
    arrived = []
    for k in range(mp):
        mine = grad_attended[:, k * padded_heads : (k + 1) * padded_heads]
        arrived.append(mine if k == 0 else shift_back(mine, k))
    grad_heads = place_rows(
        [arrived[(mp - k) % mp] for k in range(mp)], jnp.reshape(place, (1,))
    )

    mlp_sum = ring_scatter(lambda c: outer_cols(row_block(hidden, c), down))
    block_out = middle + BRANCH * mlp_sum

    ff_share = dp_scatter(inner_rows(normed_two, grad_both).astype(BF16)).astype(F32)
    down_share = dp_scatter(inner_rows(grad_mlp, hidden).astype(BF16)).astype(F32)
    grad_w_gate, grad_w_up = separate(ff_share, 2, FF_BLOCK, width_ff)
    grad_w_down = down_share[:, :width_ff].T

    attended_own = jnp.concatenate(
        [row_block(piece, place) for piece in attended_pieces], axis=1
    )
    out_share = dp_scatter(inner_rows(grad_attn, attended_own).astype(BF16))
    out_total = out_share[:, :padded_heads].astype(F32)
    for k in range(1, mp):
        mine = out_share[:, k * padded_heads : (k + 1) * padded_heads]
        out_total = out_total + shift_back(mine, k).astype(F32)
    grad_w_out = out_total[:, :width_heads].T

    back = attend_back(qkv, attended, grad_heads, log_total, tables, prefix, heads)
    attn_share = dp_scatter(inner_rows(normed_one, back).astype(BF16)).astype(F32)
    grad_w_query, grad_w_key, grad_w_value = separate(attn_share, 3, LANES, width_heads)

    grad_one = ring_scatter(lambda c: outer_cols(row_block(back, c), attn_weights))
    grad_input_norm, gain_one = normalize_back(tokens.astype(F32), attn_gain, grad_one)
    input_grad = grad_middle + grad_input_norm
    gains = sum_all(jnp.stack([gain_one, gain_two]))
    return (
        block_out.astype(BF16),
        input_grad.astype(BF16),
        grad_w_query,
        grad_w_key,
        grad_w_value,
        grad_w_out,
        grad_w_gate,
        grad_w_up,
        grad_w_down,
        gains[0],
        gains[1],
    )


def solution(mesh):
    return jax.shard_map(
        body,
        mesh=mesh,
        in_specs=(
            P(("dp", "mp"), None),
            P(),
            P(),
            P("dp", "mp"),
            P("dp", "mp"),
            P("dp", "mp"),
            P("mp", "dp"),
            P("dp", "mp"),
            P("dp", "mp"),
            P("mp", "dp"),
            P("dp"),
            P(("dp", "mp"), None),
        ),
        out_specs=(
            P(("dp", "mp"), None),
            P(("dp", "mp"), None),
            P("dp", "mp"),
            P("dp", "mp"),
            P("dp", "mp"),
            P("mp", "dp"),
            P("dp", "mp"),
            P("dp", "mp"),
            P("mp", "dp"),
            P(),
            P(),
        ),
        check_vma=False,
    )
```

time: 1750 us -> 1050 us (0.60)
  waiting for transfers between devices: 1100 us -> 422 us
  Pallas kernels: 0 us -> 300 us
  matrix products: 365 us -> 185 us
  other arithmetic: 104 us -> 25.4 us
  local copies, waits for them, and re-layouts: 110 us -> 61.1 us
  blocking collectives: 45.2 us -> 0 us
  starting transfers between devices: 0.85 us -> 28.2 us
    reduce_scatter x4, waiting for transfers between devices: 587 us -> 31.3 us  [dp_scatter(): return lax.psum_scatter(value, 'dp', scatter_dimension=0, tiled=True)]
    all_gather x11 -> x4, waiting for transfers between devices: 488 us -> 0.03 us  [dp_gather(): return lax.all_gather(value, 'dp', axis=0, tiled=True)]
    ppermute x0 -> x32, waiting for transfers between devices: none -> 390 us  [the longest x21 346 us: ring_up(): return lax.ppermute(value, 'mp', [(i, (i + 1) % n) for i in range(n)])]
    pallas_call x0 -> x9, Pallas kernels: none -> 300 us  [the longest x2 185 us: place_rows(): pl.pallas_call(functools.partial(place_kernel, count), out_shape=jax.Shap...]
    dot_general x43 -> x1, matrix products: 117 us -> 7.61 us  [matmul(): return jnp.dot(left, right, preferred_element_type=F32)]
    unnamed x85 -> x80, local copies, waits for them, and re-layouts: 70.2 us -> 14.8 us
    psum x1 -> x0, blocking collectives: 45.2 us -> none  [body(): gain_one, gain_two = lax.psum((gain_one, gain_two), ('dp', 'mp'))]
    dot_general x61 -> x16, matrix products: 164 us -> 121 us  [outer_cols(): lax.dot_general(left, right, (((1,), (1,)), ((), ())), preferred_element_...]
  transfers between devices with their start and end apart: 17 -> 40, of which waited for: 15 -> 23; matrix products, arithmetic and copies ran while one was open for 29% -> 22% of each run, Pallas kernels for 0% -> 26%
where the time goes in v1:
time: 1050 us; the launch traced here: 1040 us
  waiting for transfers between devices  422 us (40%)
  Pallas kernels  300 us (29%)
  matrix products  185 us (18%)
  local copies, waits for them, and re-layouts  61.1 us (6%)
  starting transfers between devices  28.2 us (3%)
  other arithmetic  25.4 us (2%)
  between operations  16 us (2%)
    ppermute x21, waiting for transfers between devices, ring_up(): return lax.ppermute(value, 'mp', [(i, (i + 1) % n) for i in range(n)])  346 us
    pallas_call x2, Pallas kernels, place_rows(): pl.pallas_call(functools.partial(place_kernel, count), out_shape=jax.Shap...  185 us
    dot_general x16, matrix products, outer_cols(): lax.dot_general(left, right, (((1,), (1,)), ((), ())), preferred_element_...  121 us
    dot_general x4, matrix products, inner_rows(): lax.dot_general(left, right, (((0,), (0,)), ((), ())), preferred_element_...  55.8 us
    pallas_call x4, Pallas kernels, project(): pl.pallas_call(functools.partial(project_kernel, fresh), out_shape=outs,...  39 us
    reduce_scatter x4, waiting for transfers between devices, dp_scatter(): return lax.psum_scatter(value, 'dp', scatter_dimension=0, tiled=True)  31.3 us
    ppermute x5, waiting for transfers between devices, sum_all(): value = value + lax.ppermute(value, axis, [(i, i ^ bit) for i in range(n)])  30 us
    pallas_call x1, Pallas kernels, mlp(): pl.pallas_call(mlp_kernel, out_shape=(jax.ShapeDtypeStruct((LEN, 2 * hidd...  29.8 us
  transfers between devices with their start and end apart: 40, of which 23 were waited for; matrix products, arithmetic and copies ran while one was open for 22% of the time, Pallas kernels for 26%

profile of v1, /device:TPU:0, one launch (start us, length us, event | category | flops | bytes accessed | tf_op | source)
XLA Modules:
  0.0 1037.1 jit_solution(1549426882282001846)
XLA Ops:
  17.4 10.6 %collective-permute-done.3 = bf16[288,640]{1,0:T(8,128)(2,1)S(1)} collective-permute-done((bf16[288,640]{1,0:T(8,128)(2,1)S(1)}, bf16[288,640]{1,0:T(8,128)(2,1)S(1)}, u32[]{:S(2)}, u32[]{:S(2)}) %collective-permute-start.3) | collective-permute-done | bytes 368672 | tf_op jit(solution)/shard_map/ppermute | solution.py:49
  28.1 11.6 %collective-permute-done.4 = bf16[288,640]{1,0:T(8,128)(2,1)S(1)} collective-permute-done((bf16[288,640]{1,0:T(8,128)(2,1)S(1)}, bf16[288,640]{1,0:T(8,128)(2,1)S(1)}, u32[]{:S(2)}, u32[]{:S(2)}) %collective-permute-start.4) | collective-permute-done | bytes 368672 | tf_op jit(solution)/shard_map/ppermute | solution.py:49
  39.6 10.6 %collective-permute-done.5 = bf16[288,640]{1,0:T(8,128)(2,1)S(1)} collective-permute-done((bf16[288,640]{1,0:T(8,128)(2,1)S(1)}, bf16[288,640]{1,0:T(8,128)(2,1)S(1)}, u32[]{:S(2)}, u32[]{:S(2)}) %collective-permute-start.5) | collective-permute-done | bytes 368672 | tf_op jit(solution)/shard_map/ppermute | solution.py:49
  62.0 27.1 %collective-permute-done.x_ref = bf16[256,2304]{1,0:T(8,128)(2,1)S(1)} collective-permute-done((bf16[256,2304]{1,0:T(8,128)(2,1)S(1)}, bf16[256,2304]{1,0:T(8,128)(2,1)S(1)}, u32[]{:S(2)}, u32[]{:S(2)}) %collective-permute-start) | collective-permute-done | bytes 1179680 | tf_op jit(solution)/shard_map/ppermute | solution.py:49
  89.1 26.3 %collective-permute-done.1.x_ref = bf16[256,2304]{1,0:T(8,128)(2,1)} collective-permute-done((bf16[256,2304]{1,0:T(8,128)(2,1)S(1)}, bf16[256,2304]{1,0:T(8,128)(2,1)}, u32[]{:S(2)}, u32[]{:S(2)}) %collective-permute-start.1) | collective-permute-done | bytes 1179680 | tf_op jit(solution)/shard_map/ppermute | solution.py:49
  151.2 9.9 project.7
  161.1 18.0 %attend.1 = (bf16[1024,640]{1,0:T(8,128)(2,1)}, f32[5,2,1024]{2,1,0:T(2,128)}) custom-call(s32[1]{0:T(128)S(6)} %copy.65.prefix_ref, bf16[1024,1920]{1,0:T(8,128)(2,1)} %get-tuple-element.37.qkv_ref), custom_call_target="tpu_custom_call" | custom-call | flops 19327352832 | bytes 5242880 | tf_op jit(solution)/shard_map/attend/pallas_call | solution.py:265
  184.1 28.8 %collective-permute-done.6 = bf16[1024,640]{1,0:T(8,128)(2,1)} collective-permute-done((bf16[1024,640]{1,0:T(8,128)(2,1)}, bf16[1024,640]{1,0:T(8,128)(2,1)}, u32[]{:S(2)}, u32[]{:S(2)}) %collective-permute-start.6) | collective-permute-done | bytes 1310752 | tf_op jit(solution)/shard_map/ppermute | solution.py:49
  213.7 24.4 %collective-permute-done.10.refs_2_ = bf16[256,2304]{1,0:T(8,128)(2,1)S(1)} collective-permute-done((bf16[256,2304]{1,0:T(8,128)(2,1)S(1)}, bf16[256,2304]{1,0:T(8,128)(2,1)S(1)}, u32[]{:S(2)}, u32[]{:S(2)}) %collective-permute-start.10) | collective-permute-done | bytes 1179680 | tf_op jit(solution)/shard_map/ppermute | solution.py:49
  238.9 47.3 %collective-permute-done.11.refs_3_ = bf16[256,2304]{1,0:T(8,128)(2,1)S(1)} collective-permute-done((bf16[256,2304]{1,0:T(8,128)(2,1)S(1)}, bf16[256,2304]{1,0:T(8,128)(2,1)S(1)}, u32[]{:S(2)}, u32[]{:S(2)}) %collective-permute-start.11) | collective-permute-done | bytes 1179680 | tf_op jit(solution)/shard_map/ppermute | solution.py:49
  287.2 144.1 %place.2.grad_ref = bf16[1024,2304]{1,0:T(8,128)(2,1)} custom-call(s32[1]{0:T(128)} %bitcast.8.place_ref, bf16[256,2304]{1,0:T(8,128)(2,1)} %copy-done.5, bf16[256,2304]{1,0:T(8,128)(2,1)} %copy-done.8, bf16[256,2304]{1,0:T(8,128)(2,1)} %copy-done.11, bf16[256,2304]{1,0:T(8,128)(2,1)} %copy-done.12), custom_call_target="tpu_custom_call" | custom-call | tf_op jit(solution)/shard_map/place/pallas_call | solution.py:103
  431.6 9.8 fusion.10
  459.0 15.3 %multiply_reduce_fusion = (f32[1024]{0:T(1024)S(1)}, f32[1024,2304]{1,0:T(8,128)}) fusion(bf16[1024,640]{1,0:T(8,128)(2,1)S(1)} %collective-permute-done.8, bf16[2304,2560]{1,0:T(8,128)(2,1)} %all-gather.7.cloned.1.call-done, f32[1024,2304]{1,0:T(8,128)} %fusion.10, f32[1024,2304]{1,0:T(8,128)} %fusion.14, f32[1024,2304]{1,0:T(8,128)} %fusion.12, ...), kind=kOutput, calls=%fused_computation.5 | convolution fusion | flops 3038772224 | bytes 46731264 | tf_op jit(solution)/shard_map/dot_general | solution.py:38
  481.0 29.8 %mlp.1 = (bf16[1024,3072]{1,0:T(8,128)(2,1)}, bf16[1024,1536]{1,0:T(8,128)(2,1)}) custom-call(bf16[1024,2304]{1,0:T(8,128)(2,1)} %multiply_convert_fusion.normed_ref, bf16[1024,2304]{1,0:T(8,128)(2,1)} %place.2.grad_ref, bf16[2304,3072]{1,0:T(8,128)(2,1)} %all-gather.9.cloned.1.call-done.gate_up_ref, bf16[2304,1536]{1,0:T(8,128)(2,1)} %all-gather.11.cloned.1.call-done.down_ref), custom_call_target="tpu_custom_call" | custom-call | flops 21743271936 | bytes 40108032 | tf_op jit(solution)/shard_map/mlp/pallas_call | solution.py:394
  520.2 23.5 %collective-permute-done.15 = bf16[256,2304]{1,0:T(8,128)(2,1)S(1)} collective-permute-done((bf16[256,2304]{1,0:T(8,128)(2,1)S(1)}, bf16[256,2304]{1,0:T(8,128)(2,1)S(1)}, u32[]{:S(2)}, u32[]{:S(2)}) %collective-permute-start.15) | collective-permute-done | bytes 1179680 | tf_op jit(solution)/shard_map/ppermute | solution.py:49
  555.2 20.6 %collective-permute-done.16 = bf16[256,2304]{1,0:T(8,128)(2,1)} collective-permute-done((bf16[256,2304]{1,0:T(8,128)(2,1)S(1)}, bf16[256,2304]{1,0:T(8,128)(2,1)}, u32[]{:S(2)}, u32[]{:S(2)}) %collective-permute-start.16) | collective-permute-done | bytes 1179680 | tf_op jit(solution)/shard_map/ppermute | solution.py:49
  575.8 10.6 %fusion.2 = bf16[256,2304]{1,0:T(8,128)(2,1)} fusion(bf16[2304,3072]{1,0:T(8,128)(2,1)} %all-gather.9.cloned.1.call-done.gate_up_ref, bf16[256,2304]{1,0:T(8,128)(2,1)} %collective-permute-done.16, bf16[1024,3072]{1,0:T(8,128)(2,1)} %get-tuple-element.40, s32[]{:T(128)S(6)} %select_n.81), kind=kOutput, calls=%fused_computation.18 | convolution fusion | flops 3625648128 | bytes 18087940 | tf_op jit(solution)/shard_map/dot_general | solution.py:38
  586.4 11.5 %convolution_convert_fusion.2 = bf16[2304,1536]{1,0:T(8,128)(2,1)} fusion(bf16[1024,2304]{1,0:T(8,128)(2,1)S(1)} %bitcast.67, bf16[1024,1536]{1,0:T(8,128)(2,1)} %get-tuple-element.39), kind=kOutput, calls=%fused_computation.2 | convolution fusion | flops 7251296256 | bytes 14942208 | tf_op jit(solution)/shard_map/dot_general | solution.py:32
  598.0 10.3 collective-permute-done.17
  608.3 13.5 %multiply_reduce_fusion.1 = (f32[2304]{0:T(1024)S(1)}, f32[256]{0:T(256)S(1)}, f32[256,2304]{1,0:T(8,128)}) fusion(f32[1024,2304]{1,0:T(8,128)} %get-tuple-element.66, s32[]{:T(128)S(6)} %select_n.78, f32[256]{0:T(256)S(1)} %add_rsqrt_fusion.2, f32[2304]{0:T(1024)S(1)} %copy-done.22, bf16[256,2304]{1,0:T(8,128)(2,1)S(1)} %collective-permute-done.17, ...), kind=kOutput, calls=%fused_computation.52 | convolution fusion | flops 3628594688 | bytes 21647368 | tf_op jit(solution)/shard_map/dot_general | solution.py:38
  653.0 40.8 %place.3.grad_ref = bf16[1024,640]{1,0:T(8,128)(2,1)} custom-call(s32[1]{0:T(128)} %bitcast.8.place_ref, bf16[256,640]{1,0:T(8,128)(2,1)} %get-tuple-element.61.refs_0_, bf16[256,640]{1,0:T(8,128)(2,1)} %copy-done.18, bf16[256,640]{1,0:T(8,128)(2,1)} %copy-done.19, bf16[256,640]{1,0:T(8,128)(2,1)} %copy-done.20), custom_call_target="tpu_custom_call" | custom-call | tf_op jit(solution)/shard_map/place/pallas_call | solution.py:103
  693.9 28.1 %attend_back.1 = bf16[1024,1920]{1,0:T(8,128)(2,1)} custom-call(s32[1]{0:T(128)S(6)} %copy.65.prefix_ref, bf16[1024,1920]{1,0:T(8,128)(2,1)} %get-tuple-element.37.qkv_ref, bf16[1024,640]{1,0:T(8,128)(2,1)} %get-tuple-element.38.out_ref, bf16[1024,640]{1,0:T(8,128)(2,1)} %place.3.grad_ref, f32[5,2,1024]{2,1,0:T(2,128)} %get-tuple-element.41.log_ref, ...), custom_call_target="tpu_custom_call" | custom-call | flops 48318382080 | bytes 10485760 | tf_op jit(solution)/shard_map/attend_back/pallas_call | solution.py:344
  721.9 14.1 %convolution_convert_fusion.3 = bf16[2304,1920]{1,0:T(8,128)(2,1)} fusion(bf16[1024,2304]{1,0:T(8,128)(2,1)S(1)} %bitcast.63, bf16[1024,1920]{1,0:T(8,128)(2,1)} %attend_back.1), kind=kOutput, calls=%fused_computation.3 | convolution fusion | flops 9064120320 | bytes 17498112 | tf_op jit(solution)/shard_map/dot_general | solution.py:32
  748.0 22.5 %convolution_convert_fusion = bf16[2304,3072]{1,0:T(8,128)(2,1)} fusion(bf16[1024,2304]{1,0:T(8,128)(2,1)} %multiply_convert_fusion.normed_ref, bf16[1024,3072]{1,0:T(8,128)(2,1)} %get-tuple-element.40), kind=kOutput, calls=%fused_computation | convolution fusion | flops 14502592512 | bytes 25165824 | tf_op jit(solution)/shard_map/dot_general | solution.py:32
  781.1 21.9 %collective-permute-done.21 = bf16[256,2304]{1,0:T(8,128)(2,1)S(1)} collective-permute-done((bf16[256,2304]{1,0:T(8,128)(2,1)S(1)}, bf16[256,2304]{1,0:T(8,128)(2,1)S(1)}, u32[]{:S(2)}, u32[]{:S(2)}) %collective-permute-start.21) | collective-permute-done | bytes 1179680 | tf_op jit(solution)/shard_map/ppermute | solution.py:49
  815.9 24.6 %collective-permute-done.22 = bf16[256,2304]{1,0:T(8,128)(2,1)} collective-permute-done((bf16[256,2304]{1,0:T(8,128)(2,1)S(1)}, bf16[256,2304]{1,0:T(8,128)(2,1)}, u32[]{:S(2)}, u32[]{:S(2)}) %collective-permute-start.22) | collective-permute-done | bytes 1179680 | tf_op jit(solution)/shard_map/ppermute | solution.py:49
  846.0 19.8 %collective-permute-done.12 = bf16[256,2304]{1,0:T(8,128)(2,1)S(1)} collective-permute-done((bf16[256,2304]{1,0:T(8,128)(2,1)S(1)}, bf16[256,2304]{1,0:T(8,128)(2,1)S(1)}, u32[]{:S(2)}, u32[]{:S(2)}) %collective-permute-start.12) | collective-permute-done | bytes 1179680 | tf_op jit(solution)/shard_map/ppermute | solution.py:49
  870.6 20.6 %collective-permute-done.23 = bf16[256,2304]{1,0:T(8,128)(2,1)} collective-permute-done((bf16[256,2304]{1,0:T(8,128)(2,1)S(1)}, bf16[256,2304]{1,0:T(8,128)(2,1)}, u32[]{:S(2)}, u32[]{:S(2)}) %collective-permute-start.23) | collective-permute-done | bytes 1179680 | tf_op jit(solution)/shard_map/ppermute | solution.py:49
  896.4 14.8 %collective-permute-done.13 = bf16[256,2304]{1,0:T(8,128)(2,1)} collective-permute-done((bf16[256,2304]{1,0:T(8,128)(2,1)}, bf16[256,2304]{1,0:T(8,128)(2,1)}, u32[]{:S(2)}, u32[]{:S(2)}) %collective-permute-start.13) | collective-permute-done | bytes 1179680 | tf_op jit(solution)/shard_map/ppermute | solution.py:49
  916.4 23.4 %collective-permute-done.28 = f32[2,2304]{1,0:T(2,128)S(1)} collective-permute-done((f32[2,2304]{1,0:T(2,128)S(1)}, f32[2,2304]{1,0:T(2,128)S(1)}, u32[]{:S(2)}, u32[]{:S(2)}) %collective-permute-start.28) | collective-permute-done | bytes 18464 | tf_op jit(solution)/shard_map/ppermute | solution.py:79
  975.1 31.3 %reduce-scatter.9.cloned.1.call-done = bf16[288,3072]{1,0:T(8,128)(2,1)} async-done(((bf16[2304,3072]{1,0:T(8,128)(2,1)}), bf16[288,3072]{1,0:T(8,128)(2,1)}) %reduce-scatter.9.cloned.1.call-update) | async-done | bytes 1769488 | tf_op jit(solution)/shard_map/reduce_scatter | solution.py:442
  1011.0 10.8 %slice_reduce_fusion = (f32[288,6,256]{2,1,0:T(8,128)}, f32[288,6,256]{2,1,0:T(8,128)}) fusion(f32[288,6,2,256]{3,2,1,0:T(2,128)S(1)} %reshape.110), kind=kLoop, calls=%fused_computation.56 | loop fusion | bytes 7077888 | tf_op jit(solution)/shard_map/slice | solution.py:434
  (223 shorter events, 245.0 us)
Async XLA Ops:
  7.2 113.9 %all-gather.5.cloned.1.call-start = ((), (), s32[]{:S(2)}) async-start(), calls=%async_computation.4 | async-start | bytes 9953280 | tf_op jit(solution)/shard_map/all_gather | solution.py:438
  14.2 417.3 %all-gather.7.cloned.1.call-start = ((), (), s32[]{:S(2)}) async-start(), calls=%async_computation.5 | async-start | bytes 13271040 | tf_op jit(solution)/shard_map/all_gather | solution.py:438
  51.5 429.4 %all-gather.11.cloned.1.call-start = ((), (), s32[]{:S(2)}) async-start(), calls=%async_computation.7 | async-start | bytes 7962624 | tf_op jit(solution)/shard_map/all_gather | solution.py:438
  52.6 428.3 %all-gather.9.cloned.1.call-start = ((), (), s32[]{:S(2)}) async-start(), calls=%async_computation.6 | async-start | bytes 15925248 | tf_op jit(solution)/shard_map/all_gather | solution.py:438
  61.9 892.2 %reduce-scatter.11.cloned.1.call-start = ((), (), s32[]{:S(2)}) async-start(), calls=%async_computation.11 | async-start | bytes 7962624 | tf_op jit(solution)/shard_map/reduce_scatter | solution.py:442
  62.0 27.2 %collective-permute-start = (bf16[256,2304]{1,0:T(8,128)(2,1)S(1)}, bf16[256,2304]{1,0:T(8,128)(2,1)S(1)}, u32[]{:S(2)}, u32[]{:S(2)}) collective-permute-start(bf16[256,2304]{1,0:T(8,128)(2,1)S(1)} %copy-done), channel_id=1, source_target_pairs={{0,1},{1,2},{2,3},{3,0},{4,5},{5,6},{6,7},{7,4},{8,9},{9,10},{10,1... | collective-permute-start | bytes 3538952 | tf_op jit(solution)/shard_map/ppermute | solution.py:49
  89.1 26.3 %collective-permute-start.1 = (bf16[256,2304]{1,0:T(8,128)(2,1)S(1)}, bf16[256,2304]{1,0:T(8,128)(2,1)}, u32[]{:S(2)}, u32[]{:S(2)}) collective-permute-start(bf16[256,2304]{1,0:T(8,128)(2,1)S(1)} %collective-permute-done.x_ref), channel_id=1, source_target_pairs={{0,1},{1,2},{2,3},{3,0},{4,5},{5,6},{6,7},{7,4},{8,9},{9,10},{10,1... | collective-permute-start | bytes 3538952 | tf_op jit(solution)/shard_map/ppermute | solution.py:49
  115.4 34.7 %collective-permute-start.2 = (bf16[256,2304]{1,0:T(8,128)(2,1)}, bf16[256,2304]{1,0:T(8,128)(2,1)S(1)}, u32[]{:S(2)}, u32[]{:S(2)}) collective-permute-start(bf16[256,2304]{1,0:T(8,128)(2,1)} %collective-permute-done.1.x_ref), channel_id=1, source_target_pairs={{0,1},{1,2},{2,3},{3,0},{4,5},{5,6},{6,7},{7,4},{8,9},{9,10},{10,1... | collective-permute-start | bytes 3538952 | tf_op jit(solution)/shard_map/ppermute | solution.py:49
  115.7 63.7 %collective-permute-start.9 = (bf16[256,2304]{1,0:T(8,128)(2,1)S(1)}, bf16[256,2304]{1,0:T(8,128)(2,1)S(1)}, u32[]{:S(2)}, u32[]{:S(2)}) collective-permute-start(bf16[256,2304]{1,0:T(8,128)(2,1)S(1)} %fusion.19.refs_0_), channel_id=1, source_target_pairs={{0,1},{1,2},{2,3},{3,0},{4,5},{5,6},{6,7},{7,4},{8,9},{9,10},{10,1... | collective-permute-start | bytes 3538952 | tf_op jit(solution)/shard_map/ppermute | solution.py:49
  179.1 33.8 %collective-permute-start.6 = (bf16[1024,640]{1,0:T(8,128)(2,1)}, bf16[1024,640]{1,0:T(8,128)(2,1)}, u32[]{:S(2)}, u32[]{:S(2)}) collective-permute-start(bf16[1024,640]{1,0:T(8,128)(2,1)} %get-tuple-element.38.out_ref), channel_id=1, source_target_pairs={{0,1},{1,2},{2,3},{3,0},{4,5},{5,6},{6,7},{7,4},{8,9},{9,10},{10,1... | collective-permute-start | bytes 3932168 | tf_op jit(solution)/shard_map/ppermute | solution.py:49
  179.4 58.7 %collective-permute-start.10 = (bf16[256,2304]{1,0:T(8,128)(2,1)S(1)}, bf16[256,2304]{1,0:T(8,128)(2,1)S(1)}, u32[]{:S(2)}, u32[]{:S(2)}) collective-permute-start(bf16[256,2304]{1,0:T(8,128)(2,1)S(1)} %collective-permute-done.9.refs_1_), channel_id=1, source_target_pairs={{0,1},{1,2},{2,3},{3,0},{4,5},{5,6},{6,7},{7,4},{8,9},{9,10},{10,1... | collective-permute-start | bytes 3538952 | tf_op jit(solution)/shard_map/ppermute | solution.py:49
  212.9 218.3 %collective-permute-start.7 = (bf16[1024,640]{1,0:T(8,128)(2,1)}, bf16[1024,640]{1,0:T(8,128)(2,1)}, u32[]{:S(2)}, u32[]{:S(2)}) collective-permute-start(bf16[1024,640]{1,0:T(8,128)(2,1)} %collective-permute-done.6), channel_id=1, source_target_pairs={{0,1},{1,2},{2,3},{3,0},{4,5},{5,6},{6,7},{7,4},{8,9},{9,10},{10,1... | collective-permute-start | bytes 3932168 | tf_op jit(solution)/shard_map/ppermute | solution.py:49
  238.1 48.0 %collective-permute-start.11 = (bf16[256,2304]{1,0:T(8,128)(2,1)S(1)}, bf16[256,2304]{1,0:T(8,128)(2,1)S(1)}, u32[]{:S(2)}, u32[]{:S(2)}) collective-permute-start(bf16[256,2304]{1,0:T(8,128)(2,1)S(1)} %collective-permute-done.10.refs_2_), channel_id=1, source_target_pairs={{0,1},{1,2},{2,3},{3,0},{4,5},{5,6},{6,7},{7,4},{8,9},{9,10},{10,1... | collective-permute-start | bytes 3538952 | tf_op jit(solution)/shard_map/ppermute | solution.py:49
  431.3 27.7 %collective-permute-start.8 = (bf16[1024,640]{1,0:T(8,128)(2,1)}, bf16[1024,640]{1,0:T(8,128)(2,1)S(1)}, u32[]{:S(2)}, u32[]{:S(2)}) collective-permute-start(bf16[1024,640]{1,0:T(8,128)(2,1)} %collective-permute-done.7), channel_id=1, source_target_pairs={{0,1},{1,2},{2,3},{3,0},{4,5},{5,6},{6,7},{7,4},{8,9},{9,10},{10,1... | collective-permute-start | bytes 3932168 | tf_op jit(solution)/shard_map/ppermute | solution.py:49
  520.1 23.6 %collective-permute-start.15 = (bf16[256,2304]{1,0:T(8,128)(2,1)S(1)}, bf16[256,2304]{1,0:T(8,128)(2,1)S(1)}, u32[]{:S(2)}, u32[]{:S(2)}) collective-permute-start(bf16[256,2304]{1,0:T(8,128)(2,1)S(1)} %convolution_convert_fusion.6), channel_id=1, source_target_pairs={{0,1},{1,2},{2,3},{3,0},{4,5},{5,6},{6,7},{7,4},{8,9},{9,10},{10,1... | collective-permute-start | bytes 3538952 | tf_op jit(solution)/shard_map/ppermute | solution.py:49
  553.0 22.7 %collective-permute-start.16 = (bf16[256,2304]{1,0:T(8,128)(2,1)S(1)}, bf16[256,2304]{1,0:T(8,128)(2,1)}, u32[]{:S(2)}, u32[]{:S(2)}) collective-permute-start(bf16[256,2304]{1,0:T(8,128)(2,1)S(1)} %fusion.3), channel_id=1, source_target_pairs={{0,1},{1,2},{2,3},{3,0},{4,5},{5,6},{6,7},{7,4},{8,9},{9,10},{10,1... | collective-permute-start | bytes 3538952 | tf_op jit(solution)/shard_map/ppermute | solution.py:49
  586.4 21.9 %collective-permute-start.17 = (bf16[256,2304]{1,0:T(8,128)(2,1)}, bf16[256,2304]{1,0:T(8,128)(2,1)S(1)}, u32[]{:S(2)}, u32[]{:S(2)}) collective-permute-start(bf16[256,2304]{1,0:T(8,128)(2,1)} %fusion.2), channel_id=1, source_target_pairs={{0,1},{1,2},{2,3},{3,0},{4,5},{5,6},{6,7},{7,4},{8,9},{9,10},{10,1... | collective-permute-start | bytes 3538952 | tf_op jit(solution)/shard_map/ppermute | solution.py:49
  597.9 358.9 %reduce-scatter.5.cloned.1.call-start = ((), (), s32[]{:S(2)}) async-start(), calls=%async_computation.8 | async-start | bytes 9953280 | tf_op jit(solution)/shard_map/reduce_scatter | solution.py:442
  633.8 18.3 %collective-permute-start.19 = (bf16[256,640]{1,0:T(8,128)(2,1)S(1)}, bf16[256,640]{1,0:T(8,128)(2,1)S(1)}, u32[]{:S(2)}, u32[]{:S(2)}) collective-permute-start(bf16[256,640]{1,0:T(8,128)(2,1)S(1)} %get-tuple-element.59), channel_id=1, source_target_pairs={{0,2},{1,3},{2,0},{3,1},{4,6},{5,7},{6,4},{7,5},{8,10},{9,11},{10,... | collective-permute-start | bytes 983048 | tf_op jit(solution)/shard_map/ppermute | solution.py:71
  736.1 232.7 %reduce-scatter.7.cloned.1.call-start = ((), (), s32[]{:S(2)}) async-start(), calls=%async_computation.9 | async-start | bytes 13271040 | tf_op jit(solution)/shard_map/reduce_scatter | solution.py:442
  748.0 258.3 %reduce-scatter.9.cloned.1.call-start = ((), (), s32[]{:S(2)}) async-start(), calls=%async_computation.10 | async-start | bytes 15925248 | tf_op jit(solution)/shard_map/reduce_scatter | solution.py:442
  777.5 25.5 %collective-permute-start.21 = (bf16[256,2304]{1,0:T(8,128)(2,1)S(1)}, bf16[256,2304]{1,0:T(8,128)(2,1)S(1)}, u32[]{:S(2)}, u32[]{:S(2)}) collective-permute-start(bf16[256,2304]{1,0:T(8,128)(2,1)S(1)} %convolution_convert_fusion.4), channel_id=1, source_target_pairs={{0,1},{1,2},{2,3},{3,0},{4,5},{5,6},{6,7},{7,4},{8,9},{9,10},{10,1... | collective-permute-start | bytes 3538952 | tf_op jit(solution)/shard_map/ppermute | solution.py:49
  809.7 30.9 %collective-permute-start.22 = (bf16[256,2304]{1,0:T(8,128)(2,1)S(1)}, bf16[256,2304]{1,0:T(8,128)(2,1)}, u32[]{:S(2)}, u32[]{:S(2)}) collective-permute-start(bf16[256,2304]{1,0:T(8,128)(2,1)S(1)} %fusion.5), channel_id=1, source_target_pairs={{0,1},{1,2},{2,3},{3,0},{4,5},{5,6},{6,7},{7,4},{8,9},{9,10},{10,1... | collective-permute-start | bytes 3538952 | tf_op jit(solution)/shard_map/ppermute | solution.py:49
  815.4 50.3 %collective-permute-start.12 = (bf16[256,2304]{1,0:T(8,128)(2,1)S(1)}, bf16[256,2304]{1,0:T(8,128)(2,1)S(1)}, u32[]{:S(2)}, u32[]{:S(2)}) collective-permute-start(bf16[256,2304]{1,0:T(8,128)(2,1)S(1)} %convolution_convert_fusion.7), channel_id=1, source_target_pairs={{0,1},{1,2},{2,3},{3,0},{4,5},{5,6},{6,7},{7,4},{8,9},{9,10},{10,1... | collective-permute-start | bytes 3538952 | tf_op jit(solution)/shard_map/ppermute | solution.py:49
  845.5 45.7 %collective-permute-start.23 = (bf16[256,2304]{1,0:T(8,128)(2,1)S(1)}, bf16[256,2304]{1,0:T(8,128)(2,1)}, u32[]{:S(2)}, u32[]{:S(2)}) collective-permute-start(bf16[256,2304]{1,0:T(8,128)(2,1)S(1)} %fusion.4), channel_id=1, source_target_pairs={{0,1},{1,2},{2,3},{3,0},{4,5},{5,6},{6,7},{7,4},{8,9},{9,10},{10,1... | collective-permute-start | bytes 3538952 | tf_op jit(solution)/shard_map/ppermute | solution.py:49
  869.9 41.3 %collective-permute-start.13 = (bf16[256,2304]{1,0:T(8,128)(2,1)}, bf16[256,2304]{1,0:T(8,128)(2,1)}, u32[]{:S(2)}, u32[]{:S(2)}) collective-permute-start(bf16[256,2304]{1,0:T(8,128)(2,1)} %fusion.8), channel_id=1, source_target_pairs={{0,1},{1,2},{2,3},{3,0},{4,5},{5,6},{6,7},{7,4},{8,9},{9,10},{10,1... | collective-permute-start | bytes 3538952 | tf_op jit(solution)/shard_map/ppermute | solution.py:49
  895.8 20.5 %collective-permute-start.27 = (f32[2,2304]{1,0:T(2,128)S(1)}, f32[2,2304]{1,0:T(2,128)S(1)}, u32[]{:S(2)}, u32[]{:S(2)}) collective-permute-start(f32[2,2304]{1,0:T(2,128)S(1)} %pad_maximum_fusion.5), channel_id=1, source_target_pairs={{0,1},{1,0},{2,3},{3,2},{4,5},{5,4},{6,7},{7,6},{8,9},{9,8},{10,11... | collective-permute-start | bytes 55304 | tf_op jit(solution)/shard_map/ppermute | solution.py:79
  914.8 25.2 %collective-permute-start.14 = (bf16[256,2304]{1,0:T(8,128)(2,1)S(1)}, bf16[256,2304]{1,0:T(8,128)(2,1)S(1)}, u32[]{:S(2)}, u32[]{:S(2)}) collective-permute-start(bf16[256,2304]{1,0:T(8,128)(2,1)S(1)} %fusion.7), channel_id=1, source_target_pairs={{0,1},{1,2},{2,3},{3,0},{4,5},{5,6},{6,7},{7,4},{8,9},{9,10},{10,1... | collective-permute-start | bytes 3538952 | tf_op jit(solution)/shard_map/ppermute | solution.py:49
  916.3 23.5 %collective-permute-start.28 = (f32[2,2304]{1,0:T(2,128)S(1)}, f32[2,2304]{1,0:T(2,128)S(1)}, u32[]{:S(2)}, u32[]{:S(2)}) collective-permute-start(f32[2,2304]{1,0:T(2,128)S(1)} %fusion.64), channel_id=1, source_target_pairs={{0,2},{1,3},{2,0},{3,1},{4,6},{5,7},{6,4},{7,5},{8,10},{9,11},{10,... | collective-permute-start | bytes 55304 | tf_op jit(solution)/shard_map/ppermute | solution.py:79
  971.2 56.3 %collective-permute-start.26 = (bf16[288,640]{1,0:T(8,128)(2,1)}, bf16[288,640]{1,0:T(8,128)(2,1)}, u32[]{:S(2)}, u32[]{:S(2)}) collective-permute-start(bf16[288,640]{1,0:T(8,128)(2,1)} %get-tuple-element.55), channel_id=1, source_target_pairs={{0,1},{1,2},{2,3},{3,0},{4,5},{5,6},{6,7},{7,4},{8,9},{9,10},{10,1... | collective-permute-start | bytes 1105928 | tf_op jit(solution)/shard_map/ppermute | solution.py:71
  971.4 56.2 %collective-permute-start.25 = (bf16[288,640]{1,0:T(8,128)(2,1)}, bf16[288,640]{1,0:T(8,128)(2,1)}, u32[]{:S(2)}, u32[]{:S(2)}) collective-permute-start(bf16[288,640]{1,0:T(8,128)(2,1)} %get-tuple-element.56), channel_id=1, source_target_pairs={{0,2},{1,3},{2,0},{3,1},{4,6},{5,7},{6,4},{7,5},{8,10},{9,11},{10,... | collective-permute-start | bytes 1105928 | tf_op jit(solution)/shard_map/ppermute | solution.py:71
  971.8 55.7 %collective-permute-start.24 = (bf16[288,640]{1,0:T(8,128)(2,1)}, bf16[288,640]{1,0:T(8,128)(2,1)}, u32[]{:S(2)}, u32[]{:S(2)}) collective-permute-start(bf16[288,640]{1,0:T(8,128)(2,1)} %get-tuple-element.57), channel_id=1, source_target_pairs={{0,3},{1,0},{2,1},{3,2},{4,7},{5,4},{6,5},{7,6},{8,11},{9,8},{10,9... | collective-permute-start | bytes 1105928 | tf_op jit(solution)/shard_map/ppermute | solution.py:71
  (44 other events, 995.8 us)
Sparse Core Ops, SparseCore 0:
  14.4 59.0 all-gather.4
  75.9 68.7 all-gather.6
  146.6 48.9 all-gather.10
  197.9 78.6 all-gather.8
  598.0 65.0 reduce-scatter.10
  736.2 73.2 reduce-scatter.4
  813.5 88.1 reduce-scatter.6
  905.3 101.0 reduce-scatter.8

commit v2 on v1

v2 whole, which is shorter than its diff:
```python
import functools

import jax
import jax.numpy as jnp
import numpy as np
from jax import lax
from jax.experimental import pallas as pl
from jax.experimental.pallas import tpu as pltpu
from jax.sharding import PartitionSpec as P

HD = 64
LEN = 1024
LANES = 128
EPSILON = 1e-05
BRANCH = 1.4 / 40**0.5
MASKED = -1e30
FF_BLOCK = 512
VMEM_LIMIT = 56 * 1024 * 1024

F32 = jnp.float32
BF16 = jnp.bfloat16


def round_up(value, unit):
    return -(-value // unit) * unit


def matmul(left, right):
    return jnp.dot(left, right, preferred_element_type=F32)


def inner_rows(left, right):
    return lax.dot_general(
        left, right, (((0,), (0,)), ((), ())), preferred_element_type=F32
    )


def outer_cols(left, right):
    return lax.dot_general(
        left, right, (((1,), (1,)), ((), ())), preferred_element_type=F32
    )


def cost(micros):
    return pl.CostEstimate(
        flops=int(micros * 3.0e9), bytes_accessed=0, transcendentals=0
    )


def params(limit=VMEM_LIMIT):
    return pltpu.CompilerParams(vmem_limit_bytes=limit)


def ring_up(value):
    n = lax.axis_size("mp")
    return lax.ppermute(value, "mp", [(i, (i + 1) % n) for i in range(n)])


def ring_gather(value):
    pieces = [value]
    for _ in range(lax.axis_size("mp") - 1):
        pieces.append(ring_up(pieces[-1]))
    return pieces


def ring_scatter(part):
    n = lax.axis_size("mp")
    place = lax.axis_index("mp")
    total = part((place + n - 1) % n)
    for step in range(1, n):
        sent = total.astype(BF16)
        arrived = ring_up(sent)
        term = lax.optimization_barrier(part((place + 2 * n - 1 - step) % n))
        total = term + arrived.astype(F32)
    return total


def shift_back(value, count):
    n = lax.axis_size("mp")
    return lax.ppermute(value, "mp", [(i, (i - count) % n) for i in range(n)])


def sum_all(value):
    for axis in ("mp", "dp"):
        n = lax.axis_size(axis)
        bit = 1
        while bit < n:
            value = value + lax.ppermute(value, axis, [(i, i ^ bit) for i in range(n)])
            bit *= 2
    return value


def after(value, *others):
    return lax.optimization_barrier((value, others))[0]


def swap(value, bit):
    n = lax.axis_size("dp")
    return lax.ppermute(value, "dp", [(i, i ^ bit) for i in range(n)])


def dp_gather(value):
    return lax.all_gather(value, "dp", axis=0, tiled=True)


def paired():
    return lax.axis_size("dp") == 8


def split_columns(value):
    if not paired():
        return value[None]
    core = lax.axis_index("dp") % 2
    rows, width = value.shape
    shaped = value.reshape(rows, 4, 2, width // 8)

    def pick(which):
        return lax.dynamic_index_in_dim(shaped, which, 2, False).reshape(rows, width // 2)

    return jnp.stack([pick(core), pick(1 - core)])


def after_all(waits):
    return [pl.BlockSpec(memory_space=pl.ANY)] * len(waits)


def weight_kernel(joined, left_ref, right_ref, *refs):
    value = inner_rows(left_ref[...], right_ref[...])
    if joined:
        value = value + refs[0][...].astype(F32)
    refs[-1][...] = value.astype(BF16)


def weight_grad(left, right, side, height, width, micros, arrived=None, waits=()):
    depth, columns = left.shape[-2:]
    others = right.shape[1]
    specs = [
        pl.BlockSpec((None, depth, height), lambda i, j: (side, 0, i))
        if left.ndim == 3
        else pl.BlockSpec((depth, height), lambda i, j: (0, i)),
        pl.BlockSpec((depth, width), lambda i, j: (0, j)),
    ]
    args = [left, right]
    if arrived is not None:
        specs.append(pl.BlockSpec((height, width), lambda i, j: (i, j)))
        args.append(arrived)
    return pl.pallas_call(
        functools.partial(weight_kernel, arrived is not None),
        out_shape=jax.ShapeDtypeStruct((columns, others), BF16),
        grid=(columns // height, others // width),
        in_specs=specs + after_all(waits),
        out_specs=pl.BlockSpec((height, width), lambda i, j: (i, j)),
        compiler_params=params(),
        cost_estimate=cost(micros),
        name="weight_grad",
    )(*args, *waits)


def scatter_other(left, right, width, micros, waits=()):
    if not paired():
        return None
    return weight_grad(left, right, 1, left.shape[2], width, micros, waits=waits)


def scatter_mine(left, right, width, micros, arrived, waits=()):
    if not paired():
        return inner_rows(left[0], right).astype(BF16)
    return weight_grad(left, right, 0, left.shape[2], width, micros, arrived, waits)


def pass_kernel(*refs):
    pass


def gate(value, *waits):
    return pl.pallas_call(
        pass_kernel,
        out_shape=jax.ShapeDtypeStruct(value.shape, value.dtype),
        in_specs=after_all((value, *waits)),
        out_specs=pl.BlockSpec(memory_space=pl.ANY),
        input_output_aliases={0: 0},
        cost_estimate=cost(1),
        name="gate",
    )(value, *waits)


def join_kernel(one_ref, two_ref, *refs):
    out_ref, zero_ref = refs[-2:]
    out_ref[...] = (one_ref[...].astype(F32) + two_ref[...].astype(F32)).astype(BF16)
    zero_ref[0] = 0


def join_marked(one, two, waits=()):
    whole = pl.BlockSpec(memory_space=pltpu.VMEM)
    return pl.pallas_call(
        join_kernel,
        out_shape=(
            jax.ShapeDtypeStruct(one.shape, BF16),
            jax.ShapeDtypeStruct((1,), jnp.int32),
        ),
        in_specs=[whole, whole] + after_all(waits),
        out_specs=(whole, pl.BlockSpec(memory_space=pltpu.SMEM)),
        compiler_params=params(),
        cost_estimate=cost(3),
        name="join",
    )(one, two, *waits)


def join(one, two, waits=()):
    return join_marked(one, two, waits)[0]


def scatter_first(chip):
    index = lax.axis_index("dp")
    x, y = index // 2 % 2, index // 4
    rows = chip.shape[0] // 4
    half = rows // 2
    chip = chip.reshape(2, 2, rows, -1)

    def pick(array, axis, which):
        return lax.dynamic_index_in_dim(array, which, axis, False)

    one, two = chip[:, :, :half], chip[:, :, half:]
    kept = pick(one, 0, y), pick(two, 1, x)
    return kept, (swap(pick(one, 0, 1 - y), 4), swap(pick(two, 1, 1 - x), 2))


def scatter_join(kept, moved, waits):
    return join(kept[0], moved[0], waits), join(kept[1], moved[1], waits)


def scatter_second(parts):
    index = lax.axis_index("dp")
    x, y = index // 2 % 2, index // 4
    one, two = parts

    def pick(array, which):
        return lax.dynamic_index_in_dim(array, which, 0, False)

    return [
        (pick(one, x), swap(pick(one, 1 - x), 2)),
        (pick(two, y), swap(pick(two, 1 - y), 4)),
    ]


def scatter_whole(partial):
    share = lax.psum_scatter(partial, "dp", scatter_dimension=0, tiled=True)
    half = share.shape[0] // 2
    return [(share[:half], None), (share[half:], None)]


def angle_tables():
    half = HD // 2
    rates = 10000.0 ** (-np.arange(half) * 2.0 / HD)
    angles = np.arange(LEN)[:, None] * rates[None, :]
    cosine, sine = np.cos(angles), np.sin(angles)
    return (
        jnp.asarray(np.concatenate([cosine] * 4, axis=-1), F32),
        jnp.asarray(np.concatenate([-sine, sine] * 2, axis=-1), F32),
    )


def swap_halves(value):
    lane = lax.broadcasted_iota(jnp.int32, value.shape, 1)
    low = (lane % HD) < HD // 2
    return jnp.where(
        low, pltpu.roll(value, LANES - HD // 2, 1), pltpu.roll(value, HD // 2, 1)
    )


def put_split(ref, value, core):
    if ref.shape[0] == 1:
        ref[0] = value
        return
    block = value.shape[1] // 8
    for which in (0, 1):

        @pl.when(core == which)
        def _():
            for side in (0, 1):
                for chip in range(4):
                    start = (2 * chip + (which ^ side)) * block
                    ref[side, :, chip * block : (chip + 1) * block] = value[
                        :, start : start + block
                    ]


def split_shape(rows, width):
    return (2, rows, width // 2) if paired() else (1, rows, width)


def project_kernel(fresh, where_ref, x_ref, gain_ref, w_ref, cos_ref, sin_ref, *refs):
    qkv_ref, norm_ref, copy_ref, mark_ref, held = refs[-5:]
    mark_ref[...] = jnp.zeros_like(mark_ref)

    @pl.when(pl.program_id(0) == 0)
    def _():
        value = x_ref[...].astype(F32)
        factor = lax.rsqrt(jnp.mean(value * value, axis=-1, keepdims=True) + EPSILON)
        normed = (value * factor * gain_ref[...]).astype(BF16)
        held[...] = normed
        put_split(norm_ref, normed, where_ref[1])
        copy_ref[...] = x_ref[...]

    product = matmul(held[...], w_ref[...])
    cosine, sine = cos_ref[...], sin_ref[...]
    query = product[:, :LANES]
    key = product[:, LANES : 2 * LANES]
    query = (query * cosine + swap_halves(query) * sine).astype(BF16)
    qkv_ref[:, :LANES] = query * HD**-0.5
    qkv_ref[:, LANES : 2 * LANES] = (key * cosine + swap_halves(key) * sine).astype(BF16)
    qkv_ref[:, 2 * LANES :] = product[:, 2 * LANES :].astype(BF16)


def project(where, piece, gain, weights, tables, held):
    rows, width = piece.shape
    columns = weights.shape[1]
    block = 3 * LANES
    fresh = held is None
    outs = (
        jax.ShapeDtypeStruct((LEN, columns), BF16),
        jax.ShapeDtypeStruct(split_shape(LEN, width), BF16),
        jax.ShapeDtypeStruct((LEN, width), BF16),
        jax.ShapeDtypeStruct((8, LANES), F32),
    )
    specs = [
        pl.BlockSpec((rows, width), lambda i, w: (0, 0)),
        pl.BlockSpec((1, width), lambda i, w: (0, 0)),
        pl.BlockSpec((width, block), lambda i, w: (0, i)),
        pl.BlockSpec((rows, LANES), lambda i, w: (w[0], 0)),
        pl.BlockSpec((rows, LANES), lambda i, w: (w[0], 0)),
    ]
    args = [piece, gain, weights, *tables]
    aliases = {}
    if not fresh:
        for index, array in enumerate(held):
            aliases[1 + len(args)] = index
            args.append(array)
            specs.append(pl.BlockSpec(memory_space=pl.ANY))
    return pl.pallas_call(
        functools.partial(project_kernel, fresh),
        out_shape=outs,
        grid_spec=pltpu.PrefetchScalarGridSpec(
            num_scalar_prefetch=1,
            grid=(columns // block,),
            in_specs=specs,
            out_specs=(
                pl.BlockSpec((rows, block), lambda i, w: (w[0], i)),
                pl.BlockSpec(split_shape(rows, width), lambda i, w: (0, w[0], 0)),
                pl.BlockSpec((rows, width), lambda i, w: (w[0], 0)),
                pl.BlockSpec((8, LANES), lambda i, w: (0, 0)),
            ),
            scratch_shapes=[pltpu.VMEM((rows, width), BF16)],
        ),
        input_output_aliases=aliases,
        compiler_params=params(),
        cost_estimate=cost(11),
        name="project",
    )(where, *args)


PARTS = (
    (0, 512, ((0, 512, True),)),
    (512, 256, ((0, 512, False), (512, 256, True))),
    (768, 256, ((0, 768, False), (768, 256, True))),
)


def visible(shape, first_key, first_query, limit):
    key = first_key + lax.broadcasted_iota(jnp.int32, shape, 0)
    query = first_query + lax.broadcasted_iota(jnp.int32, shape, 1)
    return (key < limit) | (key <= query)


def head_only(value, head):
    lane = lax.broadcasted_iota(jnp.int32, value.shape, 1)
    return jnp.where((lane >= HD) == (head == 1), value, jnp.zeros_like(value))


def attend_kernel(heads, prefix_ref, qkv_ref, out_ref, log_ref, turned):
    limit = prefix_ref[0]
    pair = pl.program_id(0)
    values_across = qkv_ref[:, 2 * LANES :].T
    for head in (0, 1):

        @pl.when(2 * pair + head < heads)
        def _():
            queries = head_only(qkv_ref[:, :LANES], head)
            for first, count, spans in PARTS:
                mine = queries[first : first + count]
                scores = []
                for start, keys, masked in spans:
                    raw = outer_cols(qkv_ref[start : start + keys, LANES : 2 * LANES], mine)
                    if masked:
                        raw = jnp.where(visible(raw.shape, start, first, limit), raw, MASKED)
                    scores.append(raw)
                top = functools.reduce(
                    jnp.maximum, [jnp.max(s, axis=0, keepdims=True) for s in scores]
                )
                total = jnp.zeros_like(top)
                summed = jnp.zeros((HD, count), F32)
                for (start, keys, _), raw in zip(spans, scores):
                    weight = jnp.exp(raw - top)
                    total = total + jnp.sum(weight, axis=0, keepdims=True)
                    summed = summed + matmul(
                        values_across[head * HD : (head + 1) * HD, start : start + keys],
                        weight.astype(BF16),
                    )
                turned[head * HD : (head + 1) * HD, first : first + count] = summed / total
                log_ref[0, head : head + 1, first : first + count] = top + jnp.log(total)

        @pl.when(2 * pair + head >= heads)
        def _():
            turned[head * HD : (head + 1) * HD, :] = jnp.zeros((HD, LEN), F32)
            log_ref[0, head : head + 1, :] = jnp.zeros((1, LEN), F32)

    out_ref[...] = turned[...].T.astype(BF16)


def attend(qkv, prefix, heads):
    pairs = qkv.shape[1] // (3 * LANES)
    return pl.pallas_call(
        functools.partial(attend_kernel, heads),
        out_shape=(
            jax.ShapeDtypeStruct((LEN, pairs * LANES), BF16),
            jax.ShapeDtypeStruct((pairs, 2, LEN), F32),
        ),
        grid_spec=pltpu.PrefetchScalarGridSpec(
            num_scalar_prefetch=1,
            grid=(pairs,),
            in_specs=[pl.BlockSpec((LEN, 3 * LANES), lambda i, s: (0, i))],
            out_specs=(
                pl.BlockSpec((LEN, LANES), lambda i, s: (0, i)),
                pl.BlockSpec((1, 2, LEN), lambda i, s: (i, 0, 0)),
            ),
            scratch_shapes=[pltpu.VMEM((LANES, LEN), F32)],
        ),
        compiler_params=params(),
        cost_estimate=cost(18),
        name="attend",
    )(prefix, qkv)


def attend_back_kernel(
    heads, count, prefix_ref, qkv_ref, out_ref, *refs
):
    arrived = refs[:count]
    log_ref, cos_ref, sin_ref = refs[count : count + 3]
    back_ref, turned, grad_key, grad_value, grad_ref = refs[-5:]
    limit = prefix_ref[0]
    rows = arrived[0].shape[0]
    for k in range(count):
        start = pl.multiple_of(lax.rem(prefix_ref[1] + k, count) * rows, rows)
        grad_ref[pl.ds(start, rows), :] = arrived[k][...]
    pair = pl.program_id(0)
    keys_across = qkv_ref[:, LANES : 2 * LANES].T
    inner = (out_ref[...].astype(F32) * grad_ref[...].astype(F32)).T
    grad_key[...] = jnp.zeros_like(grad_key)
    grad_value[...] = jnp.zeros_like(grad_value)
    for head in (0, 1):
        band = slice(head * HD, (head + 1) * HD)

        @pl.when(2 * pair + head < heads)
        def _():
            queries = head_only(qkv_ref[:, :LANES], head)
            grads = head_only(grad_ref[...], head)
            inner_row = jnp.sum(inner[band], axis=0, keepdims=True)
            for first, count, spans in PARTS:
                here = slice(first, first + count)
                mine, grad_mine = queries[here], grads[here]
                log_mine = log_ref[0, head : head + 1, here]
                inner_mine = inner_row[:, here]
                summed = jnp.zeros((HD, count), F32)
                for start, keys, masked in spans:
                    there = slice(start, start + keys)
                    raw = outer_cols(qkv_ref[there, LANES : 2 * LANES], mine)
                    chance = jnp.exp(raw - log_mine)
                    if masked:
                        chance = jnp.where(
                            visible(raw.shape, start, first, limit), chance, 0.0
                        )
                    grad_chance = outer_cols(qkv_ref[there, 2 * LANES :], grad_mine)
                    grad_score = (chance * (grad_chance - inner_mine)).astype(BF16)
                    grad_key[there, :] += matmul(grad_score, mine)
                    grad_value[there, :] += matmul(chance.astype(BF16), grad_mine)
                    summed = summed + matmul(keys_across[band, there], grad_score)
                turned[band, here] = summed

        @pl.when(2 * pair + head >= heads)
        def _():
            turned[band, :] = jnp.zeros((HD, LEN), F32)

    cosine, sine = cos_ref[...], sin_ref[...]
    grad_query = turned[...].T * HD**-0.5
    back_ref[:, :LANES] = (grad_query * cosine - swap_halves(grad_query) * sine).astype(BF16)
    back = grad_key[...]
    back_ref[:, LANES : 2 * LANES] = (back * cosine - swap_halves(back) * sine).astype(BF16)
    back_ref[:, 2 * LANES :] = grad_value[...].astype(BF16)


def attend_back(qkv, attended, arrived, log_total, tables, prefix, heads, waits=()):
    pairs = qkv.shape[1] // (3 * LANES)
    count, rows = len(arrived), arrived[0].shape[0]
    return pl.pallas_call(
        functools.partial(attend_back_kernel, heads, count),
        out_shape=jax.ShapeDtypeStruct(qkv.shape, BF16),
        grid_spec=pltpu.PrefetchScalarGridSpec(
            num_scalar_prefetch=1,
            grid=(pairs,),
            in_specs=[
                pl.BlockSpec((LEN, 3 * LANES), lambda i, s: (0, i)),
                pl.BlockSpec((LEN, LANES), lambda i, s: (0, i)),
            ]
            + [pl.BlockSpec((rows, LANES), lambda i, s: (0, i))] * count
            + [
                pl.BlockSpec((1, 2, LEN), lambda i, s: (i, 0, 0)),
                pl.BlockSpec((LEN, LANES), lambda i, s: (0, 0)),
                pl.BlockSpec((LEN, LANES), lambda i, s: (0, 0)),
            ]
            + after_all(waits),
            out_specs=pl.BlockSpec((LEN, 3 * LANES), lambda i, s: (0, i)),
            scratch_shapes=[
                pltpu.VMEM((LANES, LEN), F32),
                pltpu.VMEM((LEN, LANES), F32),
                pltpu.VMEM((LEN, LANES), F32),
                pltpu.VMEM((LEN, LANES), BF16),
            ],
        ),
        compiler_params=params(),
        cost_estimate=cost(28),
        name="attend_back",
    )(prefix, qkv, attended, *arrived, log_total, *tables, *waits)


def middle_kernel(count, place_ref, *refs):
    pieces = refs[:count]
    w_ref, x_ref, gain_ref, normed_ref, own_ref = refs[count:]
    depth = pieces[0].shape[1]
    total = None
    for k in range(count):
        term = outer_cols(pieces[k][...], w_ref[:, k * depth : (k + 1) * depth])
        total = term if total is None else total + term
    middle = x_ref[...].astype(F32) + BRANCH * total
    factor = lax.rsqrt(jnp.mean(middle * middle, axis=-1, keepdims=True) + EPSILON)
    normed_ref[...] = (middle * factor * gain_ref[...]).astype(BF16)
    rows, own = x_ref.shape[0], own_ref.shape[0]
    for part in range(rows // own):

        @pl.when(pl.program_id(0) * (rows // own) + part == place_ref[0])
        def _():
            own_ref[...] = middle[part * own : (part + 1) * own]


def finish_middle(place, pieces, weights, tokens, gain, own):
    width = tokens.shape[1]
    depth = pieces[0].shape[1]
    count = len(pieces)
    rows = 2 * own
    return pl.pallas_call(
        functools.partial(middle_kernel, count),
        out_shape=(
            jax.ShapeDtypeStruct((LEN, width), BF16),
            jax.ShapeDtypeStruct((own, width), F32),
        ),
        grid_spec=pltpu.PrefetchScalarGridSpec(
            num_scalar_prefetch=1,
            grid=(LEN // rows,),
            in_specs=[pl.BlockSpec((rows, depth), lambda i, s: (i, 0))] * count
            + [
                pl.BlockSpec((width, count * depth), lambda i, s: (0, 0)),
                pl.BlockSpec((rows, width), lambda i, s: (i, 0)),
                pl.BlockSpec((1, width), lambda i, s: (0, 0)),
            ],
            out_specs=(
                pl.BlockSpec((rows, width), lambda i, s: (i, 0)),
                pl.BlockSpec((own, width), lambda i, s: (0, 0)),
            ),
        ),
        compiler_params=params(),
        cost_estimate=cost(22),
        name="finish_middle",
    )(place, *pieces, weights, tokens, gain)


def gate_kernel(normed_ref, weight_ref, hidden_ref, slope_ref):
    rows = 256
    for start in range(0, LEN, rows):
        here = slice(start, start + rows)
        product = matmul(normed_ref[here], weight_ref[...])
        gate, up = product[:, :FF_BLOCK], product[:, FF_BLOCK:]
        sigmoid = jax.nn.sigmoid(gate)
        silu = gate * sigmoid
        hidden_ref[here, :] = (silu * up).astype(BF16)
        slope_ref[here, :FF_BLOCK] = (up * (sigmoid + silu * (1.0 - sigmoid))).astype(BF16)
        slope_ref[here, FF_BLOCK:] = silu.astype(BF16)


def feed(normed, gate_up):
    width = normed.shape[1]
    hidden = gate_up.shape[1] // 2
    return pl.pallas_call(
        gate_kernel,
        out_shape=(
            jax.ShapeDtypeStruct((LEN, hidden), BF16),
            jax.ShapeDtypeStruct((LEN, 2 * hidden), BF16),
        ),
        grid=(hidden // FF_BLOCK,),
        in_specs=[
            pl.BlockSpec((LEN, width), lambda i: (0, 0)),
            pl.BlockSpec((width, 2 * FF_BLOCK), lambda i: (0, i)),
        ],
        out_specs=(
            pl.BlockSpec((LEN, FF_BLOCK), lambda i: (0, i)),
            pl.BlockSpec((LEN, 2 * FF_BLOCK), lambda i: (0, i)),
        ),
        compiler_params=params(),
        cost_estimate=cost(21),
        name="feed",
    )(normed, gate_up)


def feed_back_kernel(where_ref, grad_ref, slope_ref, down_ref, weight_ref, *refs):
    both_ref, copy_ref, sum_ref, total = refs[-4:]
    step = pl.program_id(0)

    @pl.when(step == 0)
    def _():
        copy_ref[...] = grad_ref[...]
        total[...] = jnp.zeros_like(total)

    grad = matmul(grad_ref[...], down_ref[...])
    grads = jnp.concatenate([grad, grad], axis=1)
    both = (grads * slope_ref[...].astype(F32)).astype(BF16)
    both_ref[...] = both
    total[...] += outer_cols(both, weight_ref[...])

    @pl.when(step == pl.num_programs(0) - 1)
    def _():
        sum_ref[...] = total[...].astype(sum_ref.dtype)


def feed_back(where, piece, slopes, down, gate_up, held, kind, waits=()):
    rows, width = piece.shape
    hidden = down.shape[1]
    specs = [
        pl.BlockSpec((rows, width), lambda i, w: (0, 0)),
        pl.BlockSpec((rows, 2 * FF_BLOCK), lambda i, w: (w[0], i)),
        pl.BlockSpec((width, FF_BLOCK), lambda i, w: (0, i)),
        pl.BlockSpec((width, 2 * FF_BLOCK), lambda i, w: (0, i)),
    ]
    args = [piece, slopes, down, gate_up]
    aliases = {}
    if held is not None:
        for index, array in enumerate(held):
            aliases[1 + len(args)] = index
            args.append(array)
            specs.append(pl.BlockSpec(memory_space=pl.ANY))
    args += waits
    specs += after_all(waits)
    return pl.pallas_call(
        feed_back_kernel,
        out_shape=(
            jax.ShapeDtypeStruct((LEN, 2 * hidden), BF16),
            jax.ShapeDtypeStruct((LEN, width), BF16),
            jax.ShapeDtypeStruct((rows, width), kind),
        ),
        grid_spec=pltpu.PrefetchScalarGridSpec(
            num_scalar_prefetch=1,
            grid=(hidden // FF_BLOCK,),
            in_specs=specs,
            out_specs=(
                pl.BlockSpec((rows, 2 * FF_BLOCK), lambda i, w: (w[0], i)),
                pl.BlockSpec((rows, width), lambda i, w: (w[0], 0)),
                pl.BlockSpec((rows, width), lambda i, w: (0, 0)),
            ),
            scratch_shapes=[pltpu.VMEM((rows, width), F32)],
        ),
        input_output_aliases=aliases,
        compiler_params=params(),
        cost_estimate=cost(15),
        name="feed_back",
    )(where, *args)


def out_sum_kernel(parts, count, width, *refs):
    terms, outs = grouped(parts, refs)
    half = outs[0].shape[0] // 2
    for index, pair in enumerate(terms):
        value = added(pair)
        here = slice(index * half, (index + 1) * half)
        for k in range(count):
            outs[k][here, :] = value[:, k * width : (k + 1) * width].astype(outs[k].dtype)


def out_sum(parts, count, width):
    rows = 2 * parts[0][0].shape[0]
    arrays = [a for pair in parts for a in pair if a is not None]
    return pl.pallas_call(
        functools.partial(out_sum_kernel, parts_mask(parts), count, width),
        out_shape=tuple(
            jax.ShapeDtypeStruct((rows, width), BF16 if k else F32) for k in range(count)
        ),
        compiler_params=params(),
        cost_estimate=cost(3),
        name="out_sum",
    )(*arrays)


def out_final_kernel(*refs):
    total = refs[0][...]
    for ref in refs[1:-1]:
        total = total + ref[...].astype(F32)
    refs[-1][...] = total.T[: refs[-1].shape[0]]


def out_final(own, moved, width):
    return pl.pallas_call(
        out_final_kernel,
        out_shape=jax.ShapeDtypeStruct((width, own.shape[0]), F32),
        compiler_params=params(),
        cost_estimate=cost(3),
        name="out_final",
    )(own, *moved)


def norm_back(value, gain, incoming):
    factor = lax.rsqrt(jnp.mean(value * value, axis=-1, keepdims=True) + EPSILON)
    normed = value * factor
    scaled_in = incoming * gain
    inner = jnp.mean(scaled_in * normed, axis=-1, keepdims=True)
    return (
        factor * (scaled_in - normed * inner),
        jnp.sum(incoming * normed, axis=0, keepdims=True),
    )


def own_back_kernel(
    core_ref, term_ref, arrived_ref, middle_ref, grad_ref, gain_ref, *refs
):
    sum_ref, send_ref, split_ref, gain_sum_ref, zero_ref = refs[-5:]
    incoming = term_ref[...].astype(F32) + arrived_ref[...].astype(F32)
    back, gain_sum = norm_back(middle_ref[...], gain_ref[...], incoming)
    total = grad_ref[...].astype(F32) + back
    sum_ref[...] = total
    sent = (BRANCH * total).astype(BF16)
    send_ref[...] = sent
    put_split(split_ref, sent, core_ref[0])
    zero_ref[0] = 0

    @pl.when(pl.program_id(0) == 0)
    def _():
        gain_sum_ref[...] = jnp.zeros_like(gain_sum_ref)

    gain_sum_ref[...] += gain_sum


def own_back(core, term, arrived, middle, grad, gain, waits=()):
    rows, width = middle.shape
    step = rows // 2
    block = pl.BlockSpec((step, width), lambda i, s: (i, 0))
    line = pl.BlockSpec((1, width), lambda i, s: (0, 0))
    return pl.pallas_call(
        own_back_kernel,
        out_shape=(
            jax.ShapeDtypeStruct((rows, width), F32),
            jax.ShapeDtypeStruct((rows, width), BF16),
            jax.ShapeDtypeStruct(split_shape(rows, width), BF16),
            jax.ShapeDtypeStruct((1, width), F32),
            jax.ShapeDtypeStruct((1,), jnp.int32),
        ),
        grid_spec=pltpu.PrefetchScalarGridSpec(
            num_scalar_prefetch=1,
            grid=(2,),
            in_specs=[block, block, block, block, line] + after_all(waits),
            out_specs=(
                block,
                block,
                pl.BlockSpec(split_shape(step, width), lambda i, s: (0, i, 0)),
                line,
                pl.BlockSpec(memory_space=pltpu.SMEM),
            ),
        ),
        compiler_params=params(),
        cost_estimate=cost(5),
        name="own_back",
    )(core, term, arrived, middle, grad, gain, *waits)


def finish_input_kernel(term_ref, arrived_ref, x_ref, sum_ref, gain_ref, *refs):
    out_ref, gain_sum_ref, zero_ref = refs[-3:]
    incoming = term_ref[...] + arrived_ref[...].astype(F32)
    back, gain_sum = norm_back(x_ref[...].astype(F32), gain_ref[...], incoming)
    out_ref[...] = (sum_ref[...] + back).astype(BF16)
    zero_ref[0] = 0

    @pl.when(pl.program_id(0) == 0)
    def _():
        gain_sum_ref[...] = jnp.zeros_like(gain_sum_ref)

    gain_sum_ref[...] += gain_sum


def finish_input(term, arrived, x, total, gain, waits=()):
    rows, width = x.shape
    block = pl.BlockSpec((rows // 2, width), lambda i: (i, 0))
    line = pl.BlockSpec((1, width), lambda i: (0, 0))
    return pl.pallas_call(
        finish_input_kernel,
        out_shape=(
            jax.ShapeDtypeStruct((rows, width), BF16),
            jax.ShapeDtypeStruct((1, width), F32),
            jax.ShapeDtypeStruct((1,), jnp.int32),
        ),
        grid=(2,),
        in_specs=[block, block, block, block, line] + after_all(waits),
        out_specs=(block, line, pl.BlockSpec(memory_space=pltpu.SMEM)),
        compiler_params=params(),
        cost_estimate=cost(5),
        name="finish_input",
    )(term, arrived, x, total, gain, *waits)


def finish_block_kernel(middle_ref, term_ref, arrived_ref, *refs):
    total = term_ref[...] + arrived_ref[...].astype(F32)
    refs[-1][...] = (middle_ref[...] + BRANCH * total).astype(BF16)


def finish_block(middle, term, arrived, waits=()):
    rows, width = middle.shape
    block = pl.BlockSpec((rows // 2, width), lambda i: (i, 0))
    return pl.pallas_call(
        finish_block_kernel,
        out_shape=jax.ShapeDtypeStruct((rows, width), BF16),
        grid=(2,),
        in_specs=[block, block, block] + after_all(waits),
        out_specs=block,
        compiler_params=params(),
        cost_estimate=cost(3),
        name="finish_block",
    )(middle, term, arrived, *waits)


def mix(out_ref, refs, block):
    width = refs[0].shape[1]
    count = len(refs)
    for first in range(0, width, block):
        size = min(block, width - first)
        base = first * count
        for index, ref in enumerate(refs):
            spot = base + index * block
            out_ref[:, spot : spot + size] = ref[:, first : first + size]
            if size < block:
                out_ref[:, spot + size : spot + block] = jnp.zeros(
                    (ref.shape[0], block - size), out_ref.dtype
                )


def put_across(out_ref, value):
    rows = value.shape[0]
    out_ref[:, :rows] = value.T
    if rows < out_ref.shape[1]:
        out_ref[:, rows:] = jnp.zeros((out_ref.shape[0], out_ref.shape[1] - rows), BF16)


def pack_kernel(count, block, *refs):
    if count == 1:
        put_across(refs[-1], refs[0][...])
    else:
        mix(refs[-1], refs[:count], block)


def pack(values, block, width, *waits):
    count = len(values)
    rows = values[0].shape[0] if count > 1 else values[0].shape[1]
    whole = pl.BlockSpec(memory_space=pltpu.VMEM)
    return pl.pallas_call(
        functools.partial(pack_kernel, count, block),
        out_shape=jax.ShapeDtypeStruct((rows, count * width), BF16),
        in_specs=[whole] * count + [pl.BlockSpec(memory_space=pl.ANY)] * len(waits),
        out_specs=whole,
        compiler_params=params(),
        cost_estimate=cost(3),
        name="pack",
    )(*values, *waits)


def chain_kernel(count, *refs):
    out_ref = refs[-1]
    width = refs[0].shape[1]
    for k in range(count):
        out_ref[:, k * width : (k + 1) * width] = refs[k][...]


def chain(values, *waits):
    rows, width = values[0].shape
    whole = pl.BlockSpec(memory_space=pltpu.VMEM)
    return pl.pallas_call(
        functools.partial(chain_kernel, len(values)),
        out_shape=jax.ShapeDtypeStruct((rows, len(values) * width), values[0].dtype),
        in_specs=[whole] * len(values) + after_all(waits),
        out_specs=whole,
        compiler_params=params(),
        cost_estimate=cost(2),
        name="chain",
    )(*values, *waits)


def scale_kernel(value_ref, *refs):
    refs[-1][...] = (BRANCH * value_ref[...].astype(F32)).astype(BF16)


def scaled(value, *waits):
    whole = pl.BlockSpec(memory_space=pltpu.VMEM)
    return pl.pallas_call(
        scale_kernel,
        out_shape=jax.ShapeDtypeStruct(value.shape, BF16),
        in_specs=[whole] + [pl.BlockSpec(memory_space=pl.ANY)] * len(waits),
        out_specs=whole,
        compiler_params=params(),
        cost_estimate=cost(3),
        name="scaled",
    )(value, *waits)


def added(terms):
    one, two = terms
    value = one[...].astype(F32)
    return value if two is None else value + two[...].astype(F32)


def grouped(parts, refs):
    refs = list(refs)
    out = [tuple(None if a is None else refs.pop(0) for a in pair) for pair in parts]
    return out, refs


def unmix_kernel(parts, block, *refs):
    terms, outs = grouped(parts, refs)
    width = outs[0].shape[1]
    half = outs[0].shape[0] // 2
    for index, pair in enumerate(terms):
        value = added(pair)
        for first in range(0, width, block):
            size = min(block, width - first)
            for turn, out_ref in enumerate(outs):
                spot = first * len(outs) + turn * block
                out_ref[index * half : (index + 1) * half, first : first + size] = value[
                    :, spot : spot + size
                ]


def unmix(parts, count, block, width):
    rows = 2 * parts[0][0].shape[0]
    arrays = [a for pair in parts for a in pair if a is not None]
    return pl.pallas_call(
        functools.partial(unmix_kernel, parts_mask(parts), block),
        out_shape=tuple(jax.ShapeDtypeStruct((rows, width), F32) for _ in range(count)),
        compiler_params=params(),
        name="unmix",
    )(*arrays)


def parts_mask(parts):
    return [tuple(None if a is None else True for a in pair) for pair in parts]


def turn_kernel(parts, *refs):
    terms, (out_ref,) = grouped(parts, refs)
    value = jnp.concatenate([added(pair) for pair in terms], axis=0)
    out_ref[...] = value.T[: out_ref.shape[0]]


def turn(parts, width):
    rows = 2 * parts[0][0].shape[0]
    arrays = [a for pair in parts for a in pair if a is not None]
    return pl.pallas_call(
        functools.partial(turn_kernel, parts_mask(parts)),
        out_shape=jax.ShapeDtypeStruct((width, rows), F32),
        compiler_params=params(),
        name="turn",
    )(*arrays)


def body(
    tokens,
    attn_gain,
    mlp_gain,
    w_query,
    w_key,
    w_value,
    w_out,
    w_gate,
    w_up,
    w_down,
    prefix,
    out_grad,
):
    mp = lax.axis_size("mp")
    place = lax.axis_index("mp")
    rows = tokens.shape[0]
    width_heads = w_query.shape[1]
    heads = width_heads // HD
    padded_heads = round_up(width_heads, LANES)
    width_ff = w_gate.shape[1]
    padded_ff = round_up(width_ff, FF_BLOCK)
    own = place * rows

    def row_block(value, index):
        return lax.dynamic_slice_in_dim(value, index * rows, rows, 0)

    tables = angle_tables()
    core = lax.axis_index("dp") % 2
    at = [jnp.stack([(place + mp - k) % mp, core]) for k in range(mp)]

    attn_weights = dp_gather(pack([w_query, w_key, w_value], LANES, padded_heads))
    token_pieces = [tokens, ring_up(tokens)]
    ff_pack = pack([w_gate, w_up], FF_BLOCK, padded_ff, token_pieces[1])
    gate_up = dp_gather(ff_pack)
    token_pieces.append(ring_up(token_pieces[1]))
    token_pieces.append(ring_up(token_pieces[2]))
    held = None
    for k in range(mp - 1):
        *held, mark = project(
            at[k], token_pieces[k], attn_gain[None], attn_weights, tables, held
        )
    out_own = pack([w_out], LANES, padded_heads, token_pieces[-1], mark, ff_pack)
    out_pieces = [out_own] + [shift_back(out_own, mp - j) for j in range(1, mp)]
    *held, _ = project(
        at[mp - 1], token_pieces[-1], attn_gain[None], attn_weights, tables, held
    )
    qkv, normed_one, whole_tokens = held
    attended, log_total = attend(qkv, prefix, heads)
    out_pack = chain(out_pieces, attended)
    attended_pieces = [attended, ring_up(attended)]
    out_weights = dp_gather(gate(out_pack, attended_pieces[1], gate_up))
    down_pack = pack([w_down], LANES, padded_ff, attended_pieces[1])
    down = dp_gather(down_pack)
    while len(attended_pieces) < mp:
        attended_pieces.append(ring_up(attended_pieces[-1]))

    grad_own = scaled(out_grad, attended_pieces[-1], down_pack)
    grad_pieces = [grad_own] + [shift_back(grad_own, mp - k) for k in range(1, mp)]
    normed_two, middle = finish_middle(
        at[0], attended_pieces, out_weights, whole_tokens, mlp_gain[None], rows
    )
    hidden, slopes = feed(normed_two, gate_up)

    def back_of(k, held, kind=BF16, waits=()):
        *held, term = feed_back(
            at[k % mp], grad_pieces[k % mp], slopes, down, gate_up, held, kind, waits
        )
        return held, term

    width = normed_two.shape[1]
    grad_pieces.append(ring_up(grad_pieces[-1]))
    held, total = back_of(1, None)
    held, term = back_of(2, held)
    arrived = ring_up(total)
    held, term_three = back_of(3, held)
    (grad_both, grad_mlp), term_own = back_of(4, held, F32)
    total = join(term, arrived, (term_own,))
    arrived = ring_up(total)
    ff_weight = weight_grad(normed_two, grad_both, 0, width // 2, padded_ff, 21)
    total = join(term_three, arrived, (ff_weight,))
    arrived = ring_up(total)
    down_weight = weight_grad(grad_mlp, hidden, 0, width // 2, padded_ff // 2, 12)
    grad_middle, grad_attn, split_attn, gain_two, zero = own_back(
        core[None], term_own, arrived, middle, out_grad, mlp_gain[None], (down_weight,)
    )
    ff_share = scatter_whole(gate(ff_weight, total))
    down_share = scatter_whole(gate(down_weight, zero))

    grad_attended = matmul(grad_attn, out_weights).astype(BF16)
    mine = [
        grad_attended[:, k * padded_heads : (k + 1) * padded_heads] for k in range(mp)
    ]
    attended_own = jnp.concatenate(
        [row_block(piece, place) for piece in attended_pieces], axis=1
    )

    def mlp_chunk(k, zero):
        return lax.optimization_barrier(
            outer_cols(row_block(hidden, at[k % mp][0] + zero[0]), down)
        )

    by_chip = paired()
    arrived = [mine[0]] + [shift_back(mine[k], k) for k in range(1, mp)]
    out_other = scatter_other(split_attn, attended_own, 1280, 5, (grad_attended,))
    chunk_one = mlp_chunk(1, zero).astype(BF16)
    chunk_two = mlp_chunk(2, zero)
    mlp_arrived = ring_up(gate(chunk_one, *arrived[1:]))
    out_arrived = swap(out_other, 1) if by_chip else None
    spots = jnp.stack([prefix[0], place])
    back = attend_back(
        qkv, attended, arrived, log_total, tables, spots, heads,
        (chunk_two, out_other) if by_chip else (chunk_two,),
    )

    def grad_one_term(k, zero=0):
        return lax.optimization_barrier(
            outer_cols(row_block(back, at[k % mp][0] + zero), attn_weights)
        )

    total = grad_one_term(1).astype(BF16)
    arrived = ring_up(total)
    attn_other = scatter_other(normed_one, back, 640, 8, (total,))
    attn_arrived = swap(attn_other, 1) if by_chip else None
    out_chip = scatter_mine(split_attn, attended_own, 1280, 5, out_arrived, (total,))
    term = grad_one_term(2)
    total, zero = join_marked(term, arrived, (out_chip, attn_other) if by_chip else ())
    arrived = ring_up(total)
    mlp_total = join(chunk_two, mlp_arrived, (total,))
    mlp_arrived = ring_up(mlp_total)
    attn_chip = scatter_mine(normed_one, back, 640, 8, attn_arrived, (total,))
    if by_chip:
        out_kept, out_moved = scatter_first(out_chip)
        attn_kept, attn_moved = scatter_first(attn_chip)
    term = grad_one_term(3, zero[0])
    chunk = mlp_chunk(3, zero)
    total, zero = join_marked(term, arrived, (attn_chip,))
    arrived = ring_up(total)
    if by_chip:
        out_half = scatter_join(out_kept, out_moved, (total,))
        out_share = scatter_second(out_half)
        attn_half = scatter_join(attn_kept, attn_moved, (total, *out_half))
        attn_share = scatter_second(attn_half)
        mlp_total = join(chunk, mlp_arrived, (total, *out_half))
    else:
        out_share = scatter_whole(out_chip)
        attn_share = scatter_whole(attn_chip)
        mlp_total = join(chunk, mlp_arrived, (total,))
    term = grad_one_term(4, zero[0])
    mlp_arrived = ring_up(mlp_total)
    input_grad, gain_one, zero = finish_input(
        term, arrived, tokens, grad_middle, attn_gain[None], (mlp_total,)
    )
    out_total, *out_mine = out_sum(out_share, mp, padded_heads)
    out_moved = [shift_back(out_mine[k - 1], k) for k in range(1, mp)]
    gains = sum_all(jnp.concatenate([gain_one, gain_two]))
    chunk = mlp_chunk(4, zero)
    grad_w_query, grad_w_key, grad_w_value = unmix(attn_share, 3, LANES, width_heads)
    grad_w_gate, grad_w_up = unmix(ff_share, 2, FF_BLOCK, width_ff)
    grad_w_down = turn(down_share, width_ff)
    grad_w_out = out_final(out_total, out_moved, width_heads)
    block_out = finish_block(
        middle, chunk, mlp_arrived, (grad_w_gate, grad_w_down, grad_w_query, grad_w_out)
    )
    return (
        block_out,
        input_grad,
        grad_w_query,
        grad_w_key,
        grad_w_value,
        grad_w_out,
        grad_w_gate,
        grad_w_up,
        grad_w_down,
        gains[0],
        gains[1],
    )


def solution(mesh):
    return jax.shard_map(
        body,
        mesh=mesh,
        in_specs=(
            P(("dp", "mp"), None),
            P(),
            P(),
            P("dp", "mp"),
            P("dp", "mp"),
            P("dp", "mp"),
            P("mp", "dp"),
            P("dp", "mp"),
            P("dp", "mp"),
            P("mp", "dp"),
            P("dp"),
            P(("dp", "mp"), None),
        ),
        out_specs=(
            P(("dp", "mp"), None),
            P(("dp", "mp"), None),
            P("dp", "mp"),
            P("dp", "mp"),
            P("dp", "mp"),
            P("mp", "dp"),
            P("dp", "mp"),
            P("dp", "mp"),
            P("mp", "dp"),
            P(),
            P(),
        ),
        check_vma=False,
    )
```

time: 1050 us -> 844 us (0.80)
  waiting for transfers between devices: 422 us -> 253 us
  matrix products: 185 us -> 65.1 us
  starting transfers between devices: 28.2 us -> 87.2 us
  Pallas kernels: 300 us -> 349 us
  other arithmetic: 25.4 us -> 5.04 us
    ppermute x21 -> x15, waiting for transfers between devices: 346 us -> 135 us  [ring_up(): return lax.ppermute(value, 'mp', [(i, (i + 1) % n) for i in range(n)])]
    ppermute x6 -> x12, waiting for transfers between devices: 14.5 us -> 93.4 us  [shift_back(): return lax.ppermute(value, 'mp', [(i, (i - count) % n) for i in range(n)])]
    dot_general x16 -> x8, matrix products: 121 us -> 57.6 us  [outer_cols(): lax.dot_general(left, right, (((1,), (1,)), ((), ())), preferred_element_...]
    dot_general x4 -> x0, matrix products: 55.8 us -> none  [inner_rows(): lax.dot_general(left, right, (((0,), (0,)), ((), ())), preferred_element_...]
    pallas_call x4 -> x41, Pallas kernels: 243 us -> 286 us  [the longest x4 69 us: feed_back(): pl.pallas_call(feed_back_kernel, out_shape=(jax.ShapeDtypeStruct((LEN, 2...]
    ppermute x21 -> x15, starting transfers between devices: 19.2 us -> 60.3 us  [ring_up(): return lax.ppermute(value, 'mp', [(i, (i + 1) % n) for i in range(n)])]
    reduce_scatter x4 -> x2, waiting for transfers between devices: 31.3 us -> 0.01 us  [scatter_whole(): share = lax.psum_scatter(partial, 'dp', scatter_dimension=0, tiled=True)]
    ppermute x5, waiting for transfers between devices: 30 us -> 0.25 us  [sum_all(): value = value + lax.ppermute(value, axis, [(i, i ^ bit) for i in range(n)])]
  transfers between devices with their start and end apart: 40 -> 48, of which waited for: 23 -> 19; matrix products, arithmetic and copies ran while one was open for 22% -> 13% of each run, Pallas kernels for 26% -> 40%
where the time goes in v2:
time: 844 us; the launch traced here: 834 us
  Pallas kernels  349 us (41%)
  waiting for transfers between devices  253 us (30%)
  starting transfers between devices  87.2 us (10%)
  matrix products  65.1 us (8%)
  local copies, waits for them, and re-layouts  55.5 us (7%)
  between operations  18.9 us (2%)
    ppermute x15, waiting for transfers between devices, ring_up(): return lax.ppermute(value, 'mp', [(i, (i + 1) % n) for i in range(n)])  135 us
    ppermute x12, waiting for transfers between devices, shift_back(): return lax.ppermute(value, 'mp', [(i, (i - count) % n) for i in range(n)])  93.4 us
    pallas_call x4, Pallas kernels, feed_back(): pl.pallas_call(feed_back_kernel, out_shape=(jax.ShapeDtypeStruct((LEN, 2...  69 us
    pallas_call x6, Pallas kernels, weight_grad(): pl.pallas_call(functools.partial(weight_kernel, arrived is not None), out...  63.2 us
    ppermute x15, starting transfers between devices, ring_up(): return lax.ppermute(value, 'mp', [(i, (i + 1) % n) for i in range(n)])  60.3 us
    dot_general x8, matrix products, outer_cols(): lax.dot_general(left, right, (((1,), (1,)), ((), ())), preferred_element_...  57.6 us
    pallas_call x4, Pallas kernels, project(): pl.pallas_call(functools.partial(project_kernel, fresh), out_shape=outs,...  45.1 us
    pallas_call x10, Pallas kernels, join_marked(): pl.pallas_call(join_kernel, out_shape=(jax.ShapeDtypeStruct(one.shape, BF...  31 us
  transfers between devices with their start and end apart: 48, of which 19 were waited for; matrix products, arithmetic and copies ran while one was open for 13% of the time, Pallas kernels for 40%

profile of v2, /device:TPU:0, one launch (start us, length us, event | category | flops | bytes accessed | tf_op | source)
XLA Modules:
  0.0 834.5 jit_solution(14039892585916302549)
XLA Ops:
  12.9 28.0 %collective-permute-done.x_ref.refs_2_ = bf16[256,2304]{1,0:T(8,128)(2,1)S(1)} collective-permute-done((bf16[256,2304]{1,0:T(8,128)(2,1)S(1)}, bf16[256,2304]{1,0:T(8,128)(2,1)S(1)}, u32[]{:S(2)}, u32[]{:S(2)}) %collective-permute-start) | collective-permute-done | bytes 1179680 | tf_op jit(solution)/shard_map/ppermute | solution.py:56
  50.2 24.3 %collective-permute-done.1.x_ref = bf16[256,2304]{1,0:T(8,128)(2,1)S(1)} collective-permute-done((bf16[256,2304]{1,0:T(8,128)(2,1)}, bf16[256,2304]{1,0:T(8,128)(2,1)S(1)}, u32[]{:S(2)}, u32[]{:S(2)}) %collective-permute-start.1) | collective-permute-done | bytes 1179680 | tf_op jit(solution)/shard_map/ppermute | solution.py:56
  74.6 11.7 %project.4 = (bf16[1024,1920]{1,0:T(8,128)(2,1)}, bf16[2,1024,1152]{2,1,0:T(8,128)(2,1)}, bf16[1024,2304]{1,0:T(8,128)(2,1)}, f32[8,128]{1,0:T(8,128)}) custom-call(s32[2]{0:T(128)} %pad_add_fusion.where_ref.place_ref, bf16[256,2304]{1,0:T(8,128)(2,1)} %x_ref.3, f32[1,2304]{1,0:T(1,128)} %broadcast_in_dim.4.gain_ref, ...), custom_call_target="tpu_custom_call" | custom-call | flops 32999999488 | tf_op jit(solution)/shard_map/project/pallas_call | solution.py:340
  86.2 11.0 %project.5 = (bf16[1024,1920]{1,0:T(8,128)(2,1)}, bf16[2,1024,1152]{2,1,0:T(8,128)(2,1)}, bf16[1024,2304]{1,0:T(8,128)(2,1)}, f32[8,128]{1,0:T(8,128)}) custom-call(s32[2]{0:T(128)} %pad_add_fusion.3.where_ref, bf16[256,2304]{1,0:T(8,128)(2,1)} %copy-done.14, ...), custom_call_target="tpu_custom_call", output_to_operand_aliasing={{0}: (6, {}), {1}: (7, {}), {2}: (8, {})} | custom-call | flops 32999999488 | tf_op jit(solution)/shard_map/project/pallas_call | solution.py:340
  97.2 11.0 %project.6 = (bf16[1024,1920]{1,0:T(8,128)(2,1)}, bf16[2,1024,1152]{2,1,0:T(8,128)(2,1)}, bf16[1024,2304]{1,0:T(8,128)(2,1)}, f32[8,128]{1,0:T(8,128)}) custom-call(s32[2]{0:T(128)} %pad_add_fusion.2.where_ref, bf16[256,2304]{1,0:T(8,128)(2,1)} %copy-done.15, ...), custom_call_target="tpu_custom_call", output_to_operand_aliasing={{0}: (6, {}), {1}: (7, {}), {2}: (8, {})} | custom-call | flops 32999999488 | tf_op jit(solution)/shard_map/project/pallas_call | solution.py:340
  109.2 11.5 %project.7 = (bf16[1024,1920]{1,0:T(8,128)(2,1)}, bf16[2,1024,1152]{2,1,0:T(8,128)(2,1)}, bf16[1024,2304]{1,0:T(8,128)(2,1)}, f32[8,128]{1,0:T(8,128)}) custom-call(s32[2]{0:T(128)} %pad_add_fusion.1.where_ref, bf16[256,2304]{1,0:T(8,128)(2,1)} %copy-done.19, ...), custom_call_target="tpu_custom_call", output_to_operand_aliasing={{0}: (6, {}), {1}: (7, {}), {2}: (8, {})} | custom-call | flops 32999999488 | tf_op jit(solution)/shard_map/project/pallas_call | solution.py:340
  120.7 18.3 %attend.1 = (bf16[1024,640]{1,0:T(8,128)(2,1)}, f32[5,2,1024]{2,1,0:T(2,128)}) custom-call(s32[1]{0:T(128)S(6)} %copy.75.prefix_ref, bf16[1024,1920]{1,0:T(8,128)(2,1)} %get-tuple-element.80.qkv_ref), custom_call_target="tpu_custom_call" | custom-call | flops 54000001024 | tf_op jit(solution)/shard_map/attend/pallas_call | solution.py:422
  148.1 32.7 %collective-permute-done.6.refs_1_ = bf16[288,640]{1,0:T(8,128)(2,1)S(1)} collective-permute-done((bf16[288,640]{1,0:T(8,128)(2,1)}, bf16[288,640]{1,0:T(8,128)(2,1)S(1)}, u32[]{:S(2)}, u32[]{:S(2)}) %collective-permute-start.6) | collective-permute-done | bytes 368672 | tf_op jit(solution)/shard_map/ppermute | solution.py:80
  180.7 13.5 %collective-permute-done.7.refs_2_ = bf16[288,640]{1,0:T(8,128)(2,1)S(1)} collective-permute-done((bf16[288,640]{1,0:T(8,128)(2,1)}, bf16[288,640]{1,0:T(8,128)(2,1)S(1)}, u32[]{:S(2)}, u32[]{:S(2)}) %collective-permute-start.7) | collective-permute-done | bytes 368672 | tf_op jit(solution)/shard_map/ppermute | solution.py:80
  207.2 28.5 %collective-permute-done.4.refs_2_ = bf16[1024,640]{1,0:T(8,128)(2,1)S(1)} collective-permute-done((bf16[1024,640]{1,0:T(8,128)(2,1)}, bf16[1024,640]{1,0:T(8,128)(2,1)S(1)}, u32[]{:S(2)}, u32[]{:S(2)}) %collective-permute-start.4) | collective-permute-done | bytes 1310752 | tf_op jit(solution)/shard_map/ppermute | solution.py:56
  242.6 24.7 %collective-permute-done.5.refs_3_.refs_0_ = bf16[1024,640]{1,0:T(8,128)(2,1)S(1)} collective-permute-done((bf16[1024,640]{1,0:T(8,128)(2,1)S(1)}, bf16[1024,640]{1,0:T(8,128)(2,1)S(1)}, u32[]{:S(2)}, u32[]{:S(2)}) %collective-permute-start.5) | collective-permute-done | bytes 1310752 | tf_op jit(solution)/shard_map/ppermute | solution.py:56
  274.7 26.7 %finish_middle.1 = (bf16[1024,2304]{1,0:T(8,128)(2,1)}, f32[256,2304]{1,0:T(8,128)}) custom-call(s32[2]{0:T(128)} %pad_add_fusion.where_ref.place_ref, bf16[1024,640]{1,0:T(8,128)(2,1)} %get-tuple-element.81.refs_4_.refs_0_.out_ref, bf16[1024,640]{1,0:T(8,128)(2,1)} %copy-done, bf16[1024,640]{1,0:T(8,128)(2,1)} %copy-done.8, bf16[1024,640]{1,0:T(8,128)(2,1)} %copy-done.9, ...), custom_call_target="tpu_custom_call" | custom-call | flops 65999998976 | tf_op jit(solution)/shard_map/finish_middle/pallas_call | solution.py:559
  301.4 21.4 %feed.1 = (bf16[1024,1536]{1,0:T(8,128)(2,1)}, bf16[1024,3072]{1,0:T(8,128)(2,1)}) custom-call(bf16[1024,2304]{1,0:T(8,128)(2,1)} %get-tuple-element.85.normed_ref.left_ref, bf16[2304,3072]{1,0:T(8,128)(2,1)} %all-gather.7.cloned.1.call-done.refs_2_.weight_ref), custom_call_target="tpu_custom_call" | custom-call | flops 62999998464 | tf_op jit(solution)/shard_map/feed/pallas_call | solution.py:601
  323.8 23.7 %feed_back.4 = (bf16[1024,3072]{1,0:T(8,128)(2,1)}, bf16[1024,2304]{1,0:T(8,128)(2,1)}, bf16[256,2304]{1,0:T(8,128)(2,1)}) custom-call(s32[2]{0:T(128)} %pad_add_fusion.3.where_ref, bf16[256,2304]{1,0:T(8,128)(2,1)} %copy-done.22, bf16[1024,3072]{1,0:T(8,128)(2,1)} %get-tuple-element.87.slope_ref, bf16[2304,1536]{1,0:T(8,128)(2,1)} %all-gather.11.cloned.1.call-done.down_ref, ...), custom_call_target="tpu_custom_call" | custom-call | flops 44999999488 | tf_op jit(solution)/shard_map/feed_back/pallas_call | solution.py:660
  347.5 26.6 %collective-permute-start.12 = (bf16[256,2304]{1,0:T(8,128)(2,1)}, bf16[256,2304]{1,0:T(8,128)(2,1)S(1)}, u32[]{:S(2)}, u32[]{:S(2)}) collective-permute-start(bf16[256,2304]{1,0:T(8,128)(2,1)} %get-tuple-element.97), channel_id=1, source_target_pairs={{0,1},{1,2},{2,3},{3,0},{4,5},{5,6},{6,7},{7,4},{8,9},{9,10},{10,1... | collective-permute-start | bytes 3538952 | tf_op jit(solution)/shard_map/ppermute | solution.py:56
  374.1 14.9 %feed_back.5 = (bf16[1024,3072]{1,0:T(8,128)(2,1)}, bf16[1024,2304]{1,0:T(8,128)(2,1)}, bf16[256,2304]{1,0:T(8,128)(2,1)}) custom-call(s32[2]{0:T(128)} %pad_add_fusion.2.where_ref, bf16[256,2304]{1,0:T(8,128)(2,1)} %collective-permute-done.10.grad_ref, ...), custom_call_target="tpu_custom_call", output_to_operand_aliasing={{0}: (5, {}), {1}: (6, {})} | custom-call | flops 44999999488 | tf_op jit(solution)/shard_map/feed_back/pallas_call | solution.py:660
  389.0 15.0 %feed_back.6 = (bf16[1024,3072]{1,0:T(8,128)(2,1)}, bf16[1024,2304]{1,0:T(8,128)(2,1)}, bf16[256,2304]{1,0:T(8,128)(2,1)}) custom-call(s32[2]{0:T(128)} %pad_add_fusion.1.where_ref, bf16[256,2304]{1,0:T(8,128)(2,1)} %collective-permute-done.9.grad_ref, bf16[1024,3072]{1,0:T(8,128)(2,1)} %get-tuple-element.87.slope_ref, ...), custom_call_target="tpu_custom_call", output_to_operand_aliasing={{0}: (5, {}), {1}: (6, {})} | custom-call | flops 44999999488 | tf_op jit(solution)/shard_map/feed_back/pallas_call | solution.py:660
  404.0 15.4 %feed_back.7 = (bf16[1024,3072]{1,0:T(8,128)(2,1)}, bf16[1024,2304]{1,0:T(8,128)(2,1)}, f32[256,2304]{1,0:T(8,128)}) custom-call(s32[2]{0:T(128)} %pad_add_fusion.where_ref.place_ref, bf16[256,2304]{1,0:T(8,128)(2,1)} %scaled.1.grad_ref, bf16[1024,3072]{1,0:T(8,128)(2,1)} %get-tuple-element.87.slope_ref, ...), custom_call_target="tpu_custom_call", output_to_operand_aliasing={{0}: (5, {}), {1}: (6, {})} | custom-call | flops 44999999488 | tf_op jit(solution)/shard_map/feed_back/pallas_call | solution.py:660
  423.3 11.5 %collective-permute-start.13 = (bf16[256,2304]{1,0:T(8,128)(2,1)}, bf16[256,2304]{1,0:T(8,128)(2,1)S(1)}, u32[]{:S(2)}, u32[]{:S(2)}) collective-permute-start(bf16[256,2304]{1,0:T(8,128)(2,1)} %get-tuple-element.98), channel_id=1, source_target_pairs={{0,1},{1,2},{2,3},{3,0},{4,5},{5,6},{6,7},{7,4},{8,9},{9,10},{10,1... | collective-permute-start | bytes 3538952 | tf_op jit(solution)/shard_map/ppermute | solution.py:56
  434.8 20.0 %weight_grad.6.refs_0_ = bf16[2304,3072]{1,0:T(8,128)(2,1)} custom-call(bf16[1024,2304]{1,0:T(8,128)(2,1)} %get-tuple-element.85.normed_ref.left_ref, bf16[1024,3072]{1,0:T(8,128)(2,1)} %get-tuple-element.99.right_ref), custom_call_target="tpu_custom_call" | custom-call | flops 62999998464 | tf_op jit(solution)/shard_map/weight_grad/pallas_call | solution.py:147
  466.6 12.3 %weight_grad.7.refs_0_ = bf16[2304,1536]{1,0:T(8,128)(2,1)} custom-call(bf16[1024,2304]{1,0:T(8,128)(2,1)} %get-tuple-element.101.left_ref, bf16[1024,1536]{1,0:T(8,128)(2,1)} %get-tuple-element.86.right_ref), custom_call_target="tpu_custom_call" | custom-call | flops 35999997952 | tf_op jit(solution)/shard_map/weight_grad/pallas_call | solution.py:147
  479.0 13.8 %collective-permute-done.14.arrived_ref = bf16[256,2304]{1,0:T(8,128)(2,1)S(1)} collective-permute-done((bf16[256,2304]{1,0:T(8,128)(2,1)}, bf16[256,2304]{1,0:T(8,128)(2,1)S(1)}, u32[]{:S(2)}, u32[]{:S(2)}) %collective-permute-start.14) | collective-permute-done | bytes 1179680 | tf_op jit(solution)/shard_map/ppermute | solution.py:56
  539.3 14.1 %collective-permute-done.16.refs_2_ = bf16[256,640]{1,0:T(8,128)(2,1)S(1)} collective-permute-done((bf16[256,640]{1,0:T(8,128)(2,1)S(1)}, bf16[256,640]{1,0:T(8,128)(2,1)S(1)}, u32[]{:S(2)}, u32[]{:S(2)}) %collective-permute-start.16) | collective-permute-done | bytes 327712 | tf_op jit(solution)/shard_map/ppermute | solution.py:80
  554.2 28.6 %attend_back.1.right_ref = bf16[1024,1920]{1,0:T(8,128)(2,1)} custom-call(s32[2]{0:T(128)} %pad_add_fusion.4.prefix_ref, bf16[1024,1920]{1,0:T(8,128)(2,1)} %get-tuple-element.80.qkv_ref, bf16[1024,640]{1,0:T(8,128)(2,1)} %get-tuple-element.81.refs_4_.refs_0_.out_ref, bf16[256,640]{1,0:T(8,128)(2,1)} %get-tuple-element.165.refs_0_, ...), custom_call_target="tpu_custom_call" | custom-call | flops 83999997952 | tf_op jit(solution)/shard_map/attend_back/pallas_call | solution.py:504
  582.8 8.0 fusion.4.refs_1_.refs_0_
  591.9 9.5 %weight_grad.10.refs_1_ = bf16[1152,1920]{1,0:T(8,128)(2,1)} custom-call(bf16[2,1024,1152]{2,1,0:T(8,128)(2,1)} %get-tuple-element.106.left_ref, bf16[1024,1920]{1,0:T(8,128)(2,1)} %attend_back.1.right_ref, bf16[256,2304]{1,0:T(8,128)(2,1)} %copy-done.23), custom_call_target="tpu_custom_call" | custom-call | flops 24000000000 | tf_op jit(solution)/shard_map/weight_grad/pallas_call | solution.py:147
  631.9 7.9 fusion.2.one_ref
  655.2 10.2 %weight_grad.11.refs_0_ = bf16[1152,1920]{1,0:T(8,128)(2,1)} custom-call(bf16[2,1024,1152]{2,1,0:T(8,128)(2,1)} %get-tuple-element.106.left_ref, bf16[1024,1920]{1,0:T(8,128)(2,1)} %attend_back.1.right_ref, bf16[1152,1920]{1,0:T(8,128)(2,1)} %collective-permute-done.21.refs_0_, bf16[256,2304]{1,0:T(8,128)(2,1)} %get-tuple-element.108.refs_1_.refs_0_), custom_call_target="tpu_custom_call" | custom-call | flops 24000000000 | tf_op jit(solution)/shard_map/weight_grad/pallas_call | solution.py:147
  676.1 7.9 fusion.term_ref
  684.1 12.0 %collective-permute-done.25.two_ref = bf16[2,144,2560]{2,1,0:T(8,128)(2,1)} collective-permute-done((bf16[2,144,2560]{2,1,0:T(8,128)(2,1)}, bf16[2,144,2560]{2,1,0:T(8,128)(2,1)}, u32[]{:S(2)}, u32[]{:S(2)}) %collective-permute-start.25) | collective-permute-done | bytes 1474592 | tf_op jit(solution)/shard_map/ppermute | solution.py:99
  769.5 11.0 %collective-permute-done.34.refs_1_ = bf16[288,640]{1,0:T(8,128)(2,1)S(1)} collective-permute-done((bf16[288,640]{1,0:T(8,128)(2,1)}, bf16[288,640]{1,0:T(8,128)(2,1)S(1)}, u32[]{:S(2)}, u32[]{:S(2)}) %collective-permute-start.34) | collective-permute-done | bytes 368672 | tf_op jit(solution)/shard_map/ppermute | solution.py:80
  780.5 22.2 %collective-permute-done.35.refs_2_ = bf16[288,640]{1,0:T(8,128)(2,1)S(1)} collective-permute-done((bf16[288,640]{1,0:T(8,128)(2,1)}, bf16[288,640]{1,0:T(8,128)(2,1)S(1)}, u32[]{:S(2)}, u32[]{:S(2)}) %collective-permute-start.35) | collective-permute-done | bytes 368672 | tf_op jit(solution)/shard_map/ppermute | solution.py:80
  (238 shorter events, 267.7 us)
Async XLA Ops:
  7.2 67.4 %all-gather.5.cloned.1.call-start = ((), (), s32[]{:S(2)}) async-start(), calls=%async_computation.2 | async-start | bytes 9953280 | tf_op jit(solution)/shard_map/all_gather | solution.py:103
  9.8 188.5 %all-gather.7.cloned.1.call-start = ((), (), s32[]{:S(2)}) async-start(), calls=%async_computation.3 | async-start | bytes 15925248 | tf_op jit(solution)/shard_map/all_gather | solution.py:103
  45.3 229.4 %all-gather.9.cloned.1.call-start = ((), (), s32[]{:S(2)}) async-start(), calls=%async_computation.4 | async-start | bytes 13271040 | tf_op jit(solution)/shard_map/all_gather | solution.py:103
  74.6 33.7 %collective-permute-start.2 = (bf16[256,2304]{1,0:T(8,128)(2,1)S(1)}, bf16[256,2304]{1,0:T(8,128)(2,1)S(1)}, u32[]{:S(2)}, u32[]{:S(2)}) collective-permute-start(bf16[256,2304]{1,0:T(8,128)(2,1)S(1)} %collective-permute-done.1.x_ref), channel_id=1, source_target_pairs={{0,1},{1,2},{2,3},{3,0},{4,5},{5,6},{6,7},{7,4},{8,9},{9,10},{10,1... | collective-permute-start | bytes 3538952 | tf_op jit(solution)/shard_map/ppermute | solution.py:56
  139.0 59.3 %collective-permute-start.3 = (bf16[1024,640]{1,0:T(8,128)(2,1)}, bf16[1024,640]{1,0:T(8,128)(2,1)S(1)}, u32[]{:S(2)}, u32[]{:S(2)}) collective-permute-start(bf16[1024,640]{1,0:T(8,128)(2,1)} %get-tuple-element.81.refs_4_.refs_0_.out_ref), channel_id=1, source_target_pairs={{0,1},{1,2},{2,3},{3,0},{4,5},{5,6},{6,7},{7,4},{8,9},{9,10},{10,1... | collective-permute-start | bytes 3932168 | tf_op jit(solution)/shard_map/ppermute | solution.py:56
  140.9 39.8 %collective-permute-start.6 = (bf16[288,640]{1,0:T(8,128)(2,1)}, bf16[288,640]{1,0:T(8,128)(2,1)S(1)}, u32[]{:S(2)}, u32[]{:S(2)}) collective-permute-start(bf16[288,640]{1,0:T(8,128)(2,1)} %pack.6.refs_0_), channel_id=1, source_target_pairs={{0,1},{1,2},{2,3},{3,0},{4,5},{5,6},{6,7},{7,4},{8,9},{9,10},{10,1... | collective-permute-start | bytes 1105928 | tf_op jit(solution)/shard_map/ppermute | solution.py:80
  141.7 52.6 %collective-permute-start.7 = (bf16[288,640]{1,0:T(8,128)(2,1)}, bf16[288,640]{1,0:T(8,128)(2,1)S(1)}, u32[]{:S(2)}, u32[]{:S(2)}) collective-permute-start(bf16[288,640]{1,0:T(8,128)(2,1)} %pack.6.refs_0_), channel_id=1, source_target_pairs={{0,2},{1,3},{2,0},{3,1},{4,6},{5,7},{6,4},{7,5},{8,10},{9,11},{10,... | collective-permute-start | bytes 1105928 | tf_op jit(solution)/shard_map/ppermute | solution.py:80
  145.3 49.0 %collective-permute-start.8 = (bf16[288,640]{1,0:T(8,128)(2,1)}, bf16[288,640]{1,0:T(8,128)(2,1)S(1)}, u32[]{:S(2)}, u32[]{:S(2)}) collective-permute-start(bf16[288,640]{1,0:T(8,128)(2,1)} %pack.6.refs_0_), channel_id=1, source_target_pairs={{0,3},{1,0},{2,1},{3,2},{4,7},{5,4},{6,5},{7,6},{8,11},{9,8},{10,9... | collective-permute-start | bytes 1105928 | tf_op jit(solution)/shard_map/ppermute | solution.py:80
  199.4 123.4 %all-gather.11.cloned.1.call-start = ((), (), s32[]{:S(2)}) async-start(), calls=%async_computation.5 | async-start | bytes 7962624 | tf_op jit(solution)/shard_map/all_gather | solution.py:103
  199.5 36.2 %collective-permute-start.4 = (bf16[1024,640]{1,0:T(8,128)(2,1)}, bf16[1024,640]{1,0:T(8,128)(2,1)S(1)}, u32[]{:S(2)}, u32[]{:S(2)}) collective-permute-start(bf16[1024,640]{1,0:T(8,128)(2,1)} %copy-done), channel_id=1, source_target_pairs={{0,1},{1,2},{2,3},{3,0},{4,5},{5,6},{6,7},{7,4},{8,9},{9,10},{10,1... | collective-permute-start | bytes 3932168 | tf_op jit(solution)/shard_map/ppermute | solution.py:56
  235.7 31.7 %collective-permute-start.5 = (bf16[1024,640]{1,0:T(8,128)(2,1)S(1)}, bf16[1024,640]{1,0:T(8,128)(2,1)S(1)}, u32[]{:S(2)}, u32[]{:S(2)}) collective-permute-start(bf16[1024,640]{1,0:T(8,128)(2,1)S(1)} %collective-permute-done.4.refs_2_), channel_id=1, source_target_pairs={{0,1},{1,2},{2,3},{3,0},{4,5},{5,6},{6,7},{7,4},{8,9},{9,10},{10,1... | collective-permute-start | bytes 3932168 | tf_op jit(solution)/shard_map/ppermute | solution.py:56
  242.6 566.0 %reduce-scatter.5.cloned.1.call-start = ((), (), s32[]{:S(2)}) async-start(), calls=%async_computation.7 | async-start | bytes 7962624 | tf_op jit(solution)/shard_map/reduce_scatter | solution.py:247
  270.9 51.9 %collective-permute-start.11 = (bf16[256,2304]{1,0:T(8,128)(2,1)}, bf16[256,2304]{1,0:T(8,128)(2,1)S(1)}, u32[]{:S(2)}, u32[]{:S(2)}) collective-permute-start(bf16[256,2304]{1,0:T(8,128)(2,1)} %scaled.1.grad_ref), channel_id=1, source_target_pairs={{0,1},{1,2},{2,3},{3,0},{4,5},{5,6},{6,7},{7,4},{8,9},{9,10},{10,1... | collective-permute-start | bytes 3538952 | tf_op jit(solution)/shard_map/ppermute | solution.py:80
  271.5 102.6 %collective-permute-start.10 = (bf16[256,2304]{1,0:T(8,128)(2,1)}, bf16[256,2304]{1,0:T(8,128)(2,1)}, u32[]{:S(2)}, u32[]{:S(2)}) collective-permute-start(bf16[256,2304]{1,0:T(8,128)(2,1)} %scaled.1.grad_ref), channel_id=1, source_target_pairs={{0,2},{1,3},{2,0},{3,1},{4,6},{5,7},{6,4},{7,5},{8,10},{9,11},{10,... | collective-permute-start | bytes 3538952 | tf_op jit(solution)/shard_map/ppermute | solution.py:80
  271.8 117.2 %collective-permute-start.9 = (bf16[256,2304]{1,0:T(8,128)(2,1)}, bf16[256,2304]{1,0:T(8,128)(2,1)}, u32[]{:S(2)}, u32[]{:S(2)}) collective-permute-start(bf16[256,2304]{1,0:T(8,128)(2,1)} %scaled.1.grad_ref), channel_id=1, source_target_pairs={{0,3},{1,0},{2,1},{3,2},{4,7},{5,4},{6,5},{7,6},{8,11},{9,8},{10,9... | collective-permute-start | bytes 3538952 | tf_op jit(solution)/shard_map/ppermute | solution.py:80
  347.5 71.9 %collective-permute-start.12 = (bf16[256,2304]{1,0:T(8,128)(2,1)}, bf16[256,2304]{1,0:T(8,128)(2,1)S(1)}, u32[]{:S(2)}, u32[]{:S(2)}) collective-permute-start(bf16[256,2304]{1,0:T(8,128)(2,1)} %get-tuple-element.97), channel_id=1, source_target_pairs={{0,1},{1,2},{2,3},{3,0},{4,5},{5,6},{6,7},{7,4},{8,9},{9,10},{10,1... | collective-permute-start | bytes 3538952 | tf_op jit(solution)/shard_map/ppermute | solution.py:56
  423.3 36.7 %collective-permute-start.13 = (bf16[256,2304]{1,0:T(8,128)(2,1)}, bf16[256,2304]{1,0:T(8,128)(2,1)S(1)}, u32[]{:S(2)}, u32[]{:S(2)}) collective-permute-start(bf16[256,2304]{1,0:T(8,128)(2,1)} %get-tuple-element.98), channel_id=1, source_target_pairs={{0,1},{1,2},{2,3},{3,0},{4,5},{5,6},{6,7},{7,4},{8,9},{9,10},{10,1... | collective-permute-start | bytes 3538952 | tf_op jit(solution)/shard_map/ppermute | solution.py:56
  500.8 315.6 %reduce-scatter.3.cloned.1.call-start = ((), (), s32[]{:S(2)}) async-start(), calls=%async_computation.6 | async-start | bytes 15925248 | tf_op jit(solution)/shard_map/reduce_scatter | solution.py:247
  532.8 78.3 %collective-permute-start.19 = (bf16[1152,2560]{1,0:T(8,128)(2,1)}, bf16[1152,2560]{1,0:T(8,128)(2,1)}, u32[]{:S(2)}, u32[]{:S(2)}) collective-permute-start(bf16[1152,2560]{1,0:T(8,128)(2,1)} %weight_grad.8.refs_8_), channel_id=1, source_target_pairs={{0,4},{4,0},{8,12},{12,8},{16,20},{20,16},{24,28},{28,24},{1,5},{5... | collective-permute-start | bytes 17694728 | tf_op jit(solution)/shard_map/ppermute | solution.py:99
  601.3 53.8 %collective-permute-start.21 = (bf16[1152,1920]{1,0:T(8,128)(2,1)}, bf16[1152,1920]{1,0:T(8,128)(2,1)}, u32[]{:S(2)}, u32[]{:S(2)}) collective-permute-start(bf16[1152,1920]{1,0:T(8,128)(2,1)} %weight_grad.10.refs_1_), channel_id=1, source_target_pairs={{0,4},{4,0},{8,12},{12,8},{16,20},{20,16},{24,28},{28,24},{1,5},{5... | collective-permute-start | bytes 13271048 | tf_op jit(solution)/shard_map/ppermute | solution.py:99
  609.3 37.7 %collective-permute-start.23 = (bf16[256,2304]{1,0:T(8,128)(2,1)}, bf16[256,2304]{1,0:T(8,128)(2,1)}, u32[]{:S(2)}, u32[]{:S(2)}) collective-permute-start(bf16[256,2304]{1,0:T(8,128)(2,1)} %gate.5), channel_id=1, source_target_pairs={{0,1},{1,2},{2,3},{3,0},{4,5},{5,6},{6,7},{7,4},{8,9},{9,10},{10,1... | collective-permute-start | bytes 3538952 | tf_op jit(solution)/shard_map/ppermute | solution.py:56
  631.8 70.7 %collective-permute-start.26 = (bf16[2,144,2560]{2,1,0:T(8,128)(2,1)}, bf16[2,144,2560]{2,1,0:T(8,128)(2,1)}, u32[]{:S(2)}, u32[]{:S(2)}) collective-permute-start(bf16[2,144,2560]{2,1,0:T(8,128)(2,1)} %get-tuple-element.148), channel_id=1, source_target_pairs={{0,8},{4,12},{8,0},{12,4},{16,24},{20,28},{24,16},{28,20},{1,9},{5... | collective-permute-start | bytes 4423688 | tf_op jit(solution)/shard_map/ppermute | solution.py:99
  639.8 32.5 %collective-permute-start.20 = (bf16[256,2304]{1,0:T(8,128)(2,1)}, bf16[256,2304]{1,0:T(8,128)(2,1)}, u32[]{:S(2)}, u32[]{:S(2)}) collective-permute-start(bf16[256,2304]{1,0:T(8,128)(2,1)} %get-tuple-element.108.refs_1_.refs_0_), channel_id=1, source_target_pairs={{0,1},{1,2},{2,3},{3,0},{4,5},{5,6},{6,7},{7,4},{8,9},{9,10},{10,1... | collective-permute-start | bytes 3538952 | tf_op jit(solution)/shard_map/ppermute | solution.py:56
  641.6 54.5 %collective-permute-start.25 = (bf16[2,144,2560]{2,1,0:T(8,128)(2,1)}, bf16[2,144,2560]{2,1,0:T(8,128)(2,1)}, u32[]{:S(2)}, u32[]{:S(2)}) collective-permute-start(bf16[2,144,2560]{2,1,0:T(8,128)(2,1)} %get-tuple-element.150), channel_id=1, source_target_pairs={{0,16},{4,20},{8,24},{12,28},{16,0},{20,4},{24,8},{28,12},{1,17},{... | collective-permute-start | bytes 4423688 | tf_op jit(solution)/shard_map/ppermute | solution.py:99
  650.2 69.6 %collective-permute-start.24 = (bf16[256,2304]{1,0:T(8,128)(2,1)}, bf16[256,2304]{1,0:T(8,128)(2,1)S(1)}, u32[]{:S(2)}, u32[]{:S(2)}) collective-permute-start(bf16[256,2304]{1,0:T(8,128)(2,1)} %get-tuple-element.112), channel_id=1, source_target_pairs={{0,1},{1,2},{2,3},{3,0},{4,5},{5,6},{6,7},{7,4},{8,9},{9,10},{10,1... | collective-permute-start | bytes 3538952 | tf_op jit(solution)/shard_map/ppermute | solution.py:56
  669.3 44.0 %collective-permute-start.30 = (bf16[2,144,1920]{2,1,0:T(8,128)(2,1)S(1)}, bf16[2,144,1920]{2,1,0:T(8,128)(2,1)}, u32[]{:S(2)}, u32[]{:S(2)}) collective-permute-start(bf16[2,144,1920]{2,1,0:T(8,128)(2,1)S(1)} %get-tuple-element.152), channel_id=1, source_target_pairs={{0,8},{4,12},{8,0},{12,4},{16,24},{20,28},{24,16},{28,20},{1,9},{5... | collective-permute-start | bytes 3317768 | tf_op jit(solution)/shard_map/ppermute | solution.py:99
  672.3 58.3 %collective-permute-start.28 = (bf16[2,144,1920]{2,1,0:T(8,128)(2,1)S(1)}, bf16[2,144,1920]{2,1,0:T(8,128)(2,1)}, u32[]{:S(2)}, u32[]{:S(2)}) collective-permute-start(bf16[2,144,1920]{2,1,0:T(8,128)(2,1)S(1)} %get-tuple-element.154), channel_id=1, source_target_pairs={{0,16},{4,20},{8,24},{12,28},{16,0},{20,4},{24,8},{28,12},{1,17},{... | collective-permute-start | bytes 3317768 | tf_op jit(solution)/shard_map/ppermute | solution.py:99
  702.5 52.4 %collective-permute-start.32 = (bf16[144,2560]{1,0:T(8,128)(2,1)S(1)}, bf16[144,2560]{1,0:T(8,128)(2,1)}, u32[]{:S(2)}, u32[]{:S(2)}) collective-permute-start(bf16[144,2560]{1,0:T(8,128)(2,1)S(1)} %get-tuple-element.160), channel_id=1, source_target_pairs={{0,8},{4,12},{8,0},{12,4},{16,24},{20,28},{24,16},{28,20},{1,9},{5... | collective-permute-start | bytes 2211848 | tf_op jit(solution)/shard_map/ppermute | solution.py:99
  713.4 41.6 %collective-permute-start.33 = (bf16[144,2560]{1,0:T(8,128)(2,1)S(1)}, bf16[144,2560]{1,0:T(8,128)(2,1)}, u32[]{:S(2)}, u32[]{:S(2)}) collective-permute-start(bf16[144,2560]{1,0:T(8,128)(2,1)S(1)} %get-tuple-element.158), channel_id=1, source_target_pairs={{0,16},{4,20},{8,24},{12,28},{16,0},{20,4},{24,8},{28,12},{1,17},{... | collective-permute-start | bytes 2211848 | tf_op jit(solution)/shard_map/ppermute | solution.py:99
  743.2 79.5 %collective-permute-start.27 = (bf16[256,2304]{1,0:T(8,128)(2,1)S(1)}, bf16[256,2304]{1,0:T(8,128)(2,1)S(1)}, u32[]{:S(2)}, u32[]{:S(2)}) collective-permute-start(bf16[256,2304]{1,0:T(8,128)(2,1)S(1)} %copy-done.13), channel_id=1, source_target_pairs={{0,1},{1,2},{2,3},{3,0},{4,5},{5,6},{6,7},{7,4},{8,9},{9,10},{10,1... | collective-permute-start | bytes 3538952 | tf_op jit(solution)/shard_map/ppermute | solution.py:56
  758.1 44.5 %collective-permute-start.35 = (bf16[288,640]{1,0:T(8,128)(2,1)}, bf16[288,640]{1,0:T(8,128)(2,1)S(1)}, u32[]{:S(2)}, u32[]{:S(2)}) collective-permute-start(bf16[288,640]{1,0:T(8,128)(2,1)} %get-tuple-element.123), channel_id=1, source_target_pairs={{0,2},{1,3},{2,0},{3,1},{4,6},{5,7},{6,4},{7,5},{8,10},{9,11},{10,... | collective-permute-start | bytes 1105928 | tf_op jit(solution)/shard_map/ppermute | solution.py:80
  759.9 42.8 %collective-permute-start.36 = (bf16[288,640]{1,0:T(8,128)(2,1)}, bf16[288,640]{1,0:T(8,128)(2,1)S(1)}, u32[]{:S(2)}, u32[]{:S(2)}) collective-permute-start(bf16[288,640]{1,0:T(8,128)(2,1)} %get-tuple-element.124), channel_id=1, source_target_pairs={{0,1},{1,2},{2,3},{3,0},{4,5},{5,6},{6,7},{7,4},{8,9},{9,10},{10,1... | collective-permute-start | bytes 1105928 | tf_op jit(solution)/shard_map/ppermute | solution.py:80
  (54 other events, 633.8 us)
Sparse Core Ops, SparseCore 0:
  10.5 59.0 all-gather.4
  72.0 78.7 all-gather.6
  199.5 72.1 all-gather.8
  273.5 48.8 all-gather.10
  500.9 61.8 reduce-scatter.4
  566.7 128.2 reduce-scatter.2

commit v3 on v2

--- a/solution.py
+++ b/solution.py
@@ -81,7 +81,7 @@
 
 
 def sum_all(value):
-    for axis in ("mp", "dp"):
+    for axis in ("dp", "mp"):
         n = lax.axis_size(axis)
         bit = 1
         while bit < n:
@@ -162,10 +162,93 @@
     return weight_grad(left, right, 1, left.shape[2], width, micros, waits=waits)
 
 
-def scatter_mine(left, right, width, micros, arrived, waits=()):
-    if not paired():
-        return inner_rows(left[0], right).astype(BF16)
-    return weight_grad(left, right, 0, left.shape[2], width, micros, arrived, waits)
+def chip_kernel(where_ref, left_ref, right_ref, arrived_ref, *refs):
+    one_kept, one_sent, two_kept, two_sent, zero_ref, total = refs[-6:]
+    zero_ref[0] = 0
+    value = inner_rows(left_ref[...], right_ref[...]) + arrived_ref[...].astype(F32)
+    total[...] = value.astype(BF16)
+    x, y = where_ref[0], where_ref[1]
+    rows = total.shape[0] // 4
+    half = rows // 2
+    for k in (0, 1):
+        for one_ref, two_ref, near_x, near_y in (
+            (one_kept, two_kept, x, y),
+            (one_sent, two_sent, 1 - x, 1 - y),
+        ):
+            start = pl.multiple_of((2 * near_y + k) * rows, 16)
+            one_ref[k] = total[pl.ds(start, half), :]
+            start = pl.multiple_of((2 * k + near_x) * rows + half, 16)
+            two_ref[k] = total[pl.ds(start, half), :]
+
+
+def scatter_chip(where, left, right, width, micros, arrived, waits=()):
+    depth, columns = left.shape[1:]
+    others = right.shape[1]
+    half = columns // 8
+    out = jax.ShapeDtypeStruct((2, half, others), BF16)
+    block = pl.BlockSpec((2, half, width), lambda j, w: (0, 0, j))
+    *parts, zero = pl.pallas_call(
+        chip_kernel,
+        out_shape=(out, out, out, out, jax.ShapeDtypeStruct((1,), jnp.int32)),
+        grid_spec=pltpu.PrefetchScalarGridSpec(
+            num_scalar_prefetch=1,
+            grid=(others // width,),
+            in_specs=[
+                pl.BlockSpec((None, depth, columns), lambda j, w: (0, 0, 0)),
+                pl.BlockSpec((depth, width), lambda j, w: (0, j)),
+                pl.BlockSpec((columns, width), lambda j, w: (0, j)),
+            ]
+            + after_all(waits),
+            out_specs=(block, block, block, block, pl.BlockSpec(memory_space=pltpu.SMEM)),
+            scratch_shapes=[pltpu.VMEM((columns, width), BF16)],
+        ),
+        compiler_params=params(),
+        cost_estimate=cost(micros),
+        name="scatter_chip",
+    )(where, left, right, arrived, *waits)
+    return parts, zero
+
+
+def scatter_first(parts):
+    return swap(parts[1], 4), swap(parts[3], 2)
+
+
+def halves_kernel(where_ref, kept_ref, moved_ref, *refs):
+    keep_ref, send_ref, total = refs[-3:]
+    total[...] = (kept_ref[...].astype(F32) + moved_ref[...].astype(F32)).astype(BF16)
+    keep_ref[...] = total[where_ref[0]]
+    send_ref[...] = total[1 - where_ref[0]]
+
+
+def halves(where, kept, moved, waits):
+    whole = pl.BlockSpec(memory_space=pltpu.VMEM)
+    out = jax.ShapeDtypeStruct(kept.shape[1:], BF16)
+    return pl.pallas_call(
+        halves_kernel,
+        out_shape=(out, out),
+        in_specs=[pl.BlockSpec(memory_space=pltpu.SMEM), whole, whole] + after_all(waits),
+        out_specs=(whole, whole),
+        scratch_shapes=[pltpu.VMEM(kept.shape, BF16)],
+        compiler_params=params(),
+        cost_estimate=cost(3),
+        name="halves",
+    )(where, kept, moved, *waits)
+
+
+def scatter_halves(where, parts, moved, waits=()):
+    return (
+        halves(where[0:1], parts[0], moved[0], waits),
+        halves(where[1:2], parts[2], moved[1], waits),
+    )
+
+
+def scatter_second(both):
+    (one, one_sent), (two, two_sent) = both
+    return [(one, swap(one_sent, 2)), (two, swap(two_sent, 4))]
+
+
+def scatter_plain(left, right):
+    return scatter_whole(inner_rows(left[0], right).astype(BF16))
 
 
 def pass_kernel(*refs):
@@ -210,43 +293,24 @@
     return join_marked(one, two, waits)[0]
 
 
-def scatter_first(chip):
-    index = lax.axis_index("dp")
-    x, y = index // 2 % 2, index // 4
-    rows = chip.shape[0] // 4
-    half = rows // 2
-    chip = chip.reshape(2, 2, rows, -1)
-
-    def pick(array, axis, which):
-        return lax.dynamic_index_in_dim(array, which, axis, False)
-
-    one, two = chip[:, :, :half], chip[:, :, half:]
-    kept = pick(one, 0, y), pick(two, 1, x)
-    return kept, (swap(pick(one, 0, 1 - y), 4), swap(pick(two, 1, 1 - x), 2))
-
-
-def scatter_join(kept, moved, waits):
-    return join(kept[0], moved[0], waits), join(kept[1], moved[1], waits)
-
-
-def scatter_second(parts):
-    index = lax.axis_index("dp")
-    x, y = index // 2 % 2, index // 4
-    one, two = parts
-
-    def pick(array, which):
-        return lax.dynamic_index_in_dim(array, which, 0, False)
-
-    return [
-        (pick(one, x), swap(pick(one, 1 - x), 2)),
-        (pick(two, y), swap(pick(two, 1 - y), 4)),
-    ]
+def scatter_mine(left, right, width, micros, arrived, waits=()):
+    return weight_grad(left, right, 0, left.shape[2], width, micros, arrived, waits)
+
+
+def scatter_around(chip):
+    share = lax.psum_scatter(
+        chip,
+        "dp",
+        scatter_dimension=0,
+        tiled=True,
+        axis_index_groups=[[2 * k + core for k in AROUND] for core in (0, 1)],
+    )
+    return [(share, None)]
 
 
 def scatter_whole(partial):
     share = lax.psum_scatter(partial, "dp", scatter_dimension=0, tiled=True)
-    half = share.shape[0] // 2
-    return [(share[:half], None), (share[half:], None)]
+    return [(share, None)]
 
 
 def angle_tables():
@@ -268,7 +332,10 @@
     )
 
 
-def put_split(ref, value, core):
+AROUND = (0, 1, 3, 2)
+
+
+def put_split(ref, value, core, chips=(0, 1, 2, 3)):
     if ref.shape[0] == 1:
         ref[0] = value
         return
@@ -278,9 +345,9 @@
         @pl.when(core == which)
         def _():
             for side in (0, 1):
-                for chip in range(4):
+                for spot, chip in enumerate(chips):
                     start = (2 * chip + (which ^ side)) * block
-                    ref[side, :, chip * block : (chip + 1) * block] = value[
+                    ref[side, :, spot * block : (spot + 1) * block] = value[
                         :, start : start + block
                     ]
 
@@ -377,7 +444,7 @@
     return jnp.where((lane >= HD) == (head == 1), value, jnp.zeros_like(value))
 
 
-def attend_kernel(heads, prefix_ref, qkv_ref, out_ref, log_ref, turned):
+def attend_kernel(heads, prefix_ref, qkv_ref, out_ref, send_ref, log_ref, turned):
     limit = prefix_ref[0]
     pair = pl.program_id(0)
     values_across = qkv_ref[:, 2 * LANES :].T
@@ -414,7 +481,9 @@
             turned[head * HD : (head + 1) * HD, :] = jnp.zeros((HD, LEN), F32)
             log_ref[0, head : head + 1, :] = jnp.zeros((1, LEN), F32)
 
-    out_ref[...] = turned[...].T.astype(BF16)
+    value = turned[...].T.astype(BF16)
+    out_ref[...] = value
+    send_ref[...] = value
 
 
 def attend(qkv, prefix, heads):
@@ -422,6 +491,7 @@
     return pl.pallas_call(
         functools.partial(attend_kernel, heads),
         out_shape=(
+            jax.ShapeDtypeStruct((LEN, pairs * LANES), BF16),
             jax.ShapeDtypeStruct((LEN, pairs * LANES), BF16),
             jax.ShapeDtypeStruct((pairs, 2, LEN), F32),
         ),
@@ -430,6 +500,7 @@
             grid=(pairs,),
             in_specs=[pl.BlockSpec((LEN, 3 * LANES), lambda i, s: (0, i))],
             out_specs=(
+                pl.BlockSpec((LEN, LANES), lambda i, s: (0, i)),
                 pl.BlockSpec((LEN, LANES), lambda i, s: (0, i)),
                 pl.BlockSpec((1, 2, LEN), lambda i, s: (i, 0, 0)),
             ),
@@ -534,7 +605,7 @@
 
 def middle_kernel(count, place_ref, *refs):
     pieces = refs[:count]
-    w_ref, x_ref, gain_ref, normed_ref, own_ref = refs[count:]
+    w_ref, x_ref, gain_ref, normed_ref, split_ref, own_ref = refs[count:]
     depth = pieces[0].shape[1]
     total = None
     for k in range(count):
@@ -542,7 +613,9 @@
         total = term if total is None else total + term
     middle = x_ref[...].astype(F32) + BRANCH * total
     factor = lax.rsqrt(jnp.mean(middle * middle, axis=-1, keepdims=True) + EPSILON)
-    normed_ref[...] = (middle * factor * gain_ref[...]).astype(BF16)
+    normed = (middle * factor * gain_ref[...]).astype(BF16)
+    normed_ref[...] = normed
+    put_split(split_ref, normed, place_ref[1], AROUND)
     rows, own = x_ref.shape[0], own_ref.shape[0]
     for part in range(rows // own):
 
@@ -560,6 +633,7 @@
         functools.partial(middle_kernel, count),
         out_shape=(
             jax.ShapeDtypeStruct((LEN, width), BF16),
+            jax.ShapeDtypeStruct(split_shape(LEN, width), BF16),
             jax.ShapeDtypeStruct((own, width), F32),
         ),
         grid_spec=pltpu.PrefetchScalarGridSpec(
@@ -573,6 +647,7 @@
             ],
             out_specs=(
                 pl.BlockSpec((rows, width), lambda i, s: (i, 0)),
+                pl.BlockSpec(split_shape(rows, width), lambda i, s: (0, i, 0)),
                 pl.BlockSpec((own, width), lambda i, s: (0, 0)),
             ),
         ),
@@ -625,7 +700,7 @@
 
     @pl.when(step == 0)
     def _():
-        copy_ref[...] = grad_ref[...]
+        put_split(copy_ref, grad_ref[...], where_ref[1], AROUND)
         total[...] = jnp.zeros_like(total)
 
     grad = matmul(grad_ref[...], down_ref[...])
@@ -661,7 +736,7 @@
         feed_back_kernel,
         out_shape=(
             jax.ShapeDtypeStruct((LEN, 2 * hidden), BF16),
-            jax.ShapeDtypeStruct((LEN, width), BF16),
+            jax.ShapeDtypeStruct(split_shape(LEN, width), BF16),
             jax.ShapeDtypeStruct((rows, width), kind),
         ),
         grid_spec=pltpu.PrefetchScalarGridSpec(
@@ -670,7 +745,7 @@
             in_specs=specs,
             out_specs=(
                 pl.BlockSpec((rows, 2 * FF_BLOCK), lambda i, w: (w[0], i)),
-                pl.BlockSpec((rows, width), lambda i, w: (w[0], 0)),
+                pl.BlockSpec(split_shape(rows, width), lambda i, w: (0, w[0], 0)),
                 pl.BlockSpec((rows, width), lambda i, w: (0, 0)),
             ),
             scratch_shapes=[pltpu.VMEM((rows, width), F32)],
@@ -684,7 +759,8 @@
 
 def out_sum_kernel(parts, count, width, *refs):
     terms, outs = grouped(parts, refs)
-    half = outs[0].shape[0] // 2
+    outs = outs[-count:]
+    half = outs[0].shape[0] // len(parts)
     for index, pair in enumerate(terms):
         value = added(pair)
         here = slice(index * half, (index + 1) * half)
@@ -692,35 +768,70 @@
             outs[k][here, :] = value[:, k * width : (k + 1) * width].astype(outs[k].dtype)
 
 
-def out_sum(parts, count, width):
-    rows = 2 * parts[0][0].shape[0]
+def out_sum(parts, count, width, waits=()):
+    rows = len(parts) * parts[0][0].shape[0]
     arrays = [a for pair in parts for a in pair if a is not None]
     return pl.pallas_call(
         functools.partial(out_sum_kernel, parts_mask(parts), count, width),
         out_shape=tuple(
             jax.ShapeDtypeStruct((rows, width), BF16 if k else F32) for k in range(count)
         ),
+        in_specs=[pl.BlockSpec(memory_space=pltpu.VMEM)] * len(arrays) + after_all(waits),
         compiler_params=params(),
         cost_estimate=cost(3),
         name="out_sum",
-    )(*arrays)
-
-
-def out_final_kernel(*refs):
+    )(*arrays, *waits)
+
+
+def out_final_kernel(count, *refs):
     total = refs[0][...]
-    for ref in refs[1:-1]:
+    for ref in refs[1:count]:
         total = total + ref[...].astype(F32)
-    refs[-1][...] = total.T[: refs[-1].shape[0]]
-
-
-def out_final(own, moved, width):
-    return pl.pallas_call(
-        out_final_kernel,
-        out_shape=jax.ShapeDtypeStruct((width, own.shape[0]), F32),
+    refs[-1][...] = total[:, : refs[-1].shape[1]]
+
+
+def out_final(own, moved, width, waits):
+    whole = pl.BlockSpec(memory_space=pltpu.VMEM)
+    count = 1 + len(moved)
+    return pl.pallas_call(
+        functools.partial(out_final_kernel, count),
+        out_shape=jax.ShapeDtypeStruct((own.shape[0], width), F32),
+        in_specs=[whole] * count + after_all(waits),
+        out_specs=whole,
         compiler_params=params(),
         cost_estimate=cost(3),
         name="out_final",
-    )(own, *moved)
+    )(own, *moved, *waits)
+
+
+def spread_kernel(count, value_ref, weight_ref, *refs):
+    product = matmul(value_ref[...], weight_ref[...]).astype(BF16)
+    refs[-1][0] = 0
+    for k in range(count):
+
+        @pl.when(pl.program_id(0) == k)
+        def _():
+            refs[k][...] = product
+
+
+def spread(value, weights, count):
+    rows, depth = value.shape
+    width = weights.shape[1] // count
+    return pl.pallas_call(
+        functools.partial(spread_kernel, count),
+        out_shape=tuple(jax.ShapeDtypeStruct((rows, width), BF16) for _ in range(count))
+        + (jax.ShapeDtypeStruct((1,), jnp.int32),),
+        grid=(count,),
+        in_specs=[
+            pl.BlockSpec((rows, depth), lambda i: (0, 0)),
+            pl.BlockSpec((depth, width), lambda i: (0, i)),
+        ],
+        out_specs=tuple(pl.BlockSpec((rows, width), lambda i: (0, 0)) for _ in range(count))
+        + (pl.BlockSpec(memory_space=pltpu.SMEM),),
+        compiler_params=params(),
+        cost_estimate=cost(8),
+        name="spread",
+    )(value, weights)
 
 
 def norm_back(value, gain, incoming):
@@ -855,28 +966,18 @@
                 )
 
 
-def put_across(out_ref, value):
-    rows = value.shape[0]
-    out_ref[:, :rows] = value.T
-    if rows < out_ref.shape[1]:
-        out_ref[:, rows:] = jnp.zeros((out_ref.shape[0], out_ref.shape[1] - rows), BF16)
-
-
 def pack_kernel(count, block, *refs):
-    if count == 1:
-        put_across(refs[-1], refs[0][...])
-    else:
-        mix(refs[-1], refs[:count], block)
+    mix(refs[-1], refs[:count], block)
 
 
 def pack(values, block, width, *waits):
     count = len(values)
-    rows = values[0].shape[0] if count > 1 else values[0].shape[1]
+    rows = values[0].shape[0]
     whole = pl.BlockSpec(memory_space=pltpu.VMEM)
     return pl.pallas_call(
         functools.partial(pack_kernel, count, block),
         out_shape=jax.ShapeDtypeStruct((rows, count * width), BF16),
-        in_specs=[whole] * count + [pl.BlockSpec(memory_space=pl.ANY)] * len(waits),
+        in_specs=[whole] * count + after_all(waits),
         out_specs=whole,
         compiler_params=params(),
         cost_estimate=cost(3),
@@ -905,6 +1006,30 @@
     )(*values, *waits)
 
 
+def own_rows_kernel(count, place_ref, *refs):
+    width = refs[0].shape[1]
+    for k in range(count):
+        refs[-1][:, k * width : (k + 1) * width] = refs[k][...]
+
+
+def own_rows(place, pieces, rows):
+    width = pieces[0].shape[1]
+    count = len(pieces)
+    return pl.pallas_call(
+        functools.partial(own_rows_kernel, count),
+        out_shape=jax.ShapeDtypeStruct((rows, count * width), pieces[0].dtype),
+        grid_spec=pltpu.PrefetchScalarGridSpec(
+            num_scalar_prefetch=1,
+            grid=(1,),
+            in_specs=[pl.BlockSpec((rows, width), lambda i, s: (s[0], 0))] * count,
+            out_specs=pl.BlockSpec((rows, count * width), lambda i, s: (0, 0)),
+        ),
+        compiler_params=params(),
+        cost_estimate=cost(2),
+        name="own_rows",
+    )(place, *pieces)
+
+
 def scale_kernel(value_ref, *refs):
     refs[-1][...] = (BRANCH * value_ref[...].astype(F32)).astype(BF16)
 
@@ -934,10 +1059,11 @@
     return out, refs
 
 
-def unmix_kernel(parts, block, *refs):
+def unmix_kernel(parts, block, count, *refs):
     terms, outs = grouped(parts, refs)
+    outs = outs[-count:]
     width = outs[0].shape[1]
-    half = outs[0].shape[0] // 2
+    half = outs[0].shape[0] // len(parts)
     for index, pair in enumerate(terms):
         value = added(pair)
         for first in range(0, width, block):
@@ -949,36 +1075,21 @@
                 ]
 
 
-def unmix(parts, count, block, width):
-    rows = 2 * parts[0][0].shape[0]
+def unmix(parts, count, block, width, waits=()):
+    rows = len(parts) * parts[0][0].shape[0]
     arrays = [a for pair in parts for a in pair if a is not None]
     return pl.pallas_call(
-        functools.partial(unmix_kernel, parts_mask(parts), block),
+        functools.partial(unmix_kernel, parts_mask(parts), block, count),
         out_shape=tuple(jax.ShapeDtypeStruct((rows, width), F32) for _ in range(count)),
-        compiler_params=params(),
+        in_specs=[pl.BlockSpec(memory_space=pltpu.VMEM)] * len(arrays) + after_all(waits),
+        compiler_params=params(),
+        cost_estimate=cost(3),
         name="unmix",
-    )(*arrays)
+    )(*arrays, *waits)
 
 
 def parts_mask(parts):
     return [tuple(None if a is None else True for a in pair) for pair in parts]
-
-
-def turn_kernel(parts, *refs):
-    terms, (out_ref,) = grouped(parts, refs)
-    value = jnp.concatenate([added(pair) for pair in terms], axis=0)
-    out_ref[...] = value.T[: out_ref.shape[0]]
-
-
-def turn(parts, width):
-    rows = 2 * parts[0][0].shape[0]
-    arrays = [a for pair in parts for a in pair if a is not None]
-    return pl.pallas_call(
-        functools.partial(turn_kernel, parts_mask(parts)),
-        out_shape=jax.ShapeDtypeStruct((width, rows), F32),
-        compiler_params=params(),
-        name="turn",
-    )(*arrays)
 
 
 def body(
@@ -1012,38 +1123,41 @@
     core = lax.axis_index("dp") % 2
     at = [jnp.stack([(place + mp - k) % mp, core]) for k in range(mp)]
 
-    attn_weights = dp_gather(pack([w_query, w_key, w_value], LANES, padded_heads))
-    token_pieces = [tokens, ring_up(tokens)]
-    ff_pack = pack([w_gate, w_up], FF_BLOCK, padded_ff, token_pieces[1])
+    attn_pack = pack([w_query, w_key, w_value], LANES, padded_heads)
+    attn_weights = dp_gather(attn_pack)
+    ff_pack = pack([w_gate, w_up], FF_BLOCK, padded_ff, attn_pack)
     gate_up = dp_gather(ff_pack)
-    token_pieces.append(ring_up(token_pieces[1]))
-    token_pieces.append(ring_up(token_pieces[2]))
+    token_pieces = ring_gather(tokens)
     held = None
     for k in range(mp - 1):
         *held, mark = project(
             at[k], token_pieces[k], attn_gain[None], attn_weights, tables, held
         )
-    out_own = pack([w_out], LANES, padded_heads, token_pieces[-1], mark, ff_pack)
+    out_own = pack([w_out.T], LANES, padded_heads, token_pieces[-1], mark, ff_pack)
     out_pieces = [out_own] + [shift_back(out_own, mp - j) for j in range(1, mp)]
     *held, _ = project(
         at[mp - 1], token_pieces[-1], attn_gain[None], attn_weights, tables, held
     )
     qkv, normed_one, whole_tokens = held
-    attended, log_total = attend(qkv, prefix, heads)
+    attended, attended_send, log_total = attend(qkv, prefix, heads)
     out_pack = chain(out_pieces, attended)
-    attended_pieces = [attended, ring_up(attended)]
+    attended_pieces = [attended, ring_up(gate(attended_send, out_pack))]
     out_weights = dp_gather(gate(out_pack, attended_pieces[1], gate_up))
-    down_pack = pack([w_down], LANES, padded_ff, attended_pieces[1])
+    down_pack = pack([w_down.T], LANES, padded_ff, attended_pieces[1])
     down = dp_gather(down_pack)
     while len(attended_pieces) < mp:
         attended_pieces.append(ring_up(attended_pieces[-1]))
 
-    grad_own = scaled(out_grad, attended_pieces[-1], down_pack)
-    grad_pieces = [grad_own] + [shift_back(grad_own, mp - k) for k in range(1, mp)]
-    normed_two, middle = finish_middle(
+    grad_pieces = [scaled(out_grad, attended_pieces[-1], down_pack, out_weights)]
+    grad_pieces.append(ring_up(grad_pieces[0]))
+    normed_two, split_two, middle = finish_middle(
         at[0], attended_pieces, out_weights, whole_tokens, mlp_gain[None], rows
     )
+    grad_pieces.append(ring_up(gate(grad_pieces[1], normed_two)))
     hidden, slopes = feed(normed_two, gate_up)
+    while len(grad_pieces) < mp:
+        grad_pieces.append(ring_up(grad_pieces[-1]))
+    by_chip = paired()
 
     def back_of(k, held, kind=BF16, waits=()):
         *held, term = feed_back(
@@ -1053,47 +1167,56 @@
 
     width = normed_two.shape[1]
     grad_pieces.append(ring_up(grad_pieces[-1]))
-    held, total = back_of(1, None)
-    held, term = back_of(2, held)
+    held, total = back_of(1, None, waits=(grad_pieces[2],))
     arrived = ring_up(total)
+    held, term = back_of(2, held, waits=(grad_pieces[3],))
     held, term_three = back_of(3, held)
-    (grad_both, grad_mlp), term_own = back_of(4, held, F32)
-    total = join(term, arrived, (term_own,))
+    total = join(term, arrived, (term_three,))
     arrived = ring_up(total)
-    ff_weight = weight_grad(normed_two, grad_both, 0, width // 2, padded_ff, 21)
-    total = join(term_three, arrived, (ff_weight,))
-    arrived = ring_up(total)
-    down_weight = weight_grad(grad_mlp, hidden, 0, width // 2, padded_ff // 2, 12)
+    (grad_both, grad_mlp), term_own = back_of(mp, held, F32, (total,))
+    attended_own = own_rows(at[0], attended_pieces, rows)
+    if by_chip:
+        down_other = scatter_other(grad_mlp, hidden, 768, 6)
+        total = join(term_three, arrived, (down_other,))
+        arrived = ring_up(total)
+        ff_other = scatter_other(split_two, grad_both, 1024, 11, (total,))
+        down_chip = scatter_mine(
+            grad_mlp, hidden, 768, 6, swap(gate(down_other, total), 1), (ff_other,)
+        )
+        waits = (down_chip, ff_other, attended_own)
+    else:
+        total = join(term_three, arrived)
+        arrived = ring_up(total)
+        waits = (attended_own,)
     grad_middle, grad_attn, split_attn, gain_two, zero = own_back(
-        core[None], term_own, arrived, middle, out_grad, mlp_gain[None], (down_weight,)
-    )
-    ff_share = scatter_whole(gate(ff_weight, total))
-    down_share = scatter_whole(gate(down_weight, zero))
-
-    grad_attended = matmul(grad_attn, out_weights).astype(BF16)
-    mine = [
-        grad_attended[:, k * padded_heads : (k + 1) * padded_heads] for k in range(mp)
-    ]
-    attended_own = jnp.concatenate(
-        [row_block(piece, place) for piece in attended_pieces], axis=1
-    )
-
+        core[None], term_own, arrived, middle, out_grad, mlp_gain[None], waits
+    )
+    *mine, zero = spread(grad_attn, out_weights, mp)
     def mlp_chunk(k, zero):
         return lax.optimization_barrier(
             outer_cols(row_block(hidden, at[k % mp][0] + zero[0]), down)
         )
 
-    by_chip = paired()
     arrived = [mine[0]] + [shift_back(mine[k], k) for k in range(1, mp)]
-    out_other = scatter_other(split_attn, attended_own, 1280, 5, (grad_attended,))
     chunk_one = mlp_chunk(1, zero).astype(BF16)
-    chunk_two = mlp_chunk(2, zero)
+    if by_chip:
+        ff_chip = scatter_mine(
+            split_two, grad_both, 1024, 11, swap(gate(ff_other, split_attn), 1), (chunk_one,)
+        )
+        ff_share = scatter_around(ff_chip)
+        down_share = scatter_around(gate(down_chip, zero))
+        waits = (ff_chip,)
+    else:
+        ff_share = scatter_plain(split_two, grad_both)
+        down_share = scatter_plain(grad_mlp, hidden)
+        waits = ()
+    out_other = scatter_other(split_attn, attended_own, 1280, 5, (chunk_one,))
     mlp_arrived = ring_up(gate(chunk_one, *arrived[1:]))
     out_arrived = swap(out_other, 1) if by_chip else None
     spots = jnp.stack([prefix[0], place])
     back = attend_back(
         qkv, attended, arrived, log_total, tables, spots, heads,
-        (chunk_two, out_other) if by_chip else (chunk_two,),
+        (*waits, out_other) if by_chip else (),
     )
 
     def grad_one_term(k, zero=0):
@@ -1103,58 +1226,74 @@
 
     total = grad_one_term(1).astype(BF16)
     arrived = ring_up(total)
-    attn_other = scatter_other(normed_one, back, 640, 8, (total,))
-    attn_arrived = swap(attn_other, 1) if by_chip else None
-    out_chip = scatter_mine(split_attn, attended_own, 1280, 5, out_arrived, (total,))
-    term = grad_one_term(2)
-    total, zero = join_marked(term, arrived, (out_chip, attn_other) if by_chip else ())
-    arrived = ring_up(total)
-    mlp_total = join(chunk_two, mlp_arrived, (total,))
-    mlp_arrived = ring_up(mlp_total)
-    attn_chip = scatter_mine(normed_one, back, 640, 8, attn_arrived, (total,))
+    index = lax.axis_index("dp")
+    chip = jnp.stack([index // 2 % 2, index // 4])
     if by_chip:
-        out_kept, out_moved = scatter_first(out_chip)
-        attn_kept, attn_moved = scatter_first(attn_chip)
-    term = grad_one_term(3, zero[0])
-    chunk = mlp_chunk(3, zero)
-    total, zero = join_marked(term, arrived, (attn_chip,))
-    arrived = ring_up(total)
-    if by_chip:
-        out_half = scatter_join(out_kept, out_moved, (total,))
+        attn_other = scatter_other(normed_one, back, 640, 8, (total, mlp_arrived))
+        attn_arrived = swap(attn_other, 1)
+        out_parts, zero = scatter_chip(
+            chip, split_attn, attended_own, 1280, 8, out_arrived, (total, attn_other)
+        )
+        out_moved = scatter_first(out_parts)
+        chunk = mlp_chunk(2, zero)
+        total, zero = join_marked(
+            grad_one_term(2, zero[0]), arrived,
+            (attn_other, out_parts[1], out_parts[3], chunk),
+        )
+        arrived = ring_up(total)
+        mlp_total = join(chunk, mlp_arrived, (total,))
+        mlp_arrived = ring_up(mlp_total)
+        attn_parts, zero = scatter_chip(
+            chip, normed_one, back, 640, 10, attn_arrived, (total, mlp_total)
+        )
+        attn_moved = scatter_first(attn_parts)
+        term = grad_one_term(3, zero[0])
+        chunk = mlp_chunk(3, zero)
+        total, zero = join_marked(term, arrived, (attn_parts[1], attn_parts[3], chunk))
+        arrived = ring_up(total)
+        term = grad_one_term(4, zero[0])
+        out_half = scatter_halves(chip, out_parts, out_moved, (total,))
         out_share = scatter_second(out_half)
-        attn_half = scatter_join(attn_kept, attn_moved, (total, *out_half))
+        mlp_total = join(chunk, mlp_arrived, (total, out_half[0][1], out_half[1][1]))
+        mlp_arrived = ring_up(mlp_total)
+        attn_half = scatter_halves(chip, attn_parts, attn_moved, (mlp_total,))
         attn_share = scatter_second(attn_half)
-        mlp_total = join(chunk, mlp_arrived, (total, *out_half))
+        waits = (mlp_total, attn_half[0][1], attn_half[1][1])
     else:
-        out_share = scatter_whole(out_chip)
-        attn_share = scatter_whole(attn_chip)
-        mlp_total = join(chunk, mlp_arrived, (total,))
-    term = grad_one_term(4, zero[0])
-    mlp_arrived = ring_up(mlp_total)
+        out_share = scatter_plain(split_attn, attended_own)
+        attn_share = scatter_plain(normed_one, back)
+        total = join(grad_one_term(2), arrived)
+        arrived = ring_up(total)
+        mlp_arrived = ring_up(join(mlp_chunk(2, zero), mlp_arrived))
+        total = join(grad_one_term(3), arrived)
+        arrived = ring_up(total)
+        mlp_arrived = ring_up(join(mlp_chunk(3, zero), mlp_arrived))
+        term = grad_one_term(4)
+        waits = ()
     input_grad, gain_one, zero = finish_input(
-        term, arrived, tokens, grad_middle, attn_gain[None], (mlp_total,)
-    )
-    out_total, *out_mine = out_sum(out_share, mp, padded_heads)
+        term, arrived, tokens, grad_middle, attn_gain[None], waits
+    )
+    out_total, *out_mine = out_sum(out_share, mp, padded_heads, (mlp_arrived,))
     out_moved = [shift_back(out_mine[k - 1], k) for k in range(1, mp)]
     gains = sum_all(jnp.concatenate([gain_one, gain_two]))
     chunk = mlp_chunk(4, zero)
     grad_w_query, grad_w_key, grad_w_value = unmix(attn_share, 3, LANES, width_heads)
     grad_w_gate, grad_w_up = unmix(ff_share, 2, FF_BLOCK, width_ff)
-    grad_w_down = turn(down_share, width_ff)
-    grad_w_out = out_final(out_total, out_moved, width_heads)
-    block_out = finish_block(
-        middle, chunk, mlp_arrived, (grad_w_gate, grad_w_down, grad_w_query, grad_w_out)
-    )
+    (grad_w_down,) = unmix(down_share, 1, LANES, width_ff)
+    grad_w_out = out_final(
+        out_total, out_moved, width_heads, (grad_w_gate, grad_w_down, grad_w_query)
+    )
+    block_out = finish_block(middle, chunk, mlp_arrived, (grad_w_out,))
     return (
         block_out,
         input_grad,
         grad_w_query,
         grad_w_key,
         grad_w_value,
-        grad_w_out,
+        grad_w_out.T,
         grad_w_gate,
         grad_w_up,
-        grad_w_down,
+        grad_w_down.T,
         gains[0],
         gains[1],
     )

time: 844 us -> 754 us (0.89)
  starting transfers between devices: 87.2 us -> 41.4 us
  local copies, waits for them, and re-layouts: 55.5 us -> 18.7 us
  Pallas kernels: 349 us -> 367 us
  waiting for transfers between devices: 253 us -> 236 us
    ppermute x12 -> x9, waiting for transfers between devices: 93.4 us -> 6.86 us  [shift_back(): return lax.ppermute(value, 'mp', [(i, (i - count) % n) for i in range(n)])]
    ppermute x15 -> x18, waiting for transfers between devices: 135 us -> 191 us  [ring_up(): return lax.ppermute(value, 'mp', [(i, (i + 1) % n) for i in range(n)])]
    pallas_call x4 -> x12, Pallas kernels: 11.9 us -> 55 us  [the longest x2 17.6 us: scatter_chip(): pl.pallas_call(chip_kernel, out_shape=(out, out, out, out, jax.ShapeDtype...]
    ppermute x15 -> x18, starting transfers between devices: 60.3 us -> 18.6 us  [ring_up(): return lax.ppermute(value, 'mp', [(i, (i + 1) % n) for i in range(n)])]
    ppermute x5, waiting for transfers between devices: 0.25 us -> 26.7 us  [sum_all(): value = value + lax.ppermute(value, axis, [(i, i ^ bit) for i in range(n)])]
    ppermute x10 -> x12, waiting for transfers between devices: 24.3 us -> 0.03 us  [swap(): return lax.ppermute(value, 'dp', [(i, i ^ bit) for i in range(n)])]
    squeeze x8 -> x0, local copies, waits for them, and re-layouts: 14.9 us -> none  [the longest x4 8.82 us: pick(): return lax.dynamic_index_in_dim(array, which, 0, False)]
    pallas_call x10 -> x6, Pallas kernels: 31 us -> 18.7 us  [join_marked(): pl.pallas_call(join_kernel, out_shape=(jax.ShapeDtypeStruct(one.shape, BF...]
  transfers between devices with their start and end apart: 48 -> 50, of which waited for: 19 -> 19; matrix products, arithmetic and copies ran while one was open for 13% -> 9% of each run, Pallas kernels for 40% -> 46%
where the time goes in v3:
time: 754 us; the launch traced here: 746 us
  Pallas kernels  367 us (49%)
  waiting for transfers between devices  236 us (31%)
  matrix products  57.7 us (8%)
  starting transfers between devices  41.4 us (5%)
  between operations  19.1 us (3%)
  local copies, waits for them, and re-layouts  18.7 us (2%)
    ppermute x18, waiting for transfers between devices, ring_up(): return lax.ppermute(value, 'mp', [(i, (i + 1) % n) for i in range(n)])  191 us
    pallas_call x4, Pallas kernels, feed_back(): pl.pallas_call(feed_back_kernel, out_shape=(jax.ShapeDtypeStruct((LEN, 2...  63.3 us
    dot_general x8, matrix products, outer_cols(): lax.dot_general(left, right, (((1,), (1,)), ((), ())), preferred_element_...  57.7 us
    pallas_call x6, Pallas kernels, weight_grad(): pl.pallas_call(functools.partial(weight_kernel, arrived is not None), out...  55.2 us
    pallas_call x4, Pallas kernels, project(): pl.pallas_call(functools.partial(project_kernel, fresh), out_shape=outs,...  44.5 us
    pallas_call x1, Pallas kernels, finish_middle(): pl.pallas_call(functools.partial(middle_kernel, count), out_shape=(jax.Sh...  29.1 us
    pallas_call x1, Pallas kernels, attend_back(): pl.pallas_call(functools.partial(attend_back_kernel, heads, count), out_s...  28.6 us
    ppermute x5, waiting for transfers between devices, sum_all(): value = value + lax.ppermute(value, axis, [(i, i ^ bit) for i in range(n)])  26.7 us
  transfers between devices with their start and end apart: 50, of which 19 were waited for; matrix products, arithmetic and copies ran while one was open for 9% of the time, Pallas kernels for 46%

profile of v3, /device:TPU:0, one launch (start us, length us, event | category | flops | bytes accessed | tf_op | source)
XLA Modules:
  0.0 746.0 jit_solution(8976932017115919436)
XLA Ops:
  15.8 28.0 %collective-permute-done.x_ref = bf16[256,2304]{1,0:T(8,128)(2,1)S(1)} collective-permute-done((bf16[256,2304]{1,0:T(8,128)(2,1)S(1)}, bf16[256,2304]{1,0:T(8,128)(2,1)S(1)}, u32[]{:S(2)}, u32[]{:S(2)}) %collective-permute-start) | collective-permute-done | bytes 1179680 | tf_op jit(solution)/shard_map/ppermute | solution.py:56
  47.6 25.2 %collective-permute-done.1.x_ref = bf16[256,2304]{1,0:T(8,128)(2,1)S(1)} collective-permute-done((bf16[256,2304]{1,0:T(8,128)(2,1)S(1)}, bf16[256,2304]{1,0:T(8,128)(2,1)S(1)}, u32[]{:S(2)}, u32[]{:S(2)}) %collective-permute-start.1) | collective-permute-done | bytes 1179680 | tf_op jit(solution)/shard_map/ppermute | solution.py:56
  72.8 11.5 %project.4 = (bf16[1024,1920]{1,0:T(8,128)(2,1)}, bf16[2,1024,1152]{2,1,0:T(8,128)(2,1)}, bf16[1024,2304]{1,0:T(8,128)(2,1)}, f32[8,128]{1,0:T(8,128)}) custom-call(s32[2]{0:T(128)} %pad_add_fusion.where_ref.place_ref, bf16[256,2304]{1,0:T(8,128)(2,1)} %x_ref.3, f32[1,2304]{1,0:T(1,128)} %broadcast_in_dim.4.gain_ref, ...), custom_call_target="tpu_custom_call" | custom-call | flops 32999999488 | tf_op jit(solution)/shard_map/project/pallas_call | solution.py:407
  84.3 11.0 %project.5 = (bf16[1024,1920]{1,0:T(8,128)(2,1)}, bf16[2,1024,1152]{2,1,0:T(8,128)(2,1)}, bf16[1024,2304]{1,0:T(8,128)(2,1)}, f32[8,128]{1,0:T(8,128)}) custom-call(s32[2]{0:T(128)} %pad_add_fusion.3.where_ref, bf16[256,2304]{1,0:T(8,128)(2,1)} %copy-done.11, ...), custom_call_target="tpu_custom_call", output_to_operand_aliasing={{0}: (6, {}), {1}: (7, {}), {2}: (8, {})} | custom-call | flops 32999999488 | tf_op jit(solution)/shard_map/project/pallas_call | solution.py:407
  95.2 11.0 %project.6 = (bf16[1024,1920]{1,0:T(8,128)(2,1)}, bf16[2,1024,1152]{2,1,0:T(8,128)(2,1)}, bf16[1024,2304]{1,0:T(8,128)(2,1)}, f32[8,128]{1,0:T(8,128)}) custom-call(s32[2]{0:T(128)} %pad_add_fusion.2.where_ref, bf16[256,2304]{1,0:T(8,128)(2,1)} %copy-done.10, ...), custom_call_target="tpu_custom_call", output_to_operand_aliasing={{0}: (6, {}), {1}: (7, {}), {2}: (8, {})} | custom-call | flops 32999999488 | tf_op jit(solution)/shard_map/project/pallas_call | solution.py:407
  113.8 11.1 %project.7 = (bf16[1024,1920]{1,0:T(8,128)(2,1)}, bf16[2,1024,1152]{2,1,0:T(8,128)(2,1)}, bf16[1024,2304]{1,0:T(8,128)(2,1)}, f32[8,128]{1,0:T(8,128)}) custom-call(s32[2]{0:T(128)} %pad_add_fusion.1.where_ref, bf16[256,2304]{1,0:T(8,128)(2,1)} %copy-done.15, ...), custom_call_target="tpu_custom_call", output_to_operand_aliasing={{0}: (6, {}), {1}: (7, {}), {2}: (8, {})} | custom-call | flops 32999999488 | tf_op jit(solution)/shard_map/project/pallas_call | solution.py:407
  124.8 18.1 %attend.1 = (bf16[1024,640]{1,0:T(8,128)(2,1)}, bf16[1024,640]{1,0:T(8,128)(2,1)}, f32[5,2,1024]{2,1,0:T(2,128)}) custom-call(s32[1]{0:T(128)S(6)} %copy.69.prefix_ref, bf16[1024,1920]{1,0:T(8,128)(2,1)} %get-tuple-element.99.qkv_ref), custom_call_target="tpu_custom_call" | custom-call | flops 54000001024 | tf_op jit(solution)/shard_map/attend/pallas_call | solution.py:491
  149.5 27.0 %collective-permute-done.6.refs_1_ = bf16[1024,640]{1,0:T(8,128)(2,1)S(1)} collective-permute-done((bf16[1024,640]{1,0:T(8,128)(2,1)}, bf16[1024,640]{1,0:T(8,128)(2,1)S(1)}, u32[]{:S(2)}, u32[]{:S(2)}) %collective-permute-start.6) | collective-permute-done | bytes 1310752 | tf_op jit(solution)/shard_map/ppermute | solution.py:56
  178.6 28.3 %collective-permute-done.7.refs_2_ = bf16[1024,640]{1,0:T(8,128)(2,1)S(1)} collective-permute-done((bf16[1024,640]{1,0:T(8,128)(2,1)}, bf16[1024,640]{1,0:T(8,128)(2,1)S(1)}, u32[]{:S(2)}, u32[]{:S(2)}) %collective-permute-start.7) | collective-permute-done | bytes 1310752 | tf_op jit(solution)/shard_map/ppermute | solution.py:56
  210.2 24.8 %collective-permute-done.8.refs_3_.refs_0_ = bf16[1024,640]{1,0:T(8,128)(2,1)} collective-permute-done((bf16[1024,640]{1,0:T(8,128)(2,1)S(1)}, bf16[1024,640]{1,0:T(8,128)(2,1)}, u32[]{:S(2)}, u32[]{:S(2)}) %collective-permute-start.8) | collective-permute-done | bytes 1310752 | tf_op jit(solution)/shard_map/ppermute | solution.py:56
  235.0 11.0 %all-gather.9.cloned.1.call-done.refs_4_.refs_2_.weight_ref = bf16[2304,2560]{1,0:T(8,128)(2,1)} async-done(((bf16[288,2560]{1,0:T(8,128)(2,1)}), bf16[2304,2560]{1,0:T(8,128)(2,1)}) %all-gather.9.cloned.1.call-update) | async-done | bytes 11796496 | tf_op jit(solution)/shard_map/all_gather | solution.py:103
  250.5 29.1 %finish_middle.1 = (bf16[1024,2304]{1,0:T(8,128)(2,1)}, bf16[2,1024,1152]{2,1,0:T(8,128)(2,1)}, f32[256,2304]{1,0:T(8,128)}) custom-call(s32[2]{0:T(128)} %pad_add_fusion.where_ref.place_ref, bf16[1024,640]{1,0:T(8,128)(2,1)} %get-tuple-element.100.refs_4_.refs_0_.out_ref, bf16[1024,640]{1,0:T(8,128)(2,1)} %copy-done, bf16[1024,640]{1,0:T(8,128)(2,1)} %copy-done.8, ...), custom_call_target="tpu_custom_call" | custom-call | flops 65999998976 | tf_op jit(solution)/shard_map/finish_middle/pallas_call | solution.py:632
  282.7 21.4 %feed.1 = (bf16[1024,1536]{1,0:T(8,128)(2,1)}, bf16[1024,3072]{1,0:T(8,128)(2,1)}) custom-call(bf16[1024,2304]{1,0:T(8,128)(2,1)} %get-tuple-element.105.normed_ref.refs_1_, bf16[2304,3072]{1,0:T(8,128)(2,1)} %all-gather.7.cloned.1.call-done.refs_2_.weight_ref), custom_call_target="tpu_custom_call" | custom-call | flops 62999998464 | tf_op jit(solution)/shard_map/feed/pallas_call | solution.py:676
  312.2 15.7 %feed_back.4 = (bf16[1024,3072]{1,0:T(8,128)(2,1)}, bf16[2,1024,1152]{2,1,0:T(8,128)(2,1)}, bf16[256,2304]{1,0:T(8,128)(2,1)}) custom-call(s32[2]{0:T(128)} %pad_add_fusion.3.where_ref, bf16[256,2304]{1,0:T(8,128)(2,1)} %copy-done.1, bf16[1024,3072]{1,0:T(8,128)(2,1)} %get-tuple-element.107.slope_ref, ...), custom_call_target="tpu_custom_call" | custom-call | flops 44999999488 | tf_op jit(solution)/shard_map/feed_back/pallas_call | solution.py:735
  328.2 13.6 %collective-permute-done.11.refs_2_.grad_ref = bf16[256,2304]{1,0:T(8,128)(2,1)S(1)} collective-permute-done((bf16[256,2304]{1,0:T(8,128)(2,1)S(1)}, bf16[256,2304]{1,0:T(8,128)(2,1)S(1)}, u32[]{:S(2)}, u32[]{:S(2)}) %collective-permute-start.11) | collective-permute-done | bytes 1179680 | tf_op jit(solution)/shard_map/ppermute | solution.py:56
  342.9 15.7 %feed_back.5 = (bf16[1024,3072]{1,0:T(8,128)(2,1)}, bf16[2,1024,1152]{2,1,0:T(8,128)(2,1)}, bf16[256,2304]{1,0:T(8,128)(2,1)}) custom-call(s32[2]{0:T(128)} %pad_add_fusion.2.where_ref, bf16[256,2304]{1,0:T(8,128)(2,1)} %copy-done.16, bf16[1024,3072]{1,0:T(8,128)(2,1)} %get-tuple-element.107.slope_ref, ...), custom_call_target="tpu_custom_call", output_to_operand_aliasing={{0}: (5, {}), {1}: (6, {})} | custom-call | flops 44999999488 | tf_op jit(solution)/shard_map/feed_back/pallas_call | solution.py:735
  358.6 15.7 %feed_back.6 = (bf16[1024,3072]{1,0:T(8,128)(2,1)}, bf16[2,1024,1152]{2,1,0:T(8,128)(2,1)}, bf16[256,2304]{1,0:T(8,128)(2,1)}) custom-call(s32[2]{0:T(128)} %pad_add_fusion.1.where_ref, bf16[256,2304]{1,0:T(8,128)(2,1)} %copy-done.17, bf16[1024,3072]{1,0:T(8,128)(2,1)} %get-tuple-element.107.slope_ref, ...), custom_call_target="tpu_custom_call", output_to_operand_aliasing={{0}: (5, {}), {1}: (6, {})} | custom-call | flops 44999999488 | tf_op jit(solution)/shard_map/feed_back/pallas_call | solution.py:735
  378.6 16.1 %feed_back.7 = (bf16[1024,3072]{1,0:T(8,128)(2,1)}, bf16[2,1024,1152]{2,1,0:T(8,128)(2,1)}, f32[256,2304]{1,0:T(8,128)}) custom-call(s32[2]{0:T(128)} %pad_add_fusion.where_ref.place_ref, bf16[256,2304]{1,0:T(8,128)(2,1)} %scaled.1.grad_ref, bf16[1024,3072]{1,0:T(8,128)(2,1)} %get-tuple-element.107.slope_ref, ...), custom_call_target="tpu_custom_call", output_to_operand_aliasing={{0}: (5, {}), {1}: (6, {})} | custom-call | flops 44999999488 | tf_op jit(solution)/shard_map/feed_back/pallas_call | solution.py:735
  412.5 11.9 %weight_grad.7.refs_1_.refs_0_ = bf16[1152,3072]{1,0:T(8,128)(2,1)} custom-call(bf16[2,1024,1152]{2,1,0:T(8,128)(2,1)} %get-tuple-element.121.left_ref, bf16[1024,3072]{1,0:T(8,128)(2,1)} %get-tuple-element.122.right_ref, bf16[256,2304]{1,0:T(8,128)(2,1)} %get-tuple-element.120.refs_1_.refs_0_), custom_call_target="tpu_custom_call" | custom-call | flops 32999999488 | tf_op jit(solution)/shard_map/weight_grad/pallas_call | solution.py:147
  426.2 8.1 %weight_grad.8.refs_0_ = bf16[1152,1536]{1,0:T(8,128)(2,1)} custom-call(bf16[2,1024,1152]{2,1,0:T(8,128)(2,1)} %get-tuple-element.119.left_ref, bf16[1024,1536]{1,0:T(8,128)(2,1)} %get-tuple-element.106.right_ref, bf16[1152,1536]{1,0:T(8,128)(2,1)} %copy-done.5, bf16[1152,3072]{1,0:T(8,128)(2,1)} %weight_grad.7.refs_1_.refs_0_), custom_call_target="tpu_custom_call" | custom-call | flops 17999998976 | tf_op jit(solution)/shard_map/weight_grad/pallas_call | solution.py:147
  434.4 8.2 %collective-permute-done.14.arrived_ref = bf16[256,2304]{1,0:T(8,128)(2,1)S(1)} collective-permute-done((bf16[256,2304]{1,0:T(8,128)(2,1)S(1)}, bf16[256,2304]{1,0:T(8,128)(2,1)S(1)}, u32[]{:S(2)}, u32[]{:S(2)}) %collective-permute-start.14) | collective-permute-done | bytes 1179680 | tf_op jit(solution)/shard_map/ppermute | solution.py:56
  450.1 8.7 %spread.1 = (bf16[256,640]{1,0:T(8,128)(2,1)}, bf16[256,640]{1,0:T(8,128)(2,1)}, bf16[256,640]{1,0:T(8,128)(2,1)}, bf16[256,640]{1,0:T(8,128)(2,1)}, s32[1]{0:T(128)}) custom-call(bf16[256,2304]{1,0:T(8,128)(2,1)} %get-tuple-element.123.value_ref, bf16[2304,2560]{1,0:T(8,128)(2,1)} %all-gather.9.cloned.1.call-done.refs_4_.refs_2_.weight_ref), custom_call_target="tpu_custom_call" | custom-call | flops 24000000000 | tf_op jit(solution)/shard_map/spread/pallas_call | solution.py:820
  474.9 13.2 %weight_grad.9.refs_7_ = bf16[1152,3072]{1,0:T(8,128)(2,1)} custom-call(bf16[2,1024,1152]{2,1,0:T(8,128)(2,1)} %get-tuple-element.121.left_ref, bf16[1024,3072]{1,0:T(8,128)(2,1)} %get-tuple-element.122.right_ref, bf16[1152,3072]{1,0:T(8,128)(2,1)} %collective-permute-done.19.refs_0_, bf16[256,2304]{1,0:T(8,128)(2,1)} %fusion.14.refs_1_.refs_0_), custom_call_target="tpu_custom_call" | custom-call | flops 32999999488 | tf_op jit(solution)/shard_map/weight_grad/pallas_call | solution.py:147
  492.9 28.6 %attend_back.1.right_ref = bf16[1024,1920]{1,0:T(8,128)(2,1)} custom-call(s32[2]{0:T(128)} %pad_add_fusion.4.prefix_ref, bf16[1024,1920]{1,0:T(8,128)(2,1)} %get-tuple-element.99.qkv_ref, bf16[1024,640]{1,0:T(8,128)(2,1)} %get-tuple-element.100.refs_4_.refs_0_.out_ref, bf16[256,640]{1,0:T(8,128)(2,1)} %get-tuple-element.124.refs_0_, ...), custom_call_target="tpu_custom_call" | custom-call | flops 83999997952 | tf_op jit(solution)/shard_map/attend_back/pallas_call | solution.py:575
  532.6 9.4 %weight_grad.11.refs_1_.refs_0_ = bf16[1152,1920]{1,0:T(8,128)(2,1)} custom-call(bf16[2,1024,1152]{2,1,0:T(8,128)(2,1)} %get-tuple-element.131.left_ref, bf16[1024,1920]{1,0:T(8,128)(2,1)} %attend_back.1.right_ref, bf16[256,2304]{1,0:T(8,128)(2,1)} %fusion.6.refs_0_, bf16[256,2304]{1,0:T(8,128)(2,1)} %copy-done.14), custom_call_target="tpu_custom_call" | custom-call | flops 24000000000 | tf_op jit(solution)/shard_map/weight_grad/pallas_call | solution.py:147
  558.1 7.9 %fusion.4.one_ref = f32[256,2304]{1,0:T(8,128)} fusion(bf16[2304,1920]{1,0:T(8,128)(2,1)} %all-gather.5.cloned.1.call-done.w_ref, bf16[1024,1920]{1,0:T(8,128)(2,1)} %attend_back.1.right_ref, s32[]{:T(128)S(6)} %select_n.64), kind=kOutput, calls=%fused_computation.4 | convolution fusion | flops 2264924160 | bytes 12189700 | tf_op jit(solution)/shard_map/dot_general | solution.py:39
  574.5 10.8 %scatter_chip.3 = (bf16[2,144,1920]{2,1,0:T(8,128)(2,1)}, bf16[2,144,1920]{2,1,0:T(8,128)(2,1)}, bf16[2,144,1920]{2,1,0:T(8,128)(2,1)}, bf16[2,144,1920]{2,1,0:T(8,128)(2,1)}, s32[1]{0:T(128)}) custom-call(s32[2]{0:T(128)} %pad_add_fusion.5.where_ref, bf16[2,1024,1152]{2,1,0:T(8,128)(2,1)} %get-tuple-element.131.left_ref, ...), custom_call_target="tpu_custom_call" | custom-call | flops 30000001024 | tf_op jit(solution)/shard_map/scatter_chip/pallas_call | solution.py:190
  594.6 7.9 %fusion.2.one_ref = f32[256,2304]{1,0:T(8,128)} fusion(bf16[2304,1920]{1,0:T(8,128)(2,1)} %all-gather.5.cloned.1.call-done.w_ref, bf16[1024,1920]{1,0:T(8,128)(2,1)} %attend_back.1.right_ref, s32[]{:T(128)S(6)} %select_n.65), kind=kOutput, calls=%fused_computation.2 | convolution fusion | flops 2264924160 | bytes 12189700 | tf_op jit(solution)/shard_map/dot_general | solution.py:39
  616.3 9.3 %collective-permute-done.26.two_ref = bf16[256,2304]{1,0:T(8,128)(2,1)} collective-permute-done((bf16[256,2304]{1,0:T(8,128)(2,1)}, bf16[256,2304]{1,0:T(8,128)(2,1)}, u32[]{:S(2)}, u32[]{:S(2)}) %collective-permute-start.26) | collective-permute-done | bytes 1179680 | tf_op jit(solution)/shard_map/ppermute | solution.py:56
  667.0 11.5 %collective-permute-done.41 = f32[2,2304]{1,0:T(2,128)S(1)} collective-permute-done((f32[2,2304]{1,0:T(2,128)S(1)}, f32[2,2304]{1,0:T(2,128)S(1)}, u32[]{:S(2)}, u32[]{:S(2)}) %collective-permute-start.41) | collective-permute-done | bytes 18464 | tf_op jit(solution)/shard_map/ppermute | solution.py:88
  679.7 11.0 %collective-permute-done.31.refs_4_.arrived_ref = bf16[256,2304]{1,0:T(8,128)(2,1)S(1)} collective-permute-done((bf16[256,2304]{1,0:T(8,128)(2,1)S(1)}, bf16[256,2304]{1,0:T(8,128)(2,1)S(1)}, u32[]{:S(2)}, u32[]{:S(2)}) %collective-permute-start.31) | collective-permute-done | bytes 1179680 | tf_op jit(solution)/shard_map/ppermute | solution.py:56
  705.4 13.9 %collective-permute-done.43 = f32[2,2304]{1,0:T(2,128)S(1)} collective-permute-done((f32[2,2304]{1,0:T(2,128)S(1)}, f32[2,2304]{1,0:T(2,128)S(1)}, u32[]{:S(2)}, u32[]{:S(2)}) %collective-permute-start.43) | collective-permute-done | bytes 18464 | tf_op jit(solution)/shard_map/ppermute | solution.py:88
  (223 shorter events, 231.8 us)
Async XLA Ops:
  7.2 65.6 %all-gather.5.cloned.1.call-start = ((), (), s32[]{:S(2)}) async-start(), calls=%async_computation.2 | async-start | bytes 9953280 | tf_op jit(solution)/shard_map/all_gather | solution.py:103
  9.7 166.8 %all-gather.7.cloned.1.call-start = ((), (), s32[]{:S(2)}) async-start(), calls=%async_computation.3 | async-start | bytes 15925248 | tf_op jit(solution)/shard_map/all_gather | solution.py:103
  12.7 233.3 %all-gather.9.cloned.1.call-start = ((), (), s32[]{:S(2)}) async-start(), calls=%async_computation.4 | async-start | bytes 13271040 | tf_op jit(solution)/shard_map/all_gather | solution.py:103
  12.8 31.1 %collective-permute-start = (bf16[256,2304]{1,0:T(8,128)(2,1)S(1)}, bf16[256,2304]{1,0:T(8,128)(2,1)S(1)}, u32[]{:S(2)}, u32[]{:S(2)}) collective-permute-start(bf16[256,2304]{1,0:T(8,128)(2,1)S(1)} %copy-done.9), channel_id=1, source_target_pairs={{0,1},{1,2},{2,3},{3,0},{4,5},{5,6},{6,7},{7,4},{8,9},{9,10},{10,1... | collective-permute-start | bytes 3538952 | tf_op jit(solution)/shard_map/ppermute | solution.py:56
  72.8 33.5 %collective-permute-start.2 = (bf16[256,2304]{1,0:T(8,128)(2,1)S(1)}, bf16[256,2304]{1,0:T(8,128)(2,1)S(1)}, u32[]{:S(2)}, u32[]{:S(2)}) collective-permute-start(bf16[256,2304]{1,0:T(8,128)(2,1)S(1)} %collective-permute-done.1.x_ref), channel_id=1, source_target_pairs={{0,1},{1,2},{2,3},{3,0},{4,5},{5,6},{6,7},{7,4},{8,9},{9,10},{10,1... | collective-permute-start | bytes 3538952 | tf_op jit(solution)/shard_map/ppermute | solution.py:56
  109.1 33.9 %collective-permute-start.5 = (bf16[288,640]{1,0:T(8,128)(2,1)}, bf16[288,640]{1,0:T(8,128)(2,1)S(1)}, u32[]{:S(2)}, u32[]{:S(2)}) collective-permute-start(bf16[288,640]{1,0:T(8,128)(2,1)} %pack.6.refs_0_), channel_id=1, source_target_pairs={{0,3},{1,0},{2,1},{3,2},{4,7},{5,4},{6,5},{7,6},{8,11},{9,8},{10,9... | collective-permute-start | bytes 1105928 | tf_op jit(solution)/shard_map/ppermute | solution.py:80
  112.9 30.0 %collective-permute-start.4 = (bf16[288,640]{1,0:T(8,128)(2,1)}, bf16[288,640]{1,0:T(8,128)(2,1)S(1)}, u32[]{:S(2)}, u32[]{:S(2)}) collective-permute-start(bf16[288,640]{1,0:T(8,128)(2,1)} %pack.6.refs_0_), channel_id=1, source_target_pairs={{0,2},{1,3},{2,0},{3,1},{4,6},{5,7},{6,4},{7,5},{8,10},{9,11},{10,... | collective-permute-start | bytes 1105928 | tf_op jit(solution)/shard_map/ppermute | solution.py:80
  112.9 30.0 %collective-permute-start.3 = (bf16[288,640]{1,0:T(8,128)(2,1)}, bf16[288,640]{1,0:T(8,128)(2,1)S(1)}, u32[]{:S(2)}, u32[]{:S(2)}) collective-permute-start(bf16[288,640]{1,0:T(8,128)(2,1)} %pack.6.refs_0_), channel_id=1, source_target_pairs={{0,1},{1,2},{2,3},{3,0},{4,5},{5,6},{6,7},{7,4},{8,9},{9,10},{10,1... | collective-permute-start | bytes 1105928 | tf_op jit(solution)/shard_map/ppermute | solution.py:80
  146.5 30.0 %collective-permute-start.6 = (bf16[1024,640]{1,0:T(8,128)(2,1)}, bf16[1024,640]{1,0:T(8,128)(2,1)S(1)}, u32[]{:S(2)}, u32[]{:S(2)}) collective-permute-start(bf16[1024,640]{1,0:T(8,128)(2,1)} %gate.7), channel_id=1, source_target_pairs={{0,1},{1,2},{2,3},{3,0},{4,5},{5,6},{6,7},{7,4},{8,9},{9,10},{10,1... | collective-permute-start | bytes 3932168 | tf_op jit(solution)/shard_map/ppermute | solution.py:56
  177.6 133.5 %all-gather.11.cloned.1.call-start = ((), (), s32[]{:S(2)}) async-start(), calls=%async_computation.5 | async-start | bytes 7962624 | tf_op jit(solution)/shard_map/all_gather | solution.py:103
  210.1 454.0 %reduce-scatter.5.cloned.1.call-start = ((), (), s32[]{:S(2)}) async-start(), calls=%async_computation.7 | async-start | bytes 4423680 | tf_op jit(solution)/shard_map/reduce_scatter | solution.py:301
  248.5 31.1 %collective-permute-start.9 = (bf16[256,2304]{1,0:T(8,128)(2,1)}, bf16[256,2304]{1,0:T(8,128)(2,1)S(1)}, u32[]{:S(2)}, u32[]{:S(2)}) collective-permute-start(bf16[256,2304]{1,0:T(8,128)(2,1)} %scaled.1.grad_ref), channel_id=1, source_target_pairs={{0,1},{1,2},{2,3},{3,0},{4,5},{5,6},{6,7},{7,4},{8,9},{9,10},{10,1... | collective-permute-start | bytes 3538952 | tf_op jit(solution)/shard_map/ppermute | solution.py:56
  281.1 30.0 %collective-permute-start.10 = (bf16[256,2304]{1,0:T(8,128)(2,1)}, bf16[256,2304]{1,0:T(8,128)(2,1)S(1)}, u32[]{:S(2)}, u32[]{:S(2)}) collective-permute-start(bf16[256,2304]{1,0:T(8,128)(2,1)} %gate.9), channel_id=1, source_target_pairs={{0,1},{1,2},{2,3},{3,0},{4,5},{5,6},{6,7},{7,4},{8,9},{9,10},{10,1... | collective-permute-start | bytes 3538952 | tf_op jit(solution)/shard_map/ppermute | solution.py:56
  311.2 30.7 %collective-permute-start.11 = (bf16[256,2304]{1,0:T(8,128)(2,1)S(1)}, bf16[256,2304]{1,0:T(8,128)(2,1)S(1)}, u32[]{:S(2)}, u32[]{:S(2)}) collective-permute-start(bf16[256,2304]{1,0:T(8,128)(2,1)S(1)} %collective-permute-done.10.refs_0_.grad_ref), channel_id=1, source_target_pairs={{0,1},{1,2},{2,3},{3,0},{4,5},{5,6},{6,7},{7,4},{8,9},{9,10},{10,1... | collective-permute-start | bytes 3538952 | tf_op jit(solution)/shard_map/ppermute | solution.py:56
  327.9 46.4 %collective-permute-start.12 = (bf16[256,2304]{1,0:T(8,128)(2,1)}, bf16[256,2304]{1,0:T(8,128)(2,1)S(1)}, u32[]{:S(2)}, u32[]{:S(2)}) collective-permute-start(bf16[256,2304]{1,0:T(8,128)(2,1)} %get-tuple-element.115), channel_id=1, source_target_pairs={{0,1},{1,2},{2,3},{3,0},{4,5},{5,6},{6,7},{7,4},{8,9},{9,10},{10,1... | collective-permute-start | bytes 3538952 | tf_op jit(solution)/shard_map/ppermute | solution.py:56
  412.1 30.5 %collective-permute-start.14 = (bf16[256,2304]{1,0:T(8,128)(2,1)S(1)}, bf16[256,2304]{1,0:T(8,128)(2,1)S(1)}, u32[]{:S(2)}, u32[]{:S(2)}) collective-permute-start(bf16[256,2304]{1,0:T(8,128)(2,1)S(1)} %copy-done.19), channel_id=1, source_target_pairs={{0,1},{1,2},{2,3},{3,0},{4,5},{5,6},{6,7},{7,4},{8,9},{9,10},{10,1... | collective-permute-start | bytes 3538952 | tf_op jit(solution)/shard_map/ppermute | solution.py:56
  459.5 264.4 %reduce-scatter.3.cloned.1.call-start = ((), (), s32[]{:S(2)}) async-start(), calls=%async_computation.6 | async-start | bytes 8847360 | tf_op jit(solution)/shard_map/reduce_scatter | solution.py:301
  474.9 67.1 %collective-permute-start.22 = (bf16[1152,2560]{1,0:T(8,128)(2,1)}, bf16[1152,2560]{1,0:T(8,128)(2,1)}, u32[]{:S(2)}, u32[]{:S(2)}) collective-permute-start(bf16[1152,2560]{1,0:T(8,128)(2,1)} %weight_grad.10.refs_8_), channel_id=1, source_target_pairs={{0,4},{4,0},{8,12},{12,8},{16,20},{20,16},{24,28},{28,24},{1,5},{5... | collective-permute-start | bytes 17694728 | tf_op jit(solution)/shard_map/ppermute | solution.py:99
  492.1 39.5 %collective-permute-start.20 = (bf16[256,2304]{1,0:T(8,128)(2,1)}, bf16[256,2304]{1,0:T(8,128)(2,1)S(1)}, u32[]{:S(2)}, u32[]{:S(2)}) collective-permute-start(bf16[256,2304]{1,0:T(8,128)(2,1)} %gate.12), channel_id=1, source_target_pairs={{0,1},{1,2},{2,3},{3,0},{4,5},{5,6},{6,7},{7,4},{8,9},{9,10},{10,1... | collective-permute-start | bytes 3538952 | tf_op jit(solution)/shard_map/ppermute | solution.py:56
  529.0 37.0 %collective-permute-start.23 = (bf16[256,2304]{1,0:T(8,128)(2,1)}, bf16[256,2304]{1,0:T(8,128)(2,1)}, u32[]{:S(2)}, u32[]{:S(2)}) collective-permute-start(bf16[256,2304]{1,0:T(8,128)(2,1)} %fusion.6.refs_0_), channel_id=1, source_target_pairs={{0,1},{1,2},{2,3},{3,0},{4,5},{5,6},{6,7},{7,4},{8,9},{9,10},{10,1... | collective-permute-start | bytes 3538952 | tf_op jit(solution)/shard_map/ppermute | solution.py:56
  542.0 32.5 %collective-permute-start.21 = (bf16[1152,1920]{1,0:T(8,128)(2,1)}, bf16[1152,1920]{1,0:T(8,128)(2,1)}, u32[]{:S(2)}, u32[]{:S(2)}) collective-permute-start(bf16[1152,1920]{1,0:T(8,128)(2,1)} %weight_grad.11.refs_1_.refs_0_), channel_id=1, source_target_pairs={{0,4},{4,0},{8,12},{12,8},{16,20},{20,16},{24,28},{28,24},{1,5},{5... | collective-permute-start | bytes 13271048 | tf_op jit(solution)/shard_map/ppermute | solution.py:99
  549.4 62.0 %collective-permute-start.27 = (bf16[2,144,2560]{2,1,0:T(8,128)(2,1)}, bf16[2,144,2560]{2,1,0:T(8,128)(2,1)S(1)}, u32[]{:S(2)}, u32[]{:S(2)}) collective-permute-start(bf16[2,144,2560]{2,1,0:T(8,128)(2,1)} %get-tuple-element.133.refs_1_), channel_id=1, source_target_pairs={{0,16},{4,20},{8,24},{12,28},{16,0},{20,4},{24,8},{28,12},{1,17},{... | collective-permute-start | bytes 4423688 | tf_op jit(solution)/shard_map/ppermute | solution.py:99
  550.2 56.2 %collective-permute-start.28 = (bf16[2,144,2560]{2,1,0:T(8,128)(2,1)}, bf16[2,144,2560]{2,1,0:T(8,128)(2,1)S(1)}, u32[]{:S(2)}, u32[]{:S(2)}) collective-permute-start(bf16[2,144,2560]{2,1,0:T(8,128)(2,1)} %get-tuple-element.134.refs_2_), channel_id=1, source_target_pairs={{0,8},{4,12},{8,0},{12,4},{16,24},{20,28},{24,16},{28,20},{1,9},{5... | collective-permute-start | bytes 4423688 | tf_op jit(solution)/shard_map/ppermute | solution.py:99
  569.3 33.3 %collective-permute-start.24 = (bf16[256,2304]{1,0:T(8,128)(2,1)}, bf16[256,2304]{1,0:T(8,128)(2,1)}, u32[]{:S(2)}, u32[]{:S(2)}) collective-permute-start(bf16[256,2304]{1,0:T(8,128)(2,1)} %get-tuple-element.135.refs_0_), channel_id=1, source_target_pairs={{0,1},{1,2},{2,3},{3,0},{4,5},{5,6},{6,7},{7,4},{8,9},{9,10},{10,1... | collective-permute-start | bytes 3538952 | tf_op jit(solution)/shard_map/ppermute | solution.py:56
  572.5 53.0 %collective-permute-start.26 = (bf16[256,2304]{1,0:T(8,128)(2,1)}, bf16[256,2304]{1,0:T(8,128)(2,1)}, u32[]{:S(2)}, u32[]{:S(2)}) collective-permute-start(bf16[256,2304]{1,0:T(8,128)(2,1)} %get-tuple-element.136.refs_1_), channel_id=1, source_target_pairs={{0,1},{1,2},{2,3},{3,0},{4,5},{5,6},{6,7},{7,4},{8,9},{9,10},{10,1... | collective-permute-start | bytes 3538952 | tf_op jit(solution)/shard_map/ppermute | solution.py:56
  586.0 54.4 %collective-permute-start.29 = (bf16[2,144,1920]{2,1,0:T(8,128)(2,1)}, bf16[2,144,1920]{2,1,0:T(8,128)(2,1)}, u32[]{:S(2)}, u32[]{:S(2)}) collective-permute-start(bf16[2,144,1920]{2,1,0:T(8,128)(2,1)} %get-tuple-element.138.refs_0_), channel_id=1, source_target_pairs={{0,16},{4,20},{8,24},{12,28},{16,0},{20,4},{24,8},{28,12},{1,17},{... | collective-permute-start | bytes 3317768 | tf_op jit(solution)/shard_map/ppermute | solution.py:99
  602.5 34.7 %collective-permute-start.30 = (bf16[2,144,1920]{2,1,0:T(8,128)(2,1)}, bf16[2,144,1920]{2,1,0:T(8,128)(2,1)}, u32[]{:S(2)}, u32[]{:S(2)}) collective-permute-start(bf16[2,144,1920]{2,1,0:T(8,128)(2,1)} %get-tuple-element.139.refs_1_), channel_id=1, source_target_pairs={{0,8},{4,12},{8,0},{12,4},{16,24},{20,28},{24,16},{28,20},{1,9},{5... | collective-permute-start | bytes 3317768 | tf_op jit(solution)/shard_map/ppermute | solution.py:99
  606.4 43.3 %collective-permute-start.25 = (bf16[256,2304]{1,0:T(8,128)(2,1)}, bf16[256,2304]{1,0:T(8,128)(2,1)}, u32[]{:S(2)}, u32[]{:S(2)}) collective-permute-start(bf16[256,2304]{1,0:T(8,128)(2,1)} %get-tuple-element.141.refs_0_), channel_id=1, source_target_pairs={{0,1},{1,2},{2,3},{3,0},{4,5},{5,6},{6,7},{7,4},{8,9},{9,10},{10,1... | collective-permute-start | bytes 3538952 | tf_op jit(solution)/shard_map/ppermute | solution.py:56
  666.6 54.3 %collective-permute-start.38 = (bf16[144,1920]{1,0:T(8,128)(2,1)}, bf16[144,1920]{1,0:T(8,128)(2,1)}, u32[]{:S(2)}, u32[]{:S(2)}) collective-permute-start(bf16[144,1920]{1,0:T(8,128)(2,1)} %get-tuple-element.151.refs_2_), channel_id=1, source_target_pairs={{0,16},{4,20},{8,24},{12,28},{16,0},{20,4},{24,8},{28,12},{1,17},{... | collective-permute-start | bytes 1658888 | tf_op jit(solution)/shard_map/ppermute | solution.py:99
  678.5 42.4 %collective-permute-start.37 = (bf16[144,1920]{1,0:T(8,128)(2,1)}, bf16[144,1920]{1,0:T(8,128)(2,1)}, u32[]{:S(2)}, u32[]{:S(2)}) collective-permute-start(bf16[144,1920]{1,0:T(8,128)(2,1)} %get-tuple-element.149.refs_1_), channel_id=1, source_target_pairs={{0,8},{4,12},{8,0},{12,4},{16,24},{20,28},{24,16},{28,20},{1,9},{5... | collective-permute-start | bytes 1658888 | tf_op jit(solution)/shard_map/ppermute | solution.py:99
  695.5 31.9 %collective-permute-start.34 = (bf16[288,640]{1,0:T(8,128)(2,1)}, bf16[288,640]{1,0:T(8,128)(2,1)S(1)}, u32[]{:S(2)}, u32[]{:S(2)}) collective-permute-start(bf16[288,640]{1,0:T(8,128)(2,1)} %get-tuple-element.156), channel_id=1, source_target_pairs={{0,3},{1,0},{2,1},{3,2},{4,7},{5,4},{6,5},{7,6},{8,11},{9,8},{10,9... | collective-permute-start | bytes 1105928 | tf_op jit(solution)/shard_map/ppermute | solution.py:80
  695.6 31.8 %collective-permute-start.35 = (bf16[288,640]{1,0:T(8,128)(2,1)}, bf16[288,640]{1,0:T(8,128)(2,1)S(1)}, u32[]{:S(2)}, u32[]{:S(2)}) collective-permute-start(bf16[288,640]{1,0:T(8,128)(2,1)} %get-tuple-element.157), channel_id=1, source_target_pairs={{0,2},{1,3},{2,0},{3,1},{4,6},{5,7},{6,4},{7,5},{8,10},{9,11},{10,... | collective-permute-start | bytes 1105928 | tf_op jit(solution)/shard_map/ppermute | solution.py:80
  (54 other events, 625.1 us)
Sparse Core Ops, SparseCore 0:
  10.5 59.0 all-gather.4
  72.0 78.7 all-gather.6
  177.7 68.2 all-gather.8
  247.8 48.8 all-gather.10
  459.7 35.1 reduce-scatter.4
  497.0 75.5 reduce-scatter.2

commit v4 on v3

--- a/solution.py
+++ b/solution.py
@@ -80,18 +80,13 @@
     return lax.ppermute(value, "mp", [(i, (i - count) % n) for i in range(n)])
 
 
-def sum_all(value):
-    for axis in ("dp", "mp"):
-        n = lax.axis_size(axis)
-        bit = 1
-        while bit < n:
-            value = value + lax.ppermute(value, axis, [(i, i ^ bit) for i in range(n)])
-            bit *= 2
+def sum_over(value, axis):
+    n = lax.axis_size(axis)
+    bit = 1
+    while bit < n:
+        value = value + lax.ppermute(value, axis, [(i, i ^ bit) for i in range(n)])
+        bit *= 2
     return value
-
-
-def after(value, *others):
-    return lax.optimization_barrier((value, others))[0]
 
 
 def swap(value, bit):
@@ -335,9 +330,9 @@
 AROUND = (0, 1, 3, 2)
 
 
-def put_split(ref, value, core, chips=(0, 1, 2, 3)):
+def put_split(ref, value, core, chips=(0, 1, 2, 3), rows=slice(None)):
     if ref.shape[0] == 1:
-        ref[0] = value
+        ref[0, rows, :] = value
         return
     block = value.shape[1] // 8
     for which in (0, 1):
@@ -347,7 +342,7 @@
             for side in (0, 1):
                 for spot, chip in enumerate(chips):
                     start = (2 * chip + (which ^ side)) * block
-                    ref[side, :, spot * block : (spot + 1) * block] = value[
+                    ref[side, rows, spot * block : (spot + 1) * block] = value[
                         :, start : start + block
                     ]
 
@@ -356,18 +351,19 @@
     return (2, rows, width // 2) if paired() else (1, rows, width)
 
 
-def project_kernel(fresh, where_ref, x_ref, gain_ref, w_ref, cos_ref, sin_ref, *refs):
-    qkv_ref, norm_ref, copy_ref, mark_ref, held = refs[-5:]
-    mark_ref[...] = jnp.zeros_like(mark_ref)
+def normed_of(value, gain):
+    value = value.astype(F32)
+    factor = lax.rsqrt(jnp.mean(value * value, axis=-1, keepdims=True) + EPSILON)
+    return (value * factor * gain).astype(BF16)
+
+
+def project_kernel(where_ref, x_ref, gain_ref, w_ref, cos_ref, sin_ref, *refs):
+    qkv_ref, mark_ref, held = refs[-3:]
 
     @pl.when(pl.program_id(0) == 0)
     def _():
-        value = x_ref[...].astype(F32)
-        factor = lax.rsqrt(jnp.mean(value * value, axis=-1, keepdims=True) + EPSILON)
-        normed = (value * factor * gain_ref[...]).astype(BF16)
-        held[...] = normed
-        put_split(norm_ref, normed, where_ref[1])
-        copy_ref[...] = x_ref[...]
+        mark_ref[...] = jnp.zeros_like(mark_ref)
+        held[...] = normed_of(x_ref[...], gain_ref[...])
 
     product = matmul(held[...], w_ref[...])
     cosine, sine = cos_ref[...], sin_ref[...]
@@ -383,13 +379,6 @@
     rows, width = piece.shape
     columns = weights.shape[1]
     block = 3 * LANES
-    fresh = held is None
-    outs = (
-        jax.ShapeDtypeStruct((LEN, columns), BF16),
-        jax.ShapeDtypeStruct(split_shape(LEN, width), BF16),
-        jax.ShapeDtypeStruct((LEN, width), BF16),
-        jax.ShapeDtypeStruct((8, LANES), F32),
-    )
     specs = [
         pl.BlockSpec((rows, width), lambda i, w: (0, 0)),
         pl.BlockSpec((1, width), lambda i, w: (0, 0)),
@@ -399,31 +388,60 @@
     ]
     args = [piece, gain, weights, *tables]
     aliases = {}
-    if not fresh:
-        for index, array in enumerate(held):
-            aliases[1 + len(args)] = index
-            args.append(array)
-            specs.append(pl.BlockSpec(memory_space=pl.ANY))
-    return pl.pallas_call(
-        functools.partial(project_kernel, fresh),
-        out_shape=outs,
+    if held is not None:
+        aliases[1 + len(args)] = 0
+        args.append(held)
+        specs.append(pl.BlockSpec(memory_space=pl.ANY))
+    return pl.pallas_call(
+        project_kernel,
+        out_shape=(
+            jax.ShapeDtypeStruct((LEN, columns), BF16),
+            jax.ShapeDtypeStruct((8, LANES), F32),
+        ),
         grid_spec=pltpu.PrefetchScalarGridSpec(
             num_scalar_prefetch=1,
             grid=(columns // block,),
             in_specs=specs,
             out_specs=(
                 pl.BlockSpec((rows, block), lambda i, w: (w[0], i)),
-                pl.BlockSpec(split_shape(rows, width), lambda i, w: (0, w[0], 0)),
-                pl.BlockSpec((rows, width), lambda i, w: (w[0], 0)),
                 pl.BlockSpec((8, LANES), lambda i, w: (0, 0)),
             ),
             scratch_shapes=[pltpu.VMEM((rows, width), BF16)],
         ),
         input_output_aliases=aliases,
         compiler_params=params(),
-        cost_estimate=cost(11),
+        cost_estimate=cost(9),
         name="project",
     )(where, *args)
+
+
+def lay_tokens_kernel(count, place_ref, gain_ref, *refs):
+    norm_ref, copy_ref = refs[-2:]
+    rows = refs[0].shape[0]
+    for k in range(count):
+        start = pl.multiple_of(lax.rem(place_ref[0] + count - k, count) * rows, rows)
+        here = pl.ds(start, rows)
+        copy_ref[here, :] = refs[k][...]
+        put_split(norm_ref, normed_of(refs[k][...], gain_ref[...]), place_ref[1], rows=here)
+
+
+def lay_tokens(place, pieces, gain, waits):
+    rows, width = pieces[0].shape
+    count = len(pieces)
+    whole = pl.BlockSpec(memory_space=pltpu.VMEM)
+    return pl.pallas_call(
+        functools.partial(lay_tokens_kernel, count),
+        out_shape=(
+            jax.ShapeDtypeStruct(split_shape(count * rows, width), BF16),
+            jax.ShapeDtypeStruct((count * rows, width), BF16),
+        ),
+        in_specs=[pl.BlockSpec(memory_space=pltpu.SMEM)] + [whole] * (1 + count)
+        + after_all(waits),
+        out_specs=(whole, whole),
+        compiler_params=params(),
+        cost_estimate=cost(10),
+        name="lay_tokens",
+    )(place, gain, *pieces, *waits)
 
 
 PARTS = (
@@ -1128,22 +1146,26 @@
     ff_pack = pack([w_gate, w_up], FF_BLOCK, padded_ff, attn_pack)
     gate_up = dp_gather(ff_pack)
     token_pieces = ring_gather(tokens)
-    held = None
+    qkv = None
     for k in range(mp - 1):
-        *held, mark = project(
-            at[k], token_pieces[k], attn_gain[None], attn_weights, tables, held
+        qkv, mark = project(
+            at[k], token_pieces[k], attn_gain[None], attn_weights, tables, qkv
         )
-    out_own = pack([w_out.T], LANES, padded_heads, token_pieces[-1], mark, ff_pack)
+    out_own = gate(
+        pack([w_out.T], LANES, padded_heads, ff_pack), token_pieces[-1], mark
+    )
     out_pieces = [out_own] + [shift_back(out_own, mp - j) for j in range(1, mp)]
-    *held, _ = project(
-        at[mp - 1], token_pieces[-1], attn_gain[None], attn_weights, tables, held
-    )
-    qkv, normed_one, whole_tokens = held
+    qkv, _ = project(
+        at[mp - 1], token_pieces[-1], attn_gain[None], attn_weights, tables, qkv
+    )
     attended, attended_send, log_total = attend(qkv, prefix, heads)
     out_pack = chain(out_pieces, attended)
     attended_pieces = [attended, ring_up(gate(attended_send, out_pack))]
     out_weights = dp_gather(gate(out_pack, attended_pieces[1], gate_up))
-    down_pack = pack([w_down.T], LANES, padded_ff, attended_pieces[1])
+    normed_one, whole_tokens = lay_tokens(
+        at[0], token_pieces, attn_gain[None], (attended_pieces[1],)
+    )
+    down_pack = pack([w_down.T], LANES, padded_ff, whole_tokens)
     down = dp_gather(down_pack)
     while len(attended_pieces) < mp:
         attended_pieces.append(ring_up(attended_pieces[-1]))
@@ -1173,8 +1195,8 @@
     held, term_three = back_of(3, held)
     total = join(term, arrived, (term_three,))
     arrived = ring_up(total)
-    (grad_both, grad_mlp), term_own = back_of(mp, held, F32, (total,))
     attended_own = own_rows(at[0], attended_pieces, rows)
+    (grad_both, grad_mlp), term_own = back_of(mp, held, F32, (total, attended_own))
     if by_chip:
         down_other = scatter_other(grad_mlp, hidden, 768, 6)
         total = join(term_three, arrived, (down_other,))
@@ -1183,11 +1205,11 @@
         down_chip = scatter_mine(
             grad_mlp, hidden, 768, 6, swap(gate(down_other, total), 1), (ff_other,)
         )
-        waits = (down_chip, ff_other, attended_own)
+        waits = (down_chip, ff_other)
     else:
         total = join(term_three, arrived)
         arrived = ring_up(total)
-        waits = (attended_own,)
+        waits = ()
     grad_middle, grad_attn, split_attn, gain_two, zero = own_back(
         core[None], term_own, arrived, middle, out_grad, mlp_gain[None], waits
     )
@@ -1258,7 +1280,7 @@
         mlp_arrived = ring_up(mlp_total)
         attn_half = scatter_halves(chip, attn_parts, attn_moved, (mlp_total,))
         attn_share = scatter_second(attn_half)
-        waits = (mlp_total, attn_half[0][1], attn_half[1][1])
+        waits = (attn_half[0][1], attn_half[1][1])
     else:
         out_share = scatter_plain(split_attn, attended_own)
         attn_share = scatter_plain(normed_one, back)
@@ -1270,20 +1292,22 @@
         mlp_arrived = ring_up(join(mlp_chunk(3, zero), mlp_arrived))
         term = grad_one_term(4)
         waits = ()
+    out_total, *out_mine = out_sum(out_share, mp, padded_heads)
     input_grad, gain_one, zero = finish_input(
-        term, arrived, tokens, grad_middle, attn_gain[None], waits
-    )
-    out_total, *out_mine = out_sum(out_share, mp, padded_heads, (mlp_arrived,))
+        term, arrived, tokens, grad_middle, attn_gain[None],
+        (*waits, mlp_arrived, *out_mine),
+    )
     out_moved = [shift_back(out_mine[k - 1], k) for k in range(1, mp)]
-    gains = sum_all(jnp.concatenate([gain_one, gain_two]))
+    gains = sum_over(jnp.concatenate([gain_one, gain_two]), "dp")
     chunk = mlp_chunk(4, zero)
     grad_w_query, grad_w_key, grad_w_value = unmix(attn_share, 3, LANES, width_heads)
     grad_w_gate, grad_w_up = unmix(ff_share, 2, FF_BLOCK, width_ff)
     (grad_w_down,) = unmix(down_share, 1, LANES, width_ff)
-    grad_w_out = out_final(
-        out_total, out_moved, width_heads, (grad_w_gate, grad_w_down, grad_w_query)
-    )
-    block_out = finish_block(middle, chunk, mlp_arrived, (grad_w_out,))
+    block_out = finish_block(middle, chunk, mlp_arrived)
+    gains = sum_over(
+        gate(gains, *out_moved, grad_w_query, grad_w_gate, grad_w_down, block_out), "mp"
+    )
+    grad_w_out = out_final(out_total, out_moved, width_heads, (block_out,))
     return (
         block_out,
         input_grad,

time: 754 us -> 735 us (0.975)
  waiting for transfers between devices: 236 us -> 208 us
    ppermute x5, waiting for transfers between devices: 26.7 us -> 8.12 us  [sum_over(): value = value + lax.ppermute(value, axis, [(i, i ^ bit) for i in range(n)])]
    pallas_call x4 -> x5, Pallas kernels: 44.5 us -> 50.1 us  [the longest x4 39.9 us: project(): pl.pallas_call(project_kernel, out_shape=(jax.ShapeDtypeStruct((LEN, colu...]
    unnamed x73 -> x83, local copies, waits for them, and re-layouts: 16.8 us -> 18.3 us
  transfers between devices with their start and end apart: 50 -> 50, of which waited for: 19 -> 17; matrix products, arithmetic and copies ran while one was open for 9% -> 9% of each run, Pallas kernels for 46% -> 49%
where the time goes in v4:
time: 735 us; the launch traced here: 725 us
  Pallas kernels  373 us (51%)
  waiting for transfers between devices  208 us (28%)
  matrix products  57.9 us (8%)
  starting transfers between devices  42.1 us (6%)
  local copies, waits for them, and re-layouts  20.1 us (3%)
  between operations  19.1 us (3%)
    ppermute x18, waiting for transfers between devices, ring_up(): return lax.ppermute(value, 'mp', [(i, (i + 1) % n) for i in range(n)])  184 us
    pallas_call x4, Pallas kernels, feed_back(): pl.pallas_call(feed_back_kernel, out_shape=(jax.ShapeDtypeStruct((LEN, 2...  63.3 us
    dot_general x8, matrix products, outer_cols(): lax.dot_general(left, right, (((1,), (1,)), ((), ())), preferred_element_...  57.9 us
    pallas_call x6, Pallas kernels, weight_grad(): pl.pallas_call(functools.partial(weight_kernel, arrived is not None), out...  54.9 us
    pallas_call x4, Pallas kernels, project(): pl.pallas_call(project_kernel, out_shape=(jax.ShapeDtypeStruct((LEN, colu...  39.9 us
    pallas_call x1, Pallas kernels, finish_middle(): pl.pallas_call(functools.partial(middle_kernel, count), out_shape=(jax.Sh...  29.1 us
    pallas_call x1, Pallas kernels, attend_back(): pl.pallas_call(functools.partial(attend_back_kernel, heads, count), out_s...  28.6 us
    pallas_call x1, Pallas kernels, feed(): pl.pallas_call(gate_kernel, out_shape=(jax.ShapeDtypeStruct((LEN, hidden)...  21.3 us
  transfers between devices with their start and end apart: 50, of which 17 were waited for; matrix products, arithmetic and copies ran while one was open for 9% of the time, Pallas kernels for 49%

profile of v4, /device:TPU:0, one launch (start us, length us, event | category | flops | bytes accessed | tf_op | source)
XLA Modules:
  0.0 725.3 jit_solution(13521328586697267729)
XLA Ops:
  17.1 26.7 %collective-permute-done.x_ref.refs_1_ = bf16[256,2304]{1,0:T(8,128)(2,1)S(1)} collective-permute-done((bf16[256,2304]{1,0:T(8,128)(2,1)S(1)}, bf16[256,2304]{1,0:T(8,128)(2,1)S(1)}, u32[]{:S(2)}, u32[]{:S(2)}) %collective-permute-start) | collective-permute-done | bytes 1179680 | tf_op jit(solution)/shard_map/ppermute | solution.py:56
  47.6 25.2 %collective-permute-done.1.x_ref.refs_2_ = bf16[256,2304]{1,0:T(8,128)(2,1)S(1)} collective-permute-done((bf16[256,2304]{1,0:T(8,128)(2,1)S(1)}, bf16[256,2304]{1,0:T(8,128)(2,1)S(1)}, u32[]{:S(2)}, u32[]{:S(2)}) %collective-permute-start.1) | collective-permute-done | bytes 1179680 | tf_op jit(solution)/shard_map/ppermute | solution.py:56
  72.8 10.0 %project.4 = (bf16[1024,1920]{1,0:T(8,128)(2,1)}, f32[8,128]{1,0:T(8,128)}) custom-call(s32[2]{0:T(128)} %get-tuple-element.159.where_ref.place_ref, bf16[256,2304]{1,0:T(8,128)(2,1)} %x_ref.3, f32[1,2304]{1,0:T(1,128)} %broadcast_in_dim.4.gain_ref, bf16[2304,1920]{1,0:T(8,128)(2,1)} %all-gather.5.cloned.1.call-done.w_ref, ...), custom_call_target="tpu_custom_call" | custom-call | flops 27000000512 | tf_op jit(solution)/shard_map/project/pallas_call | solution.py:395
  82.8 9.6 %project.5 = (bf16[1024,1920]{1,0:T(8,128)(2,1)}, f32[8,128]{1,0:T(8,128)}) custom-call(s32[2]{0:T(128)} %pad_add_fusion.3.where_ref, bf16[256,2304]{1,0:T(8,128)(2,1)} %copy-done.11, f32[1,2304]{1,0:T(1,128)} %broadcast_in_dim.4.gain_ref, bf16[2304,1920]{1,0:T(8,128)(2,1)} %all-gather.5.cloned.1.call-done.w_ref, ...), custom_call_target="tpu_custom_call", output_to_operand_aliasing={{0}: (6, {})} | custom-call | flops 27000000512 | tf_op jit(solution)/shard_map/project/pallas_call | solution.py:395
  92.5 9.6 %project.6 = (bf16[1024,1920]{1,0:T(8,128)(2,1)}, f32[8,128]{1,0:T(8,128)}) custom-call(s32[2]{0:T(128)} %pad_add_fusion.2.where_ref, bf16[256,2304]{1,0:T(8,128)(2,1)} %copy-done.13, f32[1,2304]{1,0:T(1,128)} %broadcast_in_dim.4.gain_ref, bf16[2304,1920]{1,0:T(8,128)(2,1)} %all-gather.5.cloned.1.call-done.w_ref, ...), custom_call_target="tpu_custom_call", output_to_operand_aliasing={{0}: (6, {})} | custom-call | flops 27000000512 | tf_op jit(solution)/shard_map/project/pallas_call | solution.py:395
  107.5 10.6 %project.7 = (bf16[1024,1920]{1,0:T(8,128)(2,1)}, f32[8,128]{1,0:T(8,128)}) custom-call(s32[2]{0:T(128)} %get-tuple-element.160.where_ref, bf16[256,2304]{1,0:T(8,128)(2,1)} %copy-done.14, f32[1,2304]{1,0:T(1,128)} %broadcast_in_dim.4.gain_ref, bf16[2304,1920]{1,0:T(8,128)(2,1)} %all-gather.5.cloned.1.call-done.w_ref, ...), custom_call_target="tpu_custom_call", output_to_operand_aliasing={{0}: (6, {})} | custom-call | flops 27000000512 | tf_op jit(solution)/shard_map/project/pallas_call | solution.py:395
  118.1 18.1 %attend.1 = (bf16[1024,640]{1,0:T(8,128)(2,1)}, bf16[1024,640]{1,0:T(8,128)(2,1)}, f32[5,2,1024]{2,1,0:T(2,128)}) custom-call(s32[1]{0:T(128)S(6)} %copy.61.prefix_ref, bf16[1024,1920]{1,0:T(8,128)(2,1)} %get-tuple-element.87.qkv_ref), custom_call_target="tpu_custom_call" | custom-call | flops 54000001024 | tf_op jit(solution)/shard_map/attend/pallas_call | solution.py:509
  142.4 27.8 %collective-permute-done.6.refs_1_.refs_4_ = bf16[1024,640]{1,0:T(8,128)(2,1)S(1)} collective-permute-done((bf16[1024,640]{1,0:T(8,128)(2,1)}, bf16[1024,640]{1,0:T(8,128)(2,1)S(1)}, u32[]{:S(2)}, u32[]{:S(2)}) %collective-permute-start.6) | collective-permute-done | bytes 1310752 | tf_op jit(solution)/shard_map/ppermute | solution.py:56
  173.1 28.1 %collective-permute-done.7.refs_2_ = bf16[1024,640]{1,0:T(8,128)(2,1)S(1)} collective-permute-done((bf16[1024,640]{1,0:T(8,128)(2,1)}, bf16[1024,640]{1,0:T(8,128)(2,1)S(1)}, u32[]{:S(2)}, u32[]{:S(2)}) %collective-permute-start.7) | collective-permute-done | bytes 1310752 | tf_op jit(solution)/shard_map/ppermute | solution.py:56
  201.6 10.2 %lay_tokens.1 = (bf16[2,1024,1152]{2,1,0:T(8,128)(2,1)}, bf16[1024,2304]{1,0:T(8,128)(2,1)}) custom-call(s32[2]{0:T(128)} %get-tuple-element.159.where_ref.place_ref, f32[1,2304]{1,0:T(1,128)} %broadcast_in_dim.4.gain_ref, bf16[256,2304]{1,0:T(8,128)(2,1)} %x_ref.3, bf16[256,2304]{1,0:T(8,128)(2,1)} %copy-done.11, bf16[256,2304]{1,0:T(8,128)(2,1)} %copy-done.13, ...), custom_call_target="tpu_custom_call" | custom-call | flops 30000001024 | tf_op jit(solution)/shard_map/lay_tokens/pallas_call | solution.py:432
  214.0 15.8 %collective-permute-done.8.refs_3_.refs_0_ = bf16[1024,640]{1,0:T(8,128)(2,1)} collective-permute-done((bf16[1024,640]{1,0:T(8,128)(2,1)S(1)}, bf16[1024,640]{1,0:T(8,128)(2,1)}, u32[]{:S(2)}, u32[]{:S(2)}) %collective-permute-start.8) | collective-permute-done | bytes 1310752 | tf_op jit(solution)/shard_map/ppermute | solution.py:56
  243.9 29.1 %finish_middle.1 = (bf16[1024,2304]{1,0:T(8,128)(2,1)}, bf16[2,1024,1152]{2,1,0:T(8,128)(2,1)}, f32[256,2304]{1,0:T(8,128)}) custom-call(s32[2]{0:T(128)} %get-tuple-element.159.where_ref.place_ref, bf16[1024,640]{1,0:T(8,128)(2,1)} %get-tuple-element.88.refs_4_.refs_0_.out_ref, bf16[1024,640]{1,0:T(8,128)(2,1)} %copy-done, bf16[1024,640]{1,0:T(8,128)(2,1)} %copy-done.9, ...), custom_call_target="tpu_custom_call" | custom-call | flops 65999998976 | tf_op jit(solution)/shard_map/finish_middle/pallas_call | solution.py:650
  276.0 21.3 %feed.1 = (bf16[1024,1536]{1,0:T(8,128)(2,1)}, bf16[1024,3072]{1,0:T(8,128)(2,1)}) custom-call(bf16[1024,2304]{1,0:T(8,128)(2,1)} %get-tuple-element.93.normed_ref.refs_1_, bf16[2304,3072]{1,0:T(8,128)(2,1)} %all-gather.7.cloned.1.call-done.refs_2_.weight_ref), custom_call_target="tpu_custom_call" | custom-call | flops 62999998464 | tf_op jit(solution)/shard_map/feed/pallas_call | solution.py:694
  305.4 15.7 %feed_back.4 = (bf16[1024,3072]{1,0:T(8,128)(2,1)}, bf16[2,1024,1152]{2,1,0:T(8,128)(2,1)}, bf16[256,2304]{1,0:T(8,128)(2,1)}) custom-call(s32[2]{0:T(128)} %pad_add_fusion.3.where_ref, bf16[256,2304]{1,0:T(8,128)(2,1)} %copy-done.1, bf16[1024,3072]{1,0:T(8,128)(2,1)} %get-tuple-element.95.slope_ref, ...), custom_call_target="tpu_custom_call" | custom-call | flops 44999999488 | tf_op jit(solution)/shard_map/feed_back/pallas_call | solution.py:753
  321.5 13.7 %collective-permute-done.11.refs_2_.grad_ref = bf16[256,2304]{1,0:T(8,128)(2,1)S(1)} collective-permute-done((bf16[256,2304]{1,0:T(8,128)(2,1)S(1)}, bf16[256,2304]{1,0:T(8,128)(2,1)S(1)}, u32[]{:S(2)}, u32[]{:S(2)}) %collective-permute-start.11) | collective-permute-done | bytes 1179680 | tf_op jit(solution)/shard_map/ppermute | solution.py:56
  336.1 15.7 %feed_back.5 = (bf16[1024,3072]{1,0:T(8,128)(2,1)}, bf16[2,1024,1152]{2,1,0:T(8,128)(2,1)}, bf16[256,2304]{1,0:T(8,128)(2,1)}) custom-call(s32[2]{0:T(128)} %pad_add_fusion.2.where_ref, bf16[256,2304]{1,0:T(8,128)(2,1)} %copy-done.17, bf16[1024,3072]{1,0:T(8,128)(2,1)} %get-tuple-element.95.slope_ref, ...), custom_call_target="tpu_custom_call", output_to_operand_aliasing={{0}: (5, {}), {1}: (6, {})} | custom-call | flops 44999999488 | tf_op jit(solution)/shard_map/feed_back/pallas_call | solution.py:753
  351.8 15.7 %feed_back.6 = (bf16[1024,3072]{1,0:T(8,128)(2,1)}, bf16[2,1024,1152]{2,1,0:T(8,128)(2,1)}, bf16[256,2304]{1,0:T(8,128)(2,1)}) custom-call(s32[2]{0:T(128)} %get-tuple-element.160.where_ref, bf16[256,2304]{1,0:T(8,128)(2,1)} %copy-done.18, bf16[1024,3072]{1,0:T(8,128)(2,1)} %get-tuple-element.95.slope_ref, ...), custom_call_target="tpu_custom_call", output_to_operand_aliasing={{0}: (5, {}), {1}: (6, {})} | custom-call | flops 44999999488 | tf_op jit(solution)/shard_map/feed_back/pallas_call | solution.py:753
  371.6 16.2 %feed_back.7 = (bf16[1024,3072]{1,0:T(8,128)(2,1)}, bf16[2,1024,1152]{2,1,0:T(8,128)(2,1)}, f32[256,2304]{1,0:T(8,128)}) custom-call(s32[2]{0:T(128)} %get-tuple-element.159.where_ref.place_ref, bf16[256,2304]{1,0:T(8,128)(2,1)} %scaled.1.grad_ref, bf16[1024,3072]{1,0:T(8,128)(2,1)} %get-tuple-element.95.slope_ref, ...), custom_call_target="tpu_custom_call", output_to_operand_aliasing={{0}: (5, {}), {1}: (6, {})} | custom-call | flops 44999999488 | tf_op jit(solution)/shard_map/feed_back/pallas_call | solution.py:753
  387.8 7.6 %weight_grad.6.refs_0_ = bf16[1152,1536]{1,0:T(8,128)(2,1)} custom-call(bf16[2,1024,1152]{2,1,0:T(8,128)(2,1)} %get-tuple-element.107.left_ref, bf16[1024,1536]{1,0:T(8,128)(2,1)} %get-tuple-element.94.right_ref), custom_call_target="tpu_custom_call" | custom-call | flops 17999998976 | tf_op jit(solution)/shard_map/weight_grad/pallas_call | solution.py:142
  402.9 11.8 %weight_grad.7.refs_1_.refs_0_ = bf16[1152,3072]{1,0:T(8,128)(2,1)} custom-call(bf16[2,1024,1152]{2,1,0:T(8,128)(2,1)} %get-tuple-element.109.left_ref, bf16[1024,3072]{1,0:T(8,128)(2,1)} %get-tuple-element.110.right_ref, bf16[256,2304]{1,0:T(8,128)(2,1)} %get-tuple-element.108.refs_1_.refs_0_), custom_call_target="tpu_custom_call" | custom-call | flops 32999999488 | tf_op jit(solution)/shard_map/weight_grad/pallas_call | solution.py:142
  416.6 8.1 %weight_grad.8.refs_0_ = bf16[1152,1536]{1,0:T(8,128)(2,1)} custom-call(bf16[2,1024,1152]{2,1,0:T(8,128)(2,1)} %get-tuple-element.107.left_ref, bf16[1024,1536]{1,0:T(8,128)(2,1)} %get-tuple-element.94.right_ref, bf16[1152,1536]{1,0:T(8,128)(2,1)} %copy-done.6, bf16[1152,3072]{1,0:T(8,128)(2,1)} %weight_grad.7.refs_1_.refs_0_), custom_call_target="tpu_custom_call" | custom-call | flops 17999998976 | tf_op jit(solution)/shard_map/weight_grad/pallas_call | solution.py:142
  439.4 8.8 %spread.1 = (bf16[256,640]{1,0:T(8,128)(2,1)}, bf16[256,640]{1,0:T(8,128)(2,1)}, bf16[256,640]{1,0:T(8,128)(2,1)}, bf16[256,640]{1,0:T(8,128)(2,1)}, s32[1]{0:T(128)}) custom-call(bf16[256,2304]{1,0:T(8,128)(2,1)} %get-tuple-element.111.value_ref, bf16[2304,2560]{1,0:T(8,128)(2,1)} %all-gather.9.cloned.1.call-done.refs_4_.refs_2_.weight_ref), custom_call_target="tpu_custom_call" | custom-call | flops 24000000000 | tf_op jit(solution)/shard_map/spread/pallas_call | solution.py:838
  464.4 13.1 %weight_grad.9.refs_7_ = bf16[1152,3072]{1,0:T(8,128)(2,1)} custom-call(bf16[2,1024,1152]{2,1,0:T(8,128)(2,1)} %get-tuple-element.109.left_ref, bf16[1024,3072]{1,0:T(8,128)(2,1)} %get-tuple-element.110.right_ref, bf16[1152,3072]{1,0:T(8,128)(2,1)} %collective-permute-done.19.refs_0_, bf16[256,2304]{1,0:T(8,128)(2,1)} %fusion.14.refs_1_.refs_0_), custom_call_target="tpu_custom_call" | custom-call | flops 32999999488 | tf_op jit(solution)/shard_map/weight_grad/pallas_call | solution.py:142
  482.3 28.6 %attend_back.1.right_ref = bf16[1024,1920]{1,0:T(8,128)(2,1)} custom-call(s32[2]{0:T(128)} %pad_add_fusion.4.prefix_ref, bf16[1024,1920]{1,0:T(8,128)(2,1)} %get-tuple-element.87.qkv_ref, bf16[1024,640]{1,0:T(8,128)(2,1)} %get-tuple-element.88.refs_4_.refs_0_.out_ref, bf16[256,640]{1,0:T(8,128)(2,1)} %get-tuple-element.112.refs_0_, ...), custom_call_target="tpu_custom_call" | custom-call | flops 83999997952 | tf_op jit(solution)/shard_map/attend_back/pallas_call | solution.py:593
  510.9 7.5 %fusion.6.refs_0_ = bf16[256,2304]{1,0:T(8,128)(2,1)} fusion(bf16[2304,1920]{1,0:T(8,128)(2,1)} %all-gather.5.cloned.1.call-done.w_ref, bf16[1024,1920]{1,0:T(8,128)(2,1)} %attend_back.1.right_ref, s32[]{:T(128)S(6)} %select_n.63), kind=kOutput, calls=%fused_computation.6 | convolution fusion | flops 2264924160 | bytes 11010052 | tf_op jit(solution)/shard_map/dot_general | solution.py:39
  521.9 9.4 %weight_grad.11.refs_1_.refs_0_ = bf16[1152,1920]{1,0:T(8,128)(2,1)} custom-call(bf16[2,1024,1152]{2,1,0:T(8,128)(2,1)} %get-tuple-element.119.left_ref, bf16[1024,1920]{1,0:T(8,128)(2,1)} %attend_back.1.right_ref, bf16[256,2304]{1,0:T(8,128)(2,1)} %fusion.6.refs_0_, bf16[256,2304]{1,0:T(8,128)(2,1)} %copy-done.15), custom_call_target="tpu_custom_call" | custom-call | flops 24000000000 | tf_op jit(solution)/shard_map/weight_grad/pallas_call | solution.py:142
  547.6 7.9 %fusion.4.one_ref = f32[256,2304]{1,0:T(8,128)} fusion(bf16[2304,1920]{1,0:T(8,128)(2,1)} %all-gather.5.cloned.1.call-done.w_ref, bf16[1024,1920]{1,0:T(8,128)(2,1)} %attend_back.1.right_ref, s32[]{:T(128)S(6)} %select_n.64), kind=kOutput, calls=%fused_computation.4 | convolution fusion | flops 2264924160 | bytes 12189700 | tf_op jit(solution)/shard_map/dot_general | solution.py:39
  564.0 10.9 %scatter_chip.3 = (bf16[2,144,1920]{2,1,0:T(8,128)(2,1)}, bf16[2,144,1920]{2,1,0:T(8,128)(2,1)}, bf16[2,144,1920]{2,1,0:T(8,128)(2,1)}, bf16[2,144,1920]{2,1,0:T(8,128)(2,1)}, s32[1]{0:T(128)}) custom-call(s32[2]{0:T(128)} %pad_add_fusion.5.where_ref, bf16[2,1024,1152]{2,1,0:T(8,128)(2,1)} %get-tuple-element.119.left_ref, ...), custom_call_target="tpu_custom_call" | custom-call | flops 30000001024 | tf_op jit(solution)/shard_map/scatter_chip/pallas_call | solution.py:185
  584.3 7.9 %fusion.2.one_ref = f32[256,2304]{1,0:T(8,128)} fusion(bf16[2304,1920]{1,0:T(8,128)(2,1)} %all-gather.5.cloned.1.call-done.w_ref, bf16[1024,1920]{1,0:T(8,128)(2,1)} %attend_back.1.right_ref, s32[]{:T(128)S(6)} %select_n.65), kind=kOutput, calls=%fused_computation.2 | convolution fusion | flops 2264924160 | bytes 12189700 | tf_op jit(solution)/shard_map/dot_general | solution.py:39
  605.6 9.5 %collective-permute-done.27.two_ref = bf16[256,2304]{1,0:T(8,128)(2,1)} collective-permute-done((bf16[256,2304]{1,0:T(8,128)(2,1)}, bf16[256,2304]{1,0:T(8,128)(2,1)}, u32[]{:S(2)}, u32[]{:S(2)}) %collective-permute-start.27) | collective-permute-done | bytes 1179680 | tf_op jit(solution)/shard_map/ppermute | solution.py:56
  620.1 8.0 %fusion.term_ref = f32[256,2304]{1,0:T(8,128)} fusion(bf16[2304,1920]{1,0:T(8,128)(2,1)} %all-gather.5.cloned.1.call-done.w_ref, bf16[1024,1920]{1,0:T(8,128)(2,1)} %attend_back.1.right_ref, s32[]{:T(128)S(6)} %select_n.66), kind=kOutput, calls=%fused_computation | convolution fusion | flops 2264924160 | bytes 12189700 | tf_op jit(solution)/shard_map/dot_general | solution.py:39
  643.9 20.5 %collective-permute-done.31.refs_2_.arrived_ref = bf16[256,2304]{1,0:T(8,128)(2,1)S(1)} collective-permute-done((bf16[256,2304]{1,0:T(8,128)(2,1)S(1)}, bf16[256,2304]{1,0:T(8,128)(2,1)S(1)}, u32[]{:S(2)}, u32[]{:S(2)}) %collective-permute-start.31) | collective-permute-done | bytes 1179680 | tf_op jit(solution)/shard_map/ppermute | solution.py:56
  (235 shorter events, 227.5 us)
Async XLA Ops:
  7.2 65.6 %all-gather.5.cloned.1.call-start = ((), (), s32[]{:S(2)}) async-start(), calls=%async_computation.2 | async-start | bytes 9953280 | tf_op jit(solution)/shard_map/all_gather | solution.py:98
  9.7 160.5 %all-gather.7.cloned.1.call-start = ((), (), s32[]{:S(2)}) async-start(), calls=%async_computation.3 | async-start | bytes 15925248 | tf_op jit(solution)/shard_map/all_gather | solution.py:98
  12.7 227.2 %all-gather.9.cloned.1.call-start = ((), (), s32[]{:S(2)}) async-start(), calls=%async_computation.4 | async-start | bytes 13271040 | tf_op jit(solution)/shard_map/all_gather | solution.py:98
  12.8 31.1 %collective-permute-start = (bf16[256,2304]{1,0:T(8,128)(2,1)S(1)}, bf16[256,2304]{1,0:T(8,128)(2,1)S(1)}, u32[]{:S(2)}, u32[]{:S(2)}) collective-permute-start(bf16[256,2304]{1,0:T(8,128)(2,1)S(1)} %copy-done.10), channel_id=1, source_target_pairs={{0,1},{1,2},{2,3},{3,0},{4,5},{5,6},{6,7},{7,4},{8,9},{9,10},{10,1... | collective-permute-start | bytes 3538952 | tf_op jit(solution)/shard_map/ppermute | solution.py:56
  72.8 29.3 %collective-permute-start.2 = (bf16[256,2304]{1,0:T(8,128)(2,1)S(1)}, bf16[256,2304]{1,0:T(8,128)(2,1)S(1)}, u32[]{:S(2)}, u32[]{:S(2)}) collective-permute-start(bf16[256,2304]{1,0:T(8,128)(2,1)S(1)} %collective-permute-done.1.x_ref.refs_2_), channel_id=1, source_target_pairs={{0,1},{1,2},{2,3},{3,0},{4,5},{5,6},{6,7},{7,4},{8,9},{9,10},{10,1... | collective-permute-start | bytes 3538952 | tf_op jit(solution)/shard_map/ppermute | solution.py:56
  103.1 33.1 %collective-permute-start.5 = (bf16[288,640]{1,0:T(8,128)(2,1)}, bf16[288,640]{1,0:T(8,128)(2,1)S(1)}, u32[]{:S(2)}, u32[]{:S(2)}) collective-permute-start(bf16[288,640]{1,0:T(8,128)(2,1)} %gate.9.refs_0_), channel_id=1, source_target_pairs={{0,3},{1,0},{2,1},{3,2},{4,7},{5,4},{6,5},{7,6},{8,11},{9,8},{10,9... | collective-permute-start | bytes 1105928 | tf_op jit(solution)/shard_map/ppermute | solution.py:80
  106.9 29.3 %collective-permute-start.4 = (bf16[288,640]{1,0:T(8,128)(2,1)}, bf16[288,640]{1,0:T(8,128)(2,1)S(1)}, u32[]{:S(2)}, u32[]{:S(2)}) collective-permute-start(bf16[288,640]{1,0:T(8,128)(2,1)} %gate.9.refs_0_), channel_id=1, source_target_pairs={{0,2},{1,3},{2,0},{3,1},{4,6},{5,7},{6,4},{7,5},{8,10},{9,11},{10,... | collective-permute-start | bytes 1105928 | tf_op jit(solution)/shard_map/ppermute | solution.py:80
  106.9 29.3 %collective-permute-start.3 = (bf16[288,640]{1,0:T(8,128)(2,1)}, bf16[288,640]{1,0:T(8,128)(2,1)S(1)}, u32[]{:S(2)}, u32[]{:S(2)}) collective-permute-start(bf16[288,640]{1,0:T(8,128)(2,1)} %gate.9.refs_0_), channel_id=1, source_target_pairs={{0,1},{1,2},{2,3},{3,0},{4,5},{5,6},{6,7},{7,4},{8,9},{9,10},{10,1... | collective-permute-start | bytes 1105928 | tf_op jit(solution)/shard_map/ppermute | solution.py:80
  139.7 30.4 %collective-permute-start.6 = (bf16[1024,640]{1,0:T(8,128)(2,1)}, bf16[1024,640]{1,0:T(8,128)(2,1)S(1)}, u32[]{:S(2)}, u32[]{:S(2)}) collective-permute-start(bf16[1024,640]{1,0:T(8,128)(2,1)} %gate.10), channel_id=1, source_target_pairs={{0,1},{1,2},{2,3},{3,0},{4,5},{5,6},{6,7},{7,4},{8,9},{9,10},{10,1... | collective-permute-start | bytes 3932168 | tf_op jit(solution)/shard_map/ppermute | solution.py:56
  171.2 133.2 %all-gather.11.cloned.1.call-start = ((), (), s32[]{:S(2)}) async-start(), calls=%async_computation.5 | async-start | bytes 7962624 | tf_op jit(solution)/shard_map/all_gather | solution.py:98
  171.3 29.8 %collective-permute-start.7 = (bf16[1024,640]{1,0:T(8,128)(2,1)}, bf16[1024,640]{1,0:T(8,128)(2,1)S(1)}, u32[]{:S(2)}, u32[]{:S(2)}) collective-permute-start(bf16[1024,640]{1,0:T(8,128)(2,1)} %copy-done), channel_id=1, source_target_pairs={{0,1},{1,2},{2,3},{3,0},{4,5},{5,6},{6,7},{7,4},{8,9},{9,10},{10,1... | collective-permute-start | bytes 3932168 | tf_op jit(solution)/shard_map/ppermute | solution.py:56
  214.0 457.6 %reduce-scatter.5.cloned.1.call-start = ((), (), s32[]{:S(2)}) async-start(), calls=%async_computation.7 | async-start | bytes 4423680 | tf_op jit(solution)/shard_map/reduce_scatter | solution.py:296
  242.4 30.6 %collective-permute-start.9 = (bf16[256,2304]{1,0:T(8,128)(2,1)}, bf16[256,2304]{1,0:T(8,128)(2,1)S(1)}, u32[]{:S(2)}, u32[]{:S(2)}) collective-permute-start(bf16[256,2304]{1,0:T(8,128)(2,1)} %scaled.1.grad_ref), channel_id=1, source_target_pairs={{0,1},{1,2},{2,3},{3,0},{4,5},{5,6},{6,7},{7,4},{8,9},{9,10},{10,1... | collective-permute-start | bytes 3538952 | tf_op jit(solution)/shard_map/ppermute | solution.py:56
  274.4 30.1 %collective-permute-start.10 = (bf16[256,2304]{1,0:T(8,128)(2,1)}, bf16[256,2304]{1,0:T(8,128)(2,1)S(1)}, u32[]{:S(2)}, u32[]{:S(2)}) collective-permute-start(bf16[256,2304]{1,0:T(8,128)(2,1)} %gate.12), channel_id=1, source_target_pairs={{0,1},{1,2},{2,3},{3,0},{4,5},{5,6},{6,7},{7,4},{8,9},{9,10},{10,1... | collective-permute-start | bytes 3538952 | tf_op jit(solution)/shard_map/ppermute | solution.py:56
  304.4 30.7 %collective-permute-start.11 = (bf16[256,2304]{1,0:T(8,128)(2,1)S(1)}, bf16[256,2304]{1,0:T(8,128)(2,1)S(1)}, u32[]{:S(2)}, u32[]{:S(2)}) collective-permute-start(bf16[256,2304]{1,0:T(8,128)(2,1)S(1)} %collective-permute-done.10.refs_0_.grad_ref), channel_id=1, source_target_pairs={{0,1},{1,2},{2,3},{3,0},{4,5},{5,6},{6,7},{7,4},{8,9},{9,10},{10,1... | collective-permute-start | bytes 3538952 | tf_op jit(solution)/shard_map/ppermute | solution.py:56
  321.2 46.4 %collective-permute-start.12 = (bf16[256,2304]{1,0:T(8,128)(2,1)}, bf16[256,2304]{1,0:T(8,128)(2,1)S(1)}, u32[]{:S(2)}, u32[]{:S(2)}) collective-permute-start(bf16[256,2304]{1,0:T(8,128)(2,1)} %get-tuple-element.103), channel_id=1, source_target_pairs={{0,1},{1,2},{2,3},{3,0},{4,5},{5,6},{6,7},{7,4},{8,9},{9,10},{10,1... | collective-permute-start | bytes 3538952 | tf_op jit(solution)/shard_map/ppermute | solution.py:56
  402.5 29.4 %collective-permute-start.14 = (bf16[256,2304]{1,0:T(8,128)(2,1)S(1)}, bf16[256,2304]{1,0:T(8,128)(2,1)S(1)}, u32[]{:S(2)}, u32[]{:S(2)}) collective-permute-start(bf16[256,2304]{1,0:T(8,128)(2,1)S(1)} %copy-done.21), channel_id=1, source_target_pairs={{0,1},{1,2},{2,3},{3,0},{4,5},{5,6},{6,7},{7,4},{8,9},{9,10},{10,1... | collective-permute-start | bytes 3538952 | tf_op jit(solution)/shard_map/ppermute | solution.py:56
  448.9 252.6 %reduce-scatter.3.cloned.1.call-start = ((), (), s32[]{:S(2)}) async-start(), calls=%async_computation.6 | async-start | bytes 8847360 | tf_op jit(solution)/shard_map/reduce_scatter | solution.py:296
  464.3 67.0 %collective-permute-start.22 = (bf16[1152,2560]{1,0:T(8,128)(2,1)}, bf16[1152,2560]{1,0:T(8,128)(2,1)}, u32[]{:S(2)}, u32[]{:S(2)}) collective-permute-start(bf16[1152,2560]{1,0:T(8,128)(2,1)} %weight_grad.10.refs_8_), channel_id=1, source_target_pairs={{0,4},{4,0},{8,12},{12,8},{16,20},{20,16},{24,28},{28,24},{1,5},{5... | collective-permute-start | bytes 17694728 | tf_op jit(solution)/shard_map/ppermute | solution.py:94
  481.4 39.4 %collective-permute-start.20 = (bf16[256,2304]{1,0:T(8,128)(2,1)}, bf16[256,2304]{1,0:T(8,128)(2,1)S(1)}, u32[]{:S(2)}, u32[]{:S(2)}) collective-permute-start(bf16[256,2304]{1,0:T(8,128)(2,1)} %gate.15), channel_id=1, source_target_pairs={{0,1},{1,2},{2,3},{3,0},{4,5},{5,6},{6,7},{7,4},{8,9},{9,10},{10,1... | collective-permute-start | bytes 3538952 | tf_op jit(solution)/shard_map/ppermute | solution.py:56
  518.4 37.1 %collective-permute-start.23 = (bf16[256,2304]{1,0:T(8,128)(2,1)}, bf16[256,2304]{1,0:T(8,128)(2,1)}, u32[]{:S(2)}, u32[]{:S(2)}) collective-permute-start(bf16[256,2304]{1,0:T(8,128)(2,1)} %fusion.6.refs_0_), channel_id=1, source_target_pairs={{0,1},{1,2},{2,3},{3,0},{4,5},{5,6},{6,7},{7,4},{8,9},{9,10},{10,1... | collective-permute-start | bytes 3538952 | tf_op jit(solution)/shard_map/ppermute | solution.py:56
  531.3 32.7 %collective-permute-start.21 = (bf16[1152,1920]{1,0:T(8,128)(2,1)}, bf16[1152,1920]{1,0:T(8,128)(2,1)}, u32[]{:S(2)}, u32[]{:S(2)}) collective-permute-start(bf16[1152,1920]{1,0:T(8,128)(2,1)} %weight_grad.11.refs_1_.refs_0_), channel_id=1, source_target_pairs={{0,4},{4,0},{8,12},{12,8},{16,20},{20,16},{24,28},{28,24},{1,5},{5... | collective-permute-start | bytes 13271048 | tf_op jit(solution)/shard_map/ppermute | solution.py:94
  538.7 61.9 %collective-permute-start.28 = (bf16[2,144,2560]{2,1,0:T(8,128)(2,1)}, bf16[2,144,2560]{2,1,0:T(8,128)(2,1)S(1)}, u32[]{:S(2)}, u32[]{:S(2)}) collective-permute-start(bf16[2,144,2560]{2,1,0:T(8,128)(2,1)} %get-tuple-element.121.refs_1_), channel_id=1, source_target_pairs={{0,16},{4,20},{8,24},{12,28},{16,0},{20,4},{24,8},{28,12},{1,17},{... | collective-permute-start | bytes 4423688 | tf_op jit(solution)/shard_map/ppermute | solution.py:94
  540.1 55.7 %collective-permute-start.29 = (bf16[2,144,2560]{2,1,0:T(8,128)(2,1)}, bf16[2,144,2560]{2,1,0:T(8,128)(2,1)S(1)}, u32[]{:S(2)}, u32[]{:S(2)}) collective-permute-start(bf16[2,144,2560]{2,1,0:T(8,128)(2,1)} %get-tuple-element.122.refs_2_), channel_id=1, source_target_pairs={{0,8},{4,12},{8,0},{12,4},{16,24},{20,28},{24,16},{28,20},{1,9},{5... | collective-permute-start | bytes 4423688 | tf_op jit(solution)/shard_map/ppermute | solution.py:94
  558.7 33.5 %collective-permute-start.24 = (bf16[256,2304]{1,0:T(8,128)(2,1)}, bf16[256,2304]{1,0:T(8,128)(2,1)}, u32[]{:S(2)}, u32[]{:S(2)}) collective-permute-start(bf16[256,2304]{1,0:T(8,128)(2,1)} %get-tuple-element.123.refs_0_), channel_id=1, source_target_pairs={{0,1},{1,2},{2,3},{3,0},{4,5},{5,6},{6,7},{7,4},{8,9},{9,10},{10,1... | collective-permute-start | bytes 3538952 | tf_op jit(solution)/shard_map/ppermute | solution.py:56
  562.1 52.9 %collective-permute-start.27 = (bf16[256,2304]{1,0:T(8,128)(2,1)}, bf16[256,2304]{1,0:T(8,128)(2,1)}, u32[]{:S(2)}, u32[]{:S(2)}) collective-permute-start(bf16[256,2304]{1,0:T(8,128)(2,1)} %get-tuple-element.124.refs_1_), channel_id=1, source_target_pairs={{0,1},{1,2},{2,3},{3,0},{4,5},{5,6},{6,7},{7,4},{8,9},{9,10},{10,1... | collective-permute-start | bytes 3538952 | tf_op jit(solution)/shard_map/ppermute | solution.py:56
  575.6 65.2 %collective-permute-start.26 = (bf16[2,144,1920]{2,1,0:T(8,128)(2,1)}, bf16[2,144,1920]{2,1,0:T(8,128)(2,1)}, u32[]{:S(2)}, u32[]{:S(2)}) collective-permute-start(bf16[2,144,1920]{2,1,0:T(8,128)(2,1)} %get-tuple-element.126.refs_0_), channel_id=1, source_target_pairs={{0,16},{4,20},{8,24},{12,28},{16,0},{20,4},{24,8},{28,12},{1,17},{... | collective-permute-start | bytes 3317768 | tf_op jit(solution)/shard_map/ppermute | solution.py:94
  592.2 45.3 %collective-permute-start.30 = (bf16[2,144,1920]{2,1,0:T(8,128)(2,1)}, bf16[2,144,1920]{2,1,0:T(8,128)(2,1)}, u32[]{:S(2)}, u32[]{:S(2)}) collective-permute-start(bf16[2,144,1920]{2,1,0:T(8,128)(2,1)} %get-tuple-element.127.refs_1_), channel_id=1, source_target_pairs={{0,8},{4,12},{8,0},{12,4},{16,24},{20,28},{24,16},{28,20},{1,9},{5... | collective-permute-start | bytes 3317768 | tf_op jit(solution)/shard_map/ppermute | solution.py:94
  595.8 68.7 %collective-permute-start.25 = (bf16[256,2304]{1,0:T(8,128)(2,1)}, bf16[256,2304]{1,0:T(8,128)(2,1)}, u32[]{:S(2)}, u32[]{:S(2)}) collective-permute-start(bf16[256,2304]{1,0:T(8,128)(2,1)} %get-tuple-element.129.refs_0_), channel_id=1, source_target_pairs={{0,1},{1,2},{2,3},{3,0},{4,5},{5,6},{6,7},{7,4},{8,9},{9,10},{10,1... | collective-permute-start | bytes 3538952 | tf_op jit(solution)/shard_map/ppermute | solution.py:56
  628.1 36.4 %collective-permute-start.31 = (bf16[256,2304]{1,0:T(8,128)(2,1)S(1)}, bf16[256,2304]{1,0:T(8,128)(2,1)S(1)}, u32[]{:S(2)}, u32[]{:S(2)}) collective-permute-start(bf16[256,2304]{1,0:T(8,128)(2,1)S(1)} %copy-done.16), channel_id=1, source_target_pairs={{0,1},{1,2},{2,3},{3,0},{4,5},{5,6},{6,7},{7,4},{8,9},{9,10},{10,1... | collective-permute-start | bytes 3538952 | tf_op jit(solution)/shard_map/ppermute | solution.py:56
  674.2 30.7 %collective-permute-start.36 = (bf16[288,640]{1,0:T(8,128)(2,1)S(1)}, bf16[288,640]{1,0:T(8,128)(2,1)}, u32[]{:S(2)}, u32[]{:S(2)}) collective-permute-start(bf16[288,640]{1,0:T(8,128)(2,1)S(1)} %copy-done.31), channel_id=1, source_target_pairs={{0,3},{1,0},{2,1},{3,2},{4,7},{5,4},{6,5},{7,6},{8,11},{9,8},{10,9... | collective-permute-start | bytes 1105928 | tf_op jit(solution)/shard_map/ppermute | solution.py:80
  674.2 30.7 %collective-permute-start.37 = (bf16[288,640]{1,0:T(8,128)(2,1)S(1)}, bf16[288,640]{1,0:T(8,128)(2,1)}, u32[]{:S(2)}, u32[]{:S(2)}) collective-permute-start(bf16[288,640]{1,0:T(8,128)(2,1)S(1)} %copy-done.30), channel_id=1, source_target_pairs={{0,2},{1,3},{2,0},{3,1},{4,6},{5,7},{6,4},{7,5},{8,10},{9,11},{10,... | collective-permute-start | bytes 1105928 | tf_op jit(solution)/shard_map/ppermute | solution.py:80
  (59 other events, 482.3 us)
Sparse Core Ops, SparseCore 0:
  10.5 59.0 all-gather.4
  72.0 78.7 all-gather.6
  171.4 68.4 all-gather.8
  241.6 48.8 all-gather.10
  449.0 35.5 reduce-scatter.4
  486.7 76.0 reduce-scatter.2

commit v5 on v4

--- a/solution.py
+++ b/solution.py
@@ -1257,26 +1257,26 @@
             chip, split_attn, attended_own, 1280, 8, out_arrived, (total, attn_other)
         )
         out_moved = scatter_first(out_parts)
-        chunk = mlp_chunk(2, zero)
         total, zero = join_marked(
-            grad_one_term(2, zero[0]), arrived,
-            (attn_other, out_parts[1], out_parts[3], chunk),
+            grad_one_term(2, zero[0]), arrived, (attn_other, out_parts[1], out_parts[3])
         )
         arrived = ring_up(total)
-        mlp_total = join(chunk, mlp_arrived, (total,))
+        mlp_total = join(mlp_chunk(2, zero), mlp_arrived, (total,))
         mlp_arrived = ring_up(mlp_total)
         attn_parts, zero = scatter_chip(
             chip, normed_one, back, 640, 10, attn_arrived, (total, mlp_total)
         )
         attn_moved = scatter_first(attn_parts)
-        term = grad_one_term(3, zero[0])
-        chunk = mlp_chunk(3, zero)
-        total, zero = join_marked(term, arrived, (attn_parts[1], attn_parts[3], chunk))
+        total, zero = join_marked(
+            grad_one_term(3, zero[0]), arrived, (attn_parts[1], attn_parts[3])
+        )
         arrived = ring_up(total)
         term = grad_one_term(4, zero[0])
         out_half = scatter_halves(chip, out_parts, out_moved, (total,))
         out_share = scatter_second(out_half)
-        mlp_total = join(chunk, mlp_arrived, (total, out_half[0][1], out_half[1][1]))
+        mlp_total = join(
+            mlp_chunk(3, zero), mlp_arrived, (total, out_half[0][1], out_half[1][1], term)
+        )
         mlp_arrived = ring_up(mlp_total)
         attn_half = scatter_halves(chip, attn_parts, attn_moved, (mlp_total,))
         attn_share = scatter_second(attn_half)

time: 735 us -> 729 us (level)
    ppermute x18, waiting for transfers between devices: 184 us -> 171 us  [ring_up(): return lax.ppermute(value, 'mp', [(i, (i + 1) % n) for i in range(n)])]
    unnamed x83 -> x87, local copies, waits for them, and re-layouts: 18.3 us -> 19.6 us
  transfers between devices with their start and end apart: 50 -> 50, of which waited for: 17 -> 17; matrix products, arithmetic and copies ran while one was open for 9% -> 9% of each run, Pallas kernels for 49% -> 50%
where the time goes in v5:
time: 729 us; the launch traced here: 719 us
  Pallas kernels  373 us (51%)
  waiting for transfers between devices  201 us (28%)
  matrix products  54.9 us (8%)
  starting transfers between devices  43.4 us (6%)
  local copies, waits for them, and re-layouts  21.4 us (3%)
  between operations  20.4 us (3%)
    ppermute x18, waiting for transfers between devices, ring_up(): return lax.ppermute(value, 'mp', [(i, (i + 1) % n) for i in range(n)])  171 us
    pallas_call x4, Pallas kernels, feed_back(): pl.pallas_call(feed_back_kernel, out_shape=(jax.ShapeDtypeStruct((LEN, 2...  63.3 us
    pallas_call x6, Pallas kernels, weight_grad(): pl.pallas_call(functools.partial(weight_kernel, arrived is not None), out...  55.3 us
    dot_general x8, matrix products, outer_cols(): lax.dot_general(left, right, (((1,), (1,)), ((), ())), preferred_element_...  54.9 us
    pallas_call x4, Pallas kernels, project(): pl.pallas_call(project_kernel, out_shape=(jax.ShapeDtypeStruct((LEN, colu...  40 us
    pallas_call x1, Pallas kernels, finish_middle(): pl.pallas_call(functools.partial(middle_kernel, count), out_shape=(jax.Sh...  29.1 us
    pallas_call x1, Pallas kernels, attend_back(): pl.pallas_call(functools.partial(attend_back_kernel, heads, count), out_s...  28.6 us
    pallas_call x1, Pallas kernels, feed(): pl.pallas_call(gate_kernel, out_shape=(jax.ShapeDtypeStruct((LEN, hidden)...  21.4 us
  transfers between devices with their start and end apart: 50, of which 17 were waited for; matrix products, arithmetic and copies ran while one was open for 9% of the time, Pallas kernels for 50%

profile of v5, /device:TPU:0, one launch (start us, length us, event | category | flops | bytes accessed | tf_op | source)
XLA Modules:
  0.0 719.4 jit_solution(1086816989334110503)
XLA Ops:
  17.1 26.7 %collective-permute-done.x_ref.refs_1_ = bf16[256,2304]{1,0:T(8,128)(2,1)S(1)} collective-permute-done((bf16[256,2304]{1,0:T(8,128)(2,1)S(1)}, bf16[256,2304]{1,0:T(8,128)(2,1)S(1)}, u32[]{:S(2)}, u32[]{:S(2)}) %collective-permute-start) | collective-permute-done | bytes 1179680 | tf_op jit(solution)/shard_map/ppermute | solution.py:56
  47.5 25.3 %collective-permute-done.1.x_ref.refs_2_ = bf16[256,2304]{1,0:T(8,128)(2,1)S(1)} collective-permute-done((bf16[256,2304]{1,0:T(8,128)(2,1)S(1)}, bf16[256,2304]{1,0:T(8,128)(2,1)S(1)}, u32[]{:S(2)}, u32[]{:S(2)}) %collective-permute-start.1) | collective-permute-done | bytes 1179680 | tf_op jit(solution)/shard_map/ppermute | solution.py:56
  72.8 10.0 %project.4 = (bf16[1024,1920]{1,0:T(8,128)(2,1)}, f32[8,128]{1,0:T(8,128)}) custom-call(s32[2]{0:T(128)} %get-tuple-element.161.where_ref.place_ref, bf16[256,2304]{1,0:T(8,128)(2,1)} %x_ref.3, f32[1,2304]{1,0:T(1,128)} %broadcast_in_dim.4.gain_ref, bf16[2304,1920]{1,0:T(8,128)(2,1)} %all-gather.5.cloned.1.call-done.w_ref, ...), custom_call_target="tpu_custom_call" | custom-call | flops 27000000512 | tf_op jit(solution)/shard_map/project/pallas_call | solution.py:395
  82.8 9.7 %project.5 = (bf16[1024,1920]{1,0:T(8,128)(2,1)}, f32[8,128]{1,0:T(8,128)}) custom-call(s32[2]{0:T(128)} %pad_add_fusion.3.where_ref, bf16[256,2304]{1,0:T(8,128)(2,1)} %copy-done.9, f32[1,2304]{1,0:T(1,128)} %broadcast_in_dim.4.gain_ref, bf16[2304,1920]{1,0:T(8,128)(2,1)} %all-gather.5.cloned.1.call-done.w_ref, ...), custom_call_target="tpu_custom_call", output_to_operand_aliasing={{0}: (6, {})} | custom-call | flops 27000000512 | tf_op jit(solution)/shard_map/project/pallas_call | solution.py:395
  92.5 9.6 %project.6 = (bf16[1024,1920]{1,0:T(8,128)(2,1)}, f32[8,128]{1,0:T(8,128)}) custom-call(s32[2]{0:T(128)} %pad_add_fusion.2.where_ref, bf16[256,2304]{1,0:T(8,128)(2,1)} %copy-done.11, f32[1,2304]{1,0:T(1,128)} %broadcast_in_dim.4.gain_ref, bf16[2304,1920]{1,0:T(8,128)(2,1)} %all-gather.5.cloned.1.call-done.w_ref, ...), custom_call_target="tpu_custom_call", output_to_operand_aliasing={{0}: (6, {})} | custom-call | flops 27000000512 | tf_op jit(solution)/shard_map/project/pallas_call | solution.py:395
  107.5 10.6 %project.7 = (bf16[1024,1920]{1,0:T(8,128)(2,1)}, f32[8,128]{1,0:T(8,128)}) custom-call(s32[2]{0:T(128)} %get-tuple-element.162.where_ref, bf16[256,2304]{1,0:T(8,128)(2,1)} %copy-done.12, f32[1,2304]{1,0:T(1,128)} %broadcast_in_dim.4.gain_ref, bf16[2304,1920]{1,0:T(8,128)(2,1)} %all-gather.5.cloned.1.call-done.w_ref, ...), custom_call_target="tpu_custom_call", output_to_operand_aliasing={{0}: (6, {})} | custom-call | flops 27000000512 | tf_op jit(solution)/shard_map/project/pallas_call | solution.py:395
  118.1 18.1 %attend.1 = (bf16[1024,640]{1,0:T(8,128)(2,1)}, bf16[1024,640]{1,0:T(8,128)(2,1)}, f32[5,2,1024]{2,1,0:T(2,128)}) custom-call(s32[1]{0:T(128)S(6)} %copy.61.prefix_ref, bf16[1024,1920]{1,0:T(8,128)(2,1)} %get-tuple-element.88.qkv_ref), custom_call_target="tpu_custom_call" | custom-call | flops 54000001024 | tf_op jit(solution)/shard_map/attend/pallas_call | solution.py:509
  142.4 27.8 %collective-permute-done.6.refs_1_.refs_4_ = bf16[1024,640]{1,0:T(8,128)(2,1)S(1)} collective-permute-done((bf16[1024,640]{1,0:T(8,128)(2,1)}, bf16[1024,640]{1,0:T(8,128)(2,1)S(1)}, u32[]{:S(2)}, u32[]{:S(2)}) %collective-permute-start.6) | collective-permute-done | bytes 1310752 | tf_op jit(solution)/shard_map/ppermute | solution.py:56
  173.1 28.0 %collective-permute-done.7.refs_2_ = bf16[1024,640]{1,0:T(8,128)(2,1)S(1)} collective-permute-done((bf16[1024,640]{1,0:T(8,128)(2,1)}, bf16[1024,640]{1,0:T(8,128)(2,1)S(1)}, u32[]{:S(2)}, u32[]{:S(2)}) %collective-permute-start.7) | collective-permute-done | bytes 1310752 | tf_op jit(solution)/shard_map/ppermute | solution.py:56
  201.6 10.2 %lay_tokens.1 = (bf16[2,1024,1152]{2,1,0:T(8,128)(2,1)}, bf16[1024,2304]{1,0:T(8,128)(2,1)}) custom-call(s32[2]{0:T(128)} %get-tuple-element.161.where_ref.place_ref, f32[1,2304]{1,0:T(1,128)} %broadcast_in_dim.4.gain_ref, bf16[256,2304]{1,0:T(8,128)(2,1)} %x_ref.3, bf16[256,2304]{1,0:T(8,128)(2,1)} %copy-done.9, bf16[256,2304]{1,0:T(8,128)(2,1)} %copy-done.11, ...), custom_call_target="tpu_custom_call" | custom-call | flops 30000001024 | tf_op jit(solution)/shard_map/lay_tokens/pallas_call | solution.py:432
  214.0 15.7 %collective-permute-done.8.refs_3_.refs_0_ = bf16[1024,640]{1,0:T(8,128)(2,1)} collective-permute-done((bf16[1024,640]{1,0:T(8,128)(2,1)S(1)}, bf16[1024,640]{1,0:T(8,128)(2,1)}, u32[]{:S(2)}, u32[]{:S(2)}) %collective-permute-start.8) | collective-permute-done | bytes 1310752 | tf_op jit(solution)/shard_map/ppermute | solution.py:56
  243.9 29.1 %finish_middle.1 = (bf16[1024,2304]{1,0:T(8,128)(2,1)}, bf16[2,1024,1152]{2,1,0:T(8,128)(2,1)}, f32[256,2304]{1,0:T(8,128)}) custom-call(s32[2]{0:T(128)} %get-tuple-element.161.where_ref.place_ref, bf16[1024,640]{1,0:T(8,128)(2,1)} %get-tuple-element.89.refs_4_.refs_0_.out_ref, bf16[1024,640]{1,0:T(8,128)(2,1)} %copy-done, bf16[1024,640]{1,0:T(8,128)(2,1)} %copy-done.7, ...), custom_call_target="tpu_custom_call" | custom-call | flops 65999998976 | tf_op jit(solution)/shard_map/finish_middle/pallas_call | solution.py:650
  276.0 21.4 %feed.1 = (bf16[1024,1536]{1,0:T(8,128)(2,1)}, bf16[1024,3072]{1,0:T(8,128)(2,1)}) custom-call(bf16[1024,2304]{1,0:T(8,128)(2,1)} %get-tuple-element.94.normed_ref.refs_1_, bf16[2304,3072]{1,0:T(8,128)(2,1)} %all-gather.7.cloned.1.call-done.refs_2_.weight_ref), custom_call_target="tpu_custom_call" | custom-call | flops 62999998464 | tf_op jit(solution)/shard_map/feed/pallas_call | solution.py:694
  305.4 15.7 %feed_back.4 = (bf16[1024,3072]{1,0:T(8,128)(2,1)}, bf16[2,1024,1152]{2,1,0:T(8,128)(2,1)}, bf16[256,2304]{1,0:T(8,128)(2,1)}) custom-call(s32[2]{0:T(128)} %pad_add_fusion.3.where_ref, bf16[256,2304]{1,0:T(8,128)(2,1)} %copy-done.1, bf16[1024,3072]{1,0:T(8,128)(2,1)} %get-tuple-element.96.slope_ref, ...), custom_call_target="tpu_custom_call" | custom-call | flops 44999999488 | tf_op jit(solution)/shard_map/feed_back/pallas_call | solution.py:753
  321.5 13.6 %collective-permute-done.11.refs_2_.grad_ref = bf16[256,2304]{1,0:T(8,128)(2,1)S(1)} collective-permute-done((bf16[256,2304]{1,0:T(8,128)(2,1)S(1)}, bf16[256,2304]{1,0:T(8,128)(2,1)S(1)}, u32[]{:S(2)}, u32[]{:S(2)}) %collective-permute-start.11) | collective-permute-done | bytes 1179680 | tf_op jit(solution)/shard_map/ppermute | solution.py:56
  336.1 15.7 %feed_back.5 = (bf16[1024,3072]{1,0:T(8,128)(2,1)}, bf16[2,1024,1152]{2,1,0:T(8,128)(2,1)}, bf16[256,2304]{1,0:T(8,128)(2,1)}) custom-call(s32[2]{0:T(128)} %pad_add_fusion.2.where_ref, bf16[256,2304]{1,0:T(8,128)(2,1)} %copy-done.17, bf16[1024,3072]{1,0:T(8,128)(2,1)} %get-tuple-element.96.slope_ref, ...), custom_call_target="tpu_custom_call", output_to_operand_aliasing={{0}: (5, {}), {1}: (6, {})} | custom-call | flops 44999999488 | tf_op jit(solution)/shard_map/feed_back/pallas_call | solution.py:753
  351.8 15.7 %feed_back.6 = (bf16[1024,3072]{1,0:T(8,128)(2,1)}, bf16[2,1024,1152]{2,1,0:T(8,128)(2,1)}, bf16[256,2304]{1,0:T(8,128)(2,1)}) custom-call(s32[2]{0:T(128)} %get-tuple-element.162.where_ref, bf16[256,2304]{1,0:T(8,128)(2,1)} %copy-done.18, bf16[1024,3072]{1,0:T(8,128)(2,1)} %get-tuple-element.96.slope_ref, ...), custom_call_target="tpu_custom_call", output_to_operand_aliasing={{0}: (5, {}), {1}: (6, {})} | custom-call | flops 44999999488 | tf_op jit(solution)/shard_map/feed_back/pallas_call | solution.py:753
  371.6 16.2 %feed_back.7 = (bf16[1024,3072]{1,0:T(8,128)(2,1)}, bf16[2,1024,1152]{2,1,0:T(8,128)(2,1)}, f32[256,2304]{1,0:T(8,128)}) custom-call(s32[2]{0:T(128)} %get-tuple-element.161.where_ref.place_ref, bf16[256,2304]{1,0:T(8,128)(2,1)} %scaled.1.grad_ref, bf16[1024,3072]{1,0:T(8,128)(2,1)} %get-tuple-element.96.slope_ref, ...), custom_call_target="tpu_custom_call", output_to_operand_aliasing={{0}: (5, {}), {1}: (6, {})} | custom-call | flops 44999999488 | tf_op jit(solution)/shard_map/feed_back/pallas_call | solution.py:753
  387.8 7.6 %weight_grad.6.refs_0_ = bf16[1152,1536]{1,0:T(8,128)(2,1)} custom-call(bf16[2,1024,1152]{2,1,0:T(8,128)(2,1)} %get-tuple-element.108.left_ref, bf16[1024,1536]{1,0:T(8,128)(2,1)} %get-tuple-element.95.right_ref), custom_call_target="tpu_custom_call" | custom-call | flops 17999998976 | tf_op jit(solution)/shard_map/weight_grad/pallas_call | solution.py:142
  402.9 11.9 %weight_grad.7.refs_1_.refs_0_ = bf16[1152,3072]{1,0:T(8,128)(2,1)} custom-call(bf16[2,1024,1152]{2,1,0:T(8,128)(2,1)} %get-tuple-element.110.left_ref, bf16[1024,3072]{1,0:T(8,128)(2,1)} %get-tuple-element.111.right_ref, bf16[256,2304]{1,0:T(8,128)(2,1)} %get-tuple-element.109.refs_1_.refs_0_), custom_call_target="tpu_custom_call" | custom-call | flops 32999999488 | tf_op jit(solution)/shard_map/weight_grad/pallas_call | solution.py:142
  416.7 8.1 %weight_grad.8.refs_0_ = bf16[1152,1536]{1,0:T(8,128)(2,1)} custom-call(bf16[2,1024,1152]{2,1,0:T(8,128)(2,1)} %get-tuple-element.108.left_ref, bf16[1024,1536]{1,0:T(8,128)(2,1)} %get-tuple-element.95.right_ref, bf16[1152,1536]{1,0:T(8,128)(2,1)} %copy-done.6, bf16[1152,3072]{1,0:T(8,128)(2,1)} %weight_grad.7.refs_1_.refs_0_), custom_call_target="tpu_custom_call" | custom-call | flops 17999998976 | tf_op jit(solution)/shard_map/weight_grad/pallas_call | solution.py:142
  424.8 7.1 collective-permute-done.14.arrived_ref
  439.4 8.7 %spread.1 = (bf16[256,640]{1,0:T(8,128)(2,1)}, bf16[256,640]{1,0:T(8,128)(2,1)}, bf16[256,640]{1,0:T(8,128)(2,1)}, bf16[256,640]{1,0:T(8,128)(2,1)}, s32[1]{0:T(128)}) custom-call(bf16[256,2304]{1,0:T(8,128)(2,1)} %get-tuple-element.112.value_ref, bf16[2304,2560]{1,0:T(8,128)(2,1)} %all-gather.9.cloned.1.call-done.refs_4_.refs_2_.weight_ref), custom_call_target="tpu_custom_call" | custom-call | flops 24000000000 | tf_op jit(solution)/shard_map/spread/pallas_call | solution.py:838
  464.3 13.2 %weight_grad.9.refs_7_ = bf16[1152,3072]{1,0:T(8,128)(2,1)} custom-call(bf16[2,1024,1152]{2,1,0:T(8,128)(2,1)} %get-tuple-element.110.left_ref, bf16[1024,3072]{1,0:T(8,128)(2,1)} %get-tuple-element.111.right_ref, bf16[1152,3072]{1,0:T(8,128)(2,1)} %collective-permute-done.19.refs_0_, bf16[256,2304]{1,0:T(8,128)(2,1)} %fusion.14.refs_1_.refs_0_), custom_call_target="tpu_custom_call" | custom-call | flops 32999999488 | tf_op jit(solution)/shard_map/weight_grad/pallas_call | solution.py:142
  482.2 28.6 %attend_back.1.right_ref = bf16[1024,1920]{1,0:T(8,128)(2,1)} custom-call(s32[2]{0:T(128)} %pad_add_fusion.4.prefix_ref, bf16[1024,1920]{1,0:T(8,128)(2,1)} %get-tuple-element.88.qkv_ref, bf16[1024,640]{1,0:T(8,128)(2,1)} %get-tuple-element.89.refs_4_.refs_0_.out_ref, bf16[256,640]{1,0:T(8,128)(2,1)} %get-tuple-element.113.refs_0_, ...), custom_call_target="tpu_custom_call" | custom-call | flops 83999997952 | tf_op jit(solution)/shard_map/attend_back/pallas_call | solution.py:593
  520.8 9.5 %weight_grad.11.refs_1_.refs_0_ = bf16[1152,1920]{1,0:T(8,128)(2,1)} custom-call(bf16[2,1024,1152]{2,1,0:T(8,128)(2,1)} %get-tuple-element.120.left_ref, bf16[1024,1920]{1,0:T(8,128)(2,1)} %attend_back.1.right_ref, bf16[256,2304]{1,0:T(8,128)(2,1)} %copy-done.16, bf16[256,2304]{1,0:T(8,128)(2,1)} %copy-done.13), custom_call_target="tpu_custom_call" | custom-call | flops 24000000000 | tf_op jit(solution)/shard_map/weight_grad/pallas_call | solution.py:142
  539.8 7.9 %fusion.4.one_ref = f32[256,2304]{1,0:T(8,128)} fusion(bf16[2304,1920]{1,0:T(8,128)(2,1)} %all-gather.5.cloned.1.call-done.w_ref, bf16[1024,1920]{1,0:T(8,128)(2,1)} %attend_back.1.right_ref, s32[]{:T(128)S(6)} %select_n.68), kind=kOutput, calls=%fused_computation.4 | convolution fusion | flops 2264924160 | bytes 12189700 | tf_op jit(solution)/shard_map/dot_general | solution.py:39
  564.8 10.9 %scatter_chip.3 = (bf16[2,144,1920]{2,1,0:T(8,128)(2,1)}, bf16[2,144,1920]{2,1,0:T(8,128)(2,1)}, bf16[2,144,1920]{2,1,0:T(8,128)(2,1)}, bf16[2,144,1920]{2,1,0:T(8,128)(2,1)}, s32[1]{0:T(128)}) custom-call(s32[2]{0:T(128)} %pad_add_fusion.5.where_ref, bf16[2,1024,1152]{2,1,0:T(8,128)(2,1)} %get-tuple-element.120.left_ref, ...), custom_call_target="tpu_custom_call" | custom-call | flops 30000001024 | tf_op jit(solution)/shard_map/scatter_chip/pallas_call | solution.py:185
  578.2 7.9 %fusion.2.one_ref = f32[256,2304]{1,0:T(8,128)} fusion(bf16[2304,1920]{1,0:T(8,128)(2,1)} %all-gather.5.cloned.1.call-done.w_ref, bf16[1024,1920]{1,0:T(8,128)(2,1)} %attend_back.1.right_ref, s32[]{:T(128)S(6)} %select_n.70), kind=kOutput, calls=%fused_computation.2 | convolution fusion | flops 2264924160 | bytes 12189700 | tf_op jit(solution)/shard_map/dot_general | solution.py:39
  591.0 8.0 %fusion.refs_3_.term_ref = f32[256,2304]{1,0:T(8,128)} fusion(bf16[2304,1920]{1,0:T(8,128)(2,1)} %all-gather.5.cloned.1.call-done.w_ref, bf16[1024,1920]{1,0:T(8,128)(2,1)} %attend_back.1.right_ref, s32[]{:T(128)S(6)} %select_n.71), kind=kOutput, calls=%fused_computation | convolution fusion | flops 2264924160 | bytes 12189700 | tf_op jit(solution)/shard_map/dot_general | solution.py:39
  617.4 9.1 %collective-permute-done.33.refs_3_ = bf16[144,2560]{1,0:T(8,128)(2,1)S(1)} collective-permute-done((bf16[144,2560]{1,0:T(8,128)(2,1)}, bf16[144,2560]{1,0:T(8,128)(2,1)S(1)}, u32[]{:S(2)}, u32[]{:S(2)}) %collective-permute-start.33) | collective-permute-done | bytes 737312 | tf_op jit(solution)/shard_map/ppermute | solution.py:94
  640.9 17.8 %collective-permute-done.31.refs_2_.arrived_ref = bf16[256,2304]{1,0:T(8,128)(2,1)S(1)} collective-permute-done((bf16[256,2304]{1,0:T(8,128)(2,1)}, bf16[256,2304]{1,0:T(8,128)(2,1)S(1)}, u32[]{:S(2)}, u32[]{:S(2)}) %collective-permute-start.31) | collective-permute-done | bytes 1179680 | tf_op jit(solution)/shard_map/ppermute | solution.py:56
  (240 shorter events, 223.7 us)
Async XLA Ops:
  7.2 65.6 %all-gather.5.cloned.1.call-start = ((), (), s32[]{:S(2)}) async-start(), calls=%async_computation.2 | async-start | bytes 9953280 | tf_op jit(solution)/shard_map/all_gather | solution.py:98
  9.7 160.5 %all-gather.7.cloned.1.call-start = ((), (), s32[]{:S(2)}) async-start(), calls=%async_computation.3 | async-start | bytes 15925248 | tf_op jit(solution)/shard_map/all_gather | solution.py:98
  12.7 227.2 %all-gather.9.cloned.1.call-start = ((), (), s32[]{:S(2)}) async-start(), calls=%async_computation.4 | async-start | bytes 13271040 | tf_op jit(solution)/shard_map/all_gather | solution.py:98
  12.8 31.1 %collective-permute-start = (bf16[256,2304]{1,0:T(8,128)(2,1)S(1)}, bf16[256,2304]{1,0:T(8,128)(2,1)S(1)}, u32[]{:S(2)}, u32[]{:S(2)}) collective-permute-start(bf16[256,2304]{1,0:T(8,128)(2,1)S(1)} %copy-done.8), channel_id=1, source_target_pairs={{0,1},{1,2},{2,3},{3,0},{4,5},{5,6},{6,7},{7,4},{8,9},{9,10},{10,1... | collective-permute-start | bytes 3538952 | tf_op jit(solution)/shard_map/ppermute | solution.py:56
  72.8 29.4 %collective-permute-start.2 = (bf16[256,2304]{1,0:T(8,128)(2,1)S(1)}, bf16[256,2304]{1,0:T(8,128)(2,1)S(1)}, u32[]{:S(2)}, u32[]{:S(2)}) collective-permute-start(bf16[256,2304]{1,0:T(8,128)(2,1)S(1)} %collective-permute-done.1.x_ref.refs_2_), channel_id=1, source_target_pairs={{0,1},{1,2},{2,3},{3,0},{4,5},{5,6},{6,7},{7,4},{8,9},{9,10},{10,1... | collective-permute-start | bytes 3538952 | tf_op jit(solution)/shard_map/ppermute | solution.py:56
  103.1 33.1 %collective-permute-start.5 = (bf16[288,640]{1,0:T(8,128)(2,1)}, bf16[288,640]{1,0:T(8,128)(2,1)S(1)}, u32[]{:S(2)}, u32[]{:S(2)}) collective-permute-start(bf16[288,640]{1,0:T(8,128)(2,1)} %gate.9.refs_0_), channel_id=1, source_target_pairs={{0,3},{1,0},{2,1},{3,2},{4,7},{5,4},{6,5},{7,6},{8,11},{9,8},{10,9... | collective-permute-start | bytes 1105928 | tf_op jit(solution)/shard_map/ppermute | solution.py:80
  106.9 29.3 %collective-permute-start.4 = (bf16[288,640]{1,0:T(8,128)(2,1)}, bf16[288,640]{1,0:T(8,128)(2,1)S(1)}, u32[]{:S(2)}, u32[]{:S(2)}) collective-permute-start(bf16[288,640]{1,0:T(8,128)(2,1)} %gate.9.refs_0_), channel_id=1, source_target_pairs={{0,2},{1,3},{2,0},{3,1},{4,6},{5,7},{6,4},{7,5},{8,10},{9,11},{10,... | collective-permute-start | bytes 1105928 | tf_op jit(solution)/shard_map/ppermute | solution.py:80
  106.9 29.3 %collective-permute-start.3 = (bf16[288,640]{1,0:T(8,128)(2,1)}, bf16[288,640]{1,0:T(8,128)(2,1)S(1)}, u32[]{:S(2)}, u32[]{:S(2)}) collective-permute-start(bf16[288,640]{1,0:T(8,128)(2,1)} %gate.9.refs_0_), channel_id=1, source_target_pairs={{0,1},{1,2},{2,3},{3,0},{4,5},{5,6},{6,7},{7,4},{8,9},{9,10},{10,1... | collective-permute-start | bytes 1105928 | tf_op jit(solution)/shard_map/ppermute | solution.py:80
  139.8 30.4 %collective-permute-start.6 = (bf16[1024,640]{1,0:T(8,128)(2,1)}, bf16[1024,640]{1,0:T(8,128)(2,1)S(1)}, u32[]{:S(2)}, u32[]{:S(2)}) collective-permute-start(bf16[1024,640]{1,0:T(8,128)(2,1)} %gate.10), channel_id=1, source_target_pairs={{0,1},{1,2},{2,3},{3,0},{4,5},{5,6},{6,7},{7,4},{8,9},{9,10},{10,1... | collective-permute-start | bytes 3932168 | tf_op jit(solution)/shard_map/ppermute | solution.py:56
  171.2 133.2 %all-gather.11.cloned.1.call-start = ((), (), s32[]{:S(2)}) async-start(), calls=%async_computation.5 | async-start | bytes 7962624 | tf_op jit(solution)/shard_map/all_gather | solution.py:98
  171.3 29.7 %collective-permute-start.7 = (bf16[1024,640]{1,0:T(8,128)(2,1)}, bf16[1024,640]{1,0:T(8,128)(2,1)S(1)}, u32[]{:S(2)}, u32[]{:S(2)}) collective-permute-start(bf16[1024,640]{1,0:T(8,128)(2,1)} %copy-done), channel_id=1, source_target_pairs={{0,1},{1,2},{2,3},{3,0},{4,5},{5,6},{6,7},{7,4},{8,9},{9,10},{10,1... | collective-permute-start | bytes 3932168 | tf_op jit(solution)/shard_map/ppermute | solution.py:56
  214.0 451.7 %reduce-scatter.5.cloned.1.call-start = ((), (), s32[]{:S(2)}) async-start(), calls=%async_computation.7 | async-start | bytes 4423680 | tf_op jit(solution)/shard_map/reduce_scatter | solution.py:296
  242.4 30.6 %collective-permute-start.9 = (bf16[256,2304]{1,0:T(8,128)(2,1)}, bf16[256,2304]{1,0:T(8,128)(2,1)S(1)}, u32[]{:S(2)}, u32[]{:S(2)}) collective-permute-start(bf16[256,2304]{1,0:T(8,128)(2,1)} %scaled.1.grad_ref), channel_id=1, source_target_pairs={{0,1},{1,2},{2,3},{3,0},{4,5},{5,6},{6,7},{7,4},{8,9},{9,10},{10,1... | collective-permute-start | bytes 3538952 | tf_op jit(solution)/shard_map/ppermute | solution.py:56
  274.3 30.1 %collective-permute-start.10 = (bf16[256,2304]{1,0:T(8,128)(2,1)}, bf16[256,2304]{1,0:T(8,128)(2,1)S(1)}, u32[]{:S(2)}, u32[]{:S(2)}) collective-permute-start(bf16[256,2304]{1,0:T(8,128)(2,1)} %gate.12), channel_id=1, source_target_pairs={{0,1},{1,2},{2,3},{3,0},{4,5},{5,6},{6,7},{7,4},{8,9},{9,10},{10,1... | collective-permute-start | bytes 3538952 | tf_op jit(solution)/shard_map/ppermute | solution.py:56
  304.4 30.7 %collective-permute-start.11 = (bf16[256,2304]{1,0:T(8,128)(2,1)S(1)}, bf16[256,2304]{1,0:T(8,128)(2,1)S(1)}, u32[]{:S(2)}, u32[]{:S(2)}) collective-permute-start(bf16[256,2304]{1,0:T(8,128)(2,1)S(1)} %collective-permute-done.10.refs_0_.grad_ref), channel_id=1, source_target_pairs={{0,1},{1,2},{2,3},{3,0},{4,5},{5,6},{6,7},{7,4},{8,9},{9,10},{10,1... | collective-permute-start | bytes 3538952 | tf_op jit(solution)/shard_map/ppermute | solution.py:56
  321.1 46.4 %collective-permute-start.12 = (bf16[256,2304]{1,0:T(8,128)(2,1)}, bf16[256,2304]{1,0:T(8,128)(2,1)S(1)}, u32[]{:S(2)}, u32[]{:S(2)}) collective-permute-start(bf16[256,2304]{1,0:T(8,128)(2,1)} %get-tuple-element.104), channel_id=1, source_target_pairs={{0,1},{1,2},{2,3},{3,0},{4,5},{5,6},{6,7},{7,4},{8,9},{9,10},{10,1... | collective-permute-start | bytes 3538952 | tf_op jit(solution)/shard_map/ppermute | solution.py:56
  402.5 29.4 %collective-permute-start.14 = (bf16[256,2304]{1,0:T(8,128)(2,1)S(1)}, bf16[256,2304]{1,0:T(8,128)(2,1)S(1)}, u32[]{:S(2)}, u32[]{:S(2)}) collective-permute-start(bf16[256,2304]{1,0:T(8,128)(2,1)S(1)} %copy-done.21), channel_id=1, source_target_pairs={{0,1},{1,2},{2,3},{3,0},{4,5},{5,6},{6,7},{7,4},{8,9},{9,10},{10,1... | collective-permute-start | bytes 3538952 | tf_op jit(solution)/shard_map/ppermute | solution.py:56
  448.8 246.8 %reduce-scatter.3.cloned.1.call-start = ((), (), s32[]{:S(2)}) async-start(), calls=%async_computation.6 | async-start | bytes 8847360 | tf_op jit(solution)/shard_map/reduce_scatter | solution.py:296
  464.2 66.2 %collective-permute-start.22 = (bf16[1152,2560]{1,0:T(8,128)(2,1)}, bf16[1152,2560]{1,0:T(8,128)(2,1)}, u32[]{:S(2)}, u32[]{:S(2)}) collective-permute-start(bf16[1152,2560]{1,0:T(8,128)(2,1)} %weight_grad.10.refs_8_), channel_id=1, source_target_pairs={{0,4},{4,0},{8,12},{12,8},{16,20},{20,16},{24,28},{28,24},{1,5},{5... | collective-permute-start | bytes 17694728 | tf_op jit(solution)/shard_map/ppermute | solution.py:94
  481.3 38.5 %collective-permute-start.20 = (bf16[256,2304]{1,0:T(8,128)(2,1)}, bf16[256,2304]{1,0:T(8,128)(2,1)S(1)}, u32[]{:S(2)}, u32[]{:S(2)}) collective-permute-start(bf16[256,2304]{1,0:T(8,128)(2,1)} %gate.15), channel_id=1, source_target_pairs={{0,1},{1,2},{2,3},{3,0},{4,5},{5,6},{6,7},{7,4},{8,9},{9,10},{10,1... | collective-permute-start | bytes 3538952 | tf_op jit(solution)/shard_map/ppermute | solution.py:56
  517.3 30.4 %collective-permute-start.23 = (bf16[256,2304]{1,0:T(8,128)(2,1)S(1)}, bf16[256,2304]{1,0:T(8,128)(2,1)S(1)}, u32[]{:S(2)}, u32[]{:S(2)}) collective-permute-start(bf16[256,2304]{1,0:T(8,128)(2,1)S(1)} %fusion.6.refs_0_), channel_id=1, source_target_pairs={{0,1},{1,2},{2,3},{3,0},{4,5},{5,6},{6,7},{7,4},{8,9},{9,10},{10,1... | collective-permute-start | bytes 3538952 | tf_op jit(solution)/shard_map/ppermute | solution.py:56
  530.4 34.5 %collective-permute-start.21 = (bf16[1152,1920]{1,0:T(8,128)(2,1)}, bf16[1152,1920]{1,0:T(8,128)(2,1)}, u32[]{:S(2)}, u32[]{:S(2)}) collective-permute-start(bf16[1152,1920]{1,0:T(8,128)(2,1)} %weight_grad.11.refs_1_.refs_0_), channel_id=1, source_target_pairs={{0,4},{4,0},{8,12},{12,8},{16,20},{20,16},{24,28},{28,24},{1,5},{5... | collective-permute-start | bytes 13271048 | tf_op jit(solution)/shard_map/ppermute | solution.py:94
  537.8 71.3 %collective-permute-start.28 = (bf16[2,144,2560]{2,1,0:T(8,128)(2,1)}, bf16[2,144,2560]{2,1,0:T(8,128)(2,1)}, u32[]{:S(2)}, u32[]{:S(2)}) collective-permute-start(bf16[2,144,2560]{2,1,0:T(8,128)(2,1)} %get-tuple-element.122.refs_1_), channel_id=1, source_target_pairs={{0,16},{4,20},{8,24},{12,28},{16,0},{20,4},{24,8},{28,12},{1,17},{... | collective-permute-start | bytes 4423688 | tf_op jit(solution)/shard_map/ppermute | solution.py:94
  539.1 60.6 %collective-permute-start.29 = (bf16[2,144,2560]{2,1,0:T(8,128)(2,1)}, bf16[2,144,2560]{2,1,0:T(8,128)(2,1)}, u32[]{:S(2)}, u32[]{:S(2)}) collective-permute-start(bf16[2,144,2560]{2,1,0:T(8,128)(2,1)} %get-tuple-element.123.refs_2_), channel_id=1, source_target_pairs={{0,8},{4,12},{8,0},{12,4},{16,24},{20,28},{24,16},{28,20},{1,9},{5... | collective-permute-start | bytes 4423688 | tf_op jit(solution)/shard_map/ppermute | solution.py:94
  552.6 33.6 %collective-permute-start.24 = (bf16[256,2304]{1,0:T(8,128)(2,1)}, bf16[256,2304]{1,0:T(8,128)(2,1)S(1)}, u32[]{:S(2)}, u32[]{:S(2)}) collective-permute-start(bf16[256,2304]{1,0:T(8,128)(2,1)} %get-tuple-element.124.refs_0_), channel_id=1, source_target_pairs={{0,1},{1,2},{2,3},{3,0},{4,5},{5,6},{6,7},{7,4},{8,9},{9,10},{10,1... | collective-permute-start | bytes 3538952 | tf_op jit(solution)/shard_map/ppermute | solution.py:56
  563.3 49.9 %collective-permute-start.27 = (bf16[256,2304]{1,0:T(8,128)(2,1)}, bf16[256,2304]{1,0:T(8,128)(2,1)}, u32[]{:S(2)}, u32[]{:S(2)}) collective-permute-start(bf16[256,2304]{1,0:T(8,128)(2,1)} %get-tuple-element.126.refs_1_), channel_id=1, source_target_pairs={{0,1},{1,2},{2,3},{3,0},{4,5},{5,6},{6,7},{7,4},{8,9},{9,10},{10,1... | collective-permute-start | bytes 3538952 | tf_op jit(solution)/shard_map/ppermute | solution.py:56
  576.4 61.3 %collective-permute-start.26 = (bf16[2,144,1920]{2,1,0:T(8,128)(2,1)}, bf16[2,144,1920]{2,1,0:T(8,128)(2,1)}, u32[]{:S(2)}, u32[]{:S(2)}) collective-permute-start(bf16[2,144,1920]{2,1,0:T(8,128)(2,1)} %get-tuple-element.128.refs_0_), channel_id=1, source_target_pairs={{0,16},{4,20},{8,24},{12,28},{16,0},{20,4},{24,8},{28,12},{1,17},{... | collective-permute-start | bytes 3317768 | tf_op jit(solution)/shard_map/ppermute | solution.py:94
  586.1 48.4 %collective-permute-start.30 = (bf16[2,144,1920]{2,1,0:T(8,128)(2,1)}, bf16[2,144,1920]{2,1,0:T(8,128)(2,1)}, u32[]{:S(2)}, u32[]{:S(2)}) collective-permute-start(bf16[2,144,1920]{2,1,0:T(8,128)(2,1)} %get-tuple-element.129.refs_1_), channel_id=1, source_target_pairs={{0,8},{4,12},{8,0},{12,4},{16,24},{20,28},{24,16},{28,20},{1,9},{5... | collective-permute-start | bytes 3317768 | tf_op jit(solution)/shard_map/ppermute | solution.py:94
  599.7 41.2 %collective-permute-start.25 = (bf16[256,2304]{1,0:T(8,128)(2,1)}, bf16[256,2304]{1,0:T(8,128)(2,1)}, u32[]{:S(2)}, u32[]{:S(2)}) collective-permute-start(bf16[256,2304]{1,0:T(8,128)(2,1)} %get-tuple-element.131.refs_0_), channel_id=1, source_target_pairs={{0,1},{1,2},{2,3},{3,0},{4,5},{5,6},{6,7},{7,4},{8,9},{9,10},{10,1... | collective-permute-start | bytes 3538952 | tf_op jit(solution)/shard_map/ppermute | solution.py:56
  626.5 32.1 %collective-permute-start.31 = (bf16[256,2304]{1,0:T(8,128)(2,1)}, bf16[256,2304]{1,0:T(8,128)(2,1)S(1)}, u32[]{:S(2)}, u32[]{:S(2)}) collective-permute-start(bf16[256,2304]{1,0:T(8,128)(2,1)} %get-tuple-element.138.refs_0_), channel_id=1, source_target_pairs={{0,1},{1,2},{2,3},{3,0},{4,5},{5,6},{6,7},{7,4},{8,9},{9,10},{10,1... | collective-permute-start | bytes 3538952 | tf_op jit(solution)/shard_map/ppermute | solution.py:56
  668.4 30.7 %collective-permute-start.36 = (bf16[288,640]{1,0:T(8,128)(2,1)S(1)}, bf16[288,640]{1,0:T(8,128)(2,1)}, u32[]{:S(2)}, u32[]{:S(2)}) collective-permute-start(bf16[288,640]{1,0:T(8,128)(2,1)S(1)} %copy-done.31), channel_id=1, source_target_pairs={{0,3},{1,0},{2,1},{3,2},{4,7},{5,4},{6,5},{7,6},{8,11},{9,8},{10,9... | collective-permute-start | bytes 1105928 | tf_op jit(solution)/shard_map/ppermute | solution.py:80
  668.4 32.7 %collective-permute-start.37 = (bf16[288,640]{1,0:T(8,128)(2,1)S(1)}, bf16[288,640]{1,0:T(8,128)(2,1)}, u32[]{:S(2)}, u32[]{:S(2)}) collective-permute-start(bf16[288,640]{1,0:T(8,128)(2,1)S(1)} %copy-done.30), channel_id=1, source_target_pairs={{0,2},{1,3},{2,0},{3,1},{4,6},{5,7},{6,4},{7,5},{8,10},{9,11},{10,... | collective-permute-start | bytes 1105928 | tf_op jit(solution)/shard_map/ppermute | solution.py:80
  (61 other events, 481.1 us)
Sparse Core Ops, SparseCore 0:
  10.5 59.0 all-gather.4
  72.0 78.7 all-gather.6
  171.4 68.4 all-gather.8
  241.6 48.8 all-gather.10
  449.0 35.5 reduce-scatter.4
  486.7 76.8 reduce-scatter.2

commit v6 on v5

--- a/solution.py
+++ b/solution.py
@@ -269,15 +269,17 @@
 
 
 def join_marked(one, two, waits=()):
-    whole = pl.BlockSpec(memory_space=pltpu.VMEM)
+    rows, width = one.shape
+    block = pl.BlockSpec((rows // 2, width), lambda i: (i, 0))
     return pl.pallas_call(
         join_kernel,
         out_shape=(
             jax.ShapeDtypeStruct(one.shape, BF16),
             jax.ShapeDtypeStruct((1,), jnp.int32),
         ),
-        in_specs=[whole, whole] + after_all(waits),
-        out_specs=(whole, pl.BlockSpec(memory_space=pltpu.SMEM)),
+        grid=(2,),
+        in_specs=[block, block] + after_all(waits),
+        out_specs=(block, pl.BlockSpec(memory_space=pltpu.SMEM)),
         compiler_params=params(),
         cost_estimate=cost(3),
         name="join",

time: 729 us -> 728 us (level)
  no operation moved by 1% of the time
where the time goes in v6:
time: 728 us; the launch traced here: 718 us
  Pallas kernels  371 us (51%)
  waiting for transfers between devices  201 us (28%)
  matrix products  54.8 us (8%)
  starting transfers between devices  43.7 us (6%)
  local copies, waits for them, and re-layouts  21.6 us (3%)
  between operations  20.2 us (3%)
    ppermute x18, waiting for transfers between devices, ring_up(): return lax.ppermute(value, 'mp', [(i, (i + 1) % n) for i in range(n)])  171 us
    pallas_call x4, Pallas kernels, feed_back(): pl.pallas_call(feed_back_kernel, out_shape=(jax.ShapeDtypeStruct((LEN, 2...  63.3 us
    pallas_call x6, Pallas kernels, weight_grad(): pl.pallas_call(functools.partial(weight_kernel, arrived is not None), out...  55.2 us
    dot_general x8, matrix products, outer_cols(): lax.dot_general(left, right, (((1,), (1,)), ((), ())), preferred_element_...  54.8 us
    pallas_call x4, Pallas kernels, project(): pl.pallas_call(project_kernel, out_shape=(jax.ShapeDtypeStruct((LEN, colu...  40 us
    pallas_call x1, Pallas kernels, finish_middle(): pl.pallas_call(functools.partial(middle_kernel, count), out_shape=(jax.Sh...  29.1 us
    pallas_call x1, Pallas kernels, attend_back(): pl.pallas_call(functools.partial(attend_back_kernel, heads, count), out_s...  28.6 us
    pallas_call x1, Pallas kernels, feed(): pl.pallas_call(gate_kernel, out_shape=(jax.ShapeDtypeStruct((LEN, hidden)...  21.4 us
  transfers between devices with their start and end apart: 50, of which 17 were waited for; matrix products, arithmetic and copies ran while one was open for 9% of the time, Pallas kernels for 50%

profile of v6, /device:TPU:0, one launch (start us, length us, event | category | flops | bytes accessed | tf_op | source)
XLA Modules:
  0.0 717.8 jit_solution(4113430094432857541)
XLA Ops:
  17.1 26.7 %collective-permute-done.x_ref.refs_1_ = bf16[256,2304]{1,0:T(8,128)(2,1)S(1)} collective-permute-done((bf16[256,2304]{1,0:T(8,128)(2,1)S(1)}, bf16[256,2304]{1,0:T(8,128)(2,1)S(1)}, u32[]{:S(2)}, u32[]{:S(2)}) %collective-permute-start) | collective-permute-done | bytes 1179680 | tf_op jit(solution)/shard_map/ppermute | solution.py:56
  47.5 25.3 %collective-permute-done.1.x_ref.refs_2_ = bf16[256,2304]{1,0:T(8,128)(2,1)S(1)} collective-permute-done((bf16[256,2304]{1,0:T(8,128)(2,1)S(1)}, bf16[256,2304]{1,0:T(8,128)(2,1)S(1)}, u32[]{:S(2)}, u32[]{:S(2)}) %collective-permute-start.1) | collective-permute-done | bytes 1179680 | tf_op jit(solution)/shard_map/ppermute | solution.py:56
  72.8 10.0 %project.4 = (bf16[1024,1920]{1,0:T(8,128)(2,1)}, f32[8,128]{1,0:T(8,128)}) custom-call(s32[2]{0:T(128)} %get-tuple-element.161.where_ref.place_ref, bf16[256,2304]{1,0:T(8,128)(2,1)} %x_ref.3, f32[1,2304]{1,0:T(1,128)} %broadcast_in_dim.4.gain_ref, bf16[2304,1920]{1,0:T(8,128)(2,1)} %all-gather.5.cloned.1.call-done.w_ref, ...), custom_call_target="tpu_custom_call" | custom-call | flops 27000000512 | tf_op jit(solution)/shard_map/project/pallas_call | solution.py:397
  82.8 9.7 %project.5 = (bf16[1024,1920]{1,0:T(8,128)(2,1)}, f32[8,128]{1,0:T(8,128)}) custom-call(s32[2]{0:T(128)} %pad_add_fusion.3.where_ref, bf16[256,2304]{1,0:T(8,128)(2,1)} %copy-done.9, f32[1,2304]{1,0:T(1,128)} %broadcast_in_dim.4.gain_ref, bf16[2304,1920]{1,0:T(8,128)(2,1)} %all-gather.5.cloned.1.call-done.w_ref, ...), custom_call_target="tpu_custom_call", output_to_operand_aliasing={{0}: (6, {})} | custom-call | flops 27000000512 | tf_op jit(solution)/shard_map/project/pallas_call | solution.py:397
  92.5 9.6 %project.6 = (bf16[1024,1920]{1,0:T(8,128)(2,1)}, f32[8,128]{1,0:T(8,128)}) custom-call(s32[2]{0:T(128)} %pad_add_fusion.2.where_ref, bf16[256,2304]{1,0:T(8,128)(2,1)} %copy-done.11, f32[1,2304]{1,0:T(1,128)} %broadcast_in_dim.4.gain_ref, bf16[2304,1920]{1,0:T(8,128)(2,1)} %all-gather.5.cloned.1.call-done.w_ref, ...), custom_call_target="tpu_custom_call", output_to_operand_aliasing={{0}: (6, {})} | custom-call | flops 27000000512 | tf_op jit(solution)/shard_map/project/pallas_call | solution.py:397
  107.5 10.6 %project.7 = (bf16[1024,1920]{1,0:T(8,128)(2,1)}, f32[8,128]{1,0:T(8,128)}) custom-call(s32[2]{0:T(128)} %get-tuple-element.162.where_ref, bf16[256,2304]{1,0:T(8,128)(2,1)} %copy-done.12, f32[1,2304]{1,0:T(1,128)} %broadcast_in_dim.4.gain_ref, bf16[2304,1920]{1,0:T(8,128)(2,1)} %all-gather.5.cloned.1.call-done.w_ref, ...), custom_call_target="tpu_custom_call", output_to_operand_aliasing={{0}: (6, {})} | custom-call | flops 27000000512 | tf_op jit(solution)/shard_map/project/pallas_call | solution.py:397
  118.1 18.1 %attend.1 = (bf16[1024,640]{1,0:T(8,128)(2,1)}, bf16[1024,640]{1,0:T(8,128)(2,1)}, f32[5,2,1024]{2,1,0:T(2,128)}) custom-call(s32[1]{0:T(128)S(6)} %copy.61.prefix_ref, bf16[1024,1920]{1,0:T(8,128)(2,1)} %get-tuple-element.88.qkv_ref), custom_call_target="tpu_custom_call" | custom-call | flops 54000001024 | tf_op jit(solution)/shard_map/attend/pallas_call | solution.py:511
  142.4 27.8 %collective-permute-done.6.refs_1_.refs_4_ = bf16[1024,640]{1,0:T(8,128)(2,1)S(1)} collective-permute-done((bf16[1024,640]{1,0:T(8,128)(2,1)}, bf16[1024,640]{1,0:T(8,128)(2,1)S(1)}, u32[]{:S(2)}, u32[]{:S(2)}) %collective-permute-start.6) | collective-permute-done | bytes 1310752 | tf_op jit(solution)/shard_map/ppermute | solution.py:56
  173.1 28.0 %collective-permute-done.7.refs_2_ = bf16[1024,640]{1,0:T(8,128)(2,1)S(1)} collective-permute-done((bf16[1024,640]{1,0:T(8,128)(2,1)}, bf16[1024,640]{1,0:T(8,128)(2,1)S(1)}, u32[]{:S(2)}, u32[]{:S(2)}) %collective-permute-start.7) | collective-permute-done | bytes 1310752 | tf_op jit(solution)/shard_map/ppermute | solution.py:56
  201.6 10.1 %lay_tokens.1 = (bf16[2,1024,1152]{2,1,0:T(8,128)(2,1)}, bf16[1024,2304]{1,0:T(8,128)(2,1)}) custom-call(s32[2]{0:T(128)} %get-tuple-element.161.where_ref.place_ref, f32[1,2304]{1,0:T(1,128)} %broadcast_in_dim.4.gain_ref, bf16[256,2304]{1,0:T(8,128)(2,1)} %x_ref.3, bf16[256,2304]{1,0:T(8,128)(2,1)} %copy-done.9, bf16[256,2304]{1,0:T(8,128)(2,1)} %copy-done.11, ...), custom_call_target="tpu_custom_call" | custom-call | flops 30000001024 | tf_op jit(solution)/shard_map/lay_tokens/pallas_call | solution.py:434
  214.0 15.7 %collective-permute-done.8.refs_3_.refs_0_ = bf16[1024,640]{1,0:T(8,128)(2,1)} collective-permute-done((bf16[1024,640]{1,0:T(8,128)(2,1)S(1)}, bf16[1024,640]{1,0:T(8,128)(2,1)}, u32[]{:S(2)}, u32[]{:S(2)}) %collective-permute-start.8) | collective-permute-done | bytes 1310752 | tf_op jit(solution)/shard_map/ppermute | solution.py:56
  243.8 29.1 %finish_middle.1 = (bf16[1024,2304]{1,0:T(8,128)(2,1)}, bf16[2,1024,1152]{2,1,0:T(8,128)(2,1)}, f32[256,2304]{1,0:T(8,128)}) custom-call(s32[2]{0:T(128)} %get-tuple-element.161.where_ref.place_ref, bf16[1024,640]{1,0:T(8,128)(2,1)} %get-tuple-element.89.refs_4_.refs_0_.out_ref, bf16[1024,640]{1,0:T(8,128)(2,1)} %copy-done, bf16[1024,640]{1,0:T(8,128)(2,1)} %copy-done.7, ...), custom_call_target="tpu_custom_call" | custom-call | flops 65999998976 | tf_op jit(solution)/shard_map/finish_middle/pallas_call | solution.py:652
  275.8 21.4 %feed.1 = (bf16[1024,1536]{1,0:T(8,128)(2,1)}, bf16[1024,3072]{1,0:T(8,128)(2,1)}) custom-call(bf16[1024,2304]{1,0:T(8,128)(2,1)} %get-tuple-element.94.normed_ref.refs_1_, bf16[2304,3072]{1,0:T(8,128)(2,1)} %all-gather.7.cloned.1.call-done.refs_2_.weight_ref), custom_call_target="tpu_custom_call" | custom-call | flops 62999998464 | tf_op jit(solution)/shard_map/feed/pallas_call | solution.py:696
  305.2 15.7 %feed_back.4 = (bf16[1024,3072]{1,0:T(8,128)(2,1)}, bf16[2,1024,1152]{2,1,0:T(8,128)(2,1)}, bf16[256,2304]{1,0:T(8,128)(2,1)}) custom-call(s32[2]{0:T(128)} %pad_add_fusion.3.where_ref, bf16[256,2304]{1,0:T(8,128)(2,1)} %copy-done.1, bf16[1024,3072]{1,0:T(8,128)(2,1)} %get-tuple-element.96.slope_ref, ...), custom_call_target="tpu_custom_call" | custom-call | flops 44999999488 | tf_op jit(solution)/shard_map/feed_back/pallas_call | solution.py:755
  321.5 13.4 %collective-permute-done.11.refs_2_.grad_ref = bf16[256,2304]{1,0:T(8,128)(2,1)S(1)} collective-permute-done((bf16[256,2304]{1,0:T(8,128)(2,1)S(1)}, bf16[256,2304]{1,0:T(8,128)(2,1)S(1)}, u32[]{:S(2)}, u32[]{:S(2)}) %collective-permute-start.11) | collective-permute-done | bytes 1179680 | tf_op jit(solution)/shard_map/ppermute | solution.py:56
  335.9 15.7 %feed_back.5 = (bf16[1024,3072]{1,0:T(8,128)(2,1)}, bf16[2,1024,1152]{2,1,0:T(8,128)(2,1)}, bf16[256,2304]{1,0:T(8,128)(2,1)}) custom-call(s32[2]{0:T(128)} %pad_add_fusion.2.where_ref, bf16[256,2304]{1,0:T(8,128)(2,1)} %copy-done.17, bf16[1024,3072]{1,0:T(8,128)(2,1)} %get-tuple-element.96.slope_ref, ...), custom_call_target="tpu_custom_call", output_to_operand_aliasing={{0}: (5, {}), {1}: (6, {})} | custom-call | flops 44999999488 | tf_op jit(solution)/shard_map/feed_back/pallas_call | solution.py:755
  351.6 15.7 %feed_back.6 = (bf16[1024,3072]{1,0:T(8,128)(2,1)}, bf16[2,1024,1152]{2,1,0:T(8,128)(2,1)}, bf16[256,2304]{1,0:T(8,128)(2,1)}) custom-call(s32[2]{0:T(128)} %get-tuple-element.162.where_ref, bf16[256,2304]{1,0:T(8,128)(2,1)} %copy-done.18, bf16[1024,3072]{1,0:T(8,128)(2,1)} %get-tuple-element.96.slope_ref, ...), custom_call_target="tpu_custom_call", output_to_operand_aliasing={{0}: (5, {}), {1}: (6, {})} | custom-call | flops 44999999488 | tf_op jit(solution)/shard_map/feed_back/pallas_call | solution.py:755
  371.1 16.2 %feed_back.7 = (bf16[1024,3072]{1,0:T(8,128)(2,1)}, bf16[2,1024,1152]{2,1,0:T(8,128)(2,1)}, f32[256,2304]{1,0:T(8,128)}) custom-call(s32[2]{0:T(128)} %get-tuple-element.161.where_ref.place_ref, bf16[256,2304]{1,0:T(8,128)(2,1)} %scaled.1.grad_ref, bf16[1024,3072]{1,0:T(8,128)(2,1)} %get-tuple-element.96.slope_ref, ...), custom_call_target="tpu_custom_call", output_to_operand_aliasing={{0}: (5, {}), {1}: (6, {})} | custom-call | flops 44999999488 | tf_op jit(solution)/shard_map/feed_back/pallas_call | solution.py:755
  387.3 7.6 %weight_grad.6.refs_0_ = bf16[1152,1536]{1,0:T(8,128)(2,1)} custom-call(bf16[2,1024,1152]{2,1,0:T(8,128)(2,1)} %get-tuple-element.108.left_ref, bf16[1024,1536]{1,0:T(8,128)(2,1)} %get-tuple-element.95.right_ref), custom_call_target="tpu_custom_call" | custom-call | flops 17999998976 | tf_op jit(solution)/shard_map/weight_grad/pallas_call | solution.py:142
  401.7 11.9 %weight_grad.7.refs_1_.refs_0_ = bf16[1152,3072]{1,0:T(8,128)(2,1)} custom-call(bf16[2,1024,1152]{2,1,0:T(8,128)(2,1)} %get-tuple-element.110.left_ref, bf16[1024,3072]{1,0:T(8,128)(2,1)} %get-tuple-element.111.right_ref, bf16[256,2304]{1,0:T(8,128)(2,1)} %get-tuple-element.109.refs_1_.refs_0_), custom_call_target="tpu_custom_call" | custom-call | flops 32999999488 | tf_op jit(solution)/shard_map/weight_grad/pallas_call | solution.py:142
  415.4 8.1 %weight_grad.8.refs_0_ = bf16[1152,1536]{1,0:T(8,128)(2,1)} custom-call(bf16[2,1024,1152]{2,1,0:T(8,128)(2,1)} %get-tuple-element.108.left_ref, bf16[1024,1536]{1,0:T(8,128)(2,1)} %get-tuple-element.95.right_ref, bf16[1152,1536]{1,0:T(8,128)(2,1)} %copy-done.6, bf16[1152,3072]{1,0:T(8,128)(2,1)} %weight_grad.7.refs_1_.refs_0_), custom_call_target="tpu_custom_call" | custom-call | flops 17999998976 | tf_op jit(solution)/shard_map/weight_grad/pallas_call | solution.py:142
  423.6 7.0 collective-permute-done.14.arrived_ref
  438.1 8.7 %spread.1 = (bf16[256,640]{1,0:T(8,128)(2,1)}, bf16[256,640]{1,0:T(8,128)(2,1)}, bf16[256,640]{1,0:T(8,128)(2,1)}, bf16[256,640]{1,0:T(8,128)(2,1)}, s32[1]{0:T(128)}) custom-call(bf16[256,2304]{1,0:T(8,128)(2,1)} %get-tuple-element.112.value_ref, bf16[2304,2560]{1,0:T(8,128)(2,1)} %all-gather.9.cloned.1.call-done.refs_4_.refs_2_.weight_ref), custom_call_target="tpu_custom_call" | custom-call | flops 24000000000 | tf_op jit(solution)/shard_map/spread/pallas_call | solution.py:840
  463.1 13.2 %weight_grad.9.refs_7_ = bf16[1152,3072]{1,0:T(8,128)(2,1)} custom-call(bf16[2,1024,1152]{2,1,0:T(8,128)(2,1)} %get-tuple-element.110.left_ref, bf16[1024,3072]{1,0:T(8,128)(2,1)} %get-tuple-element.111.right_ref, bf16[1152,3072]{1,0:T(8,128)(2,1)} %collective-permute-done.19.refs_0_, bf16[256,2304]{1,0:T(8,128)(2,1)} %fusion.14.refs_1_.refs_0_), custom_call_target="tpu_custom_call" | custom-call | flops 32999999488 | tf_op jit(solution)/shard_map/weight_grad/pallas_call | solution.py:142
  480.9 28.6 %attend_back.1.right_ref = bf16[1024,1920]{1,0:T(8,128)(2,1)} custom-call(s32[2]{0:T(128)} %pad_add_fusion.4.prefix_ref, bf16[1024,1920]{1,0:T(8,128)(2,1)} %get-tuple-element.88.qkv_ref, bf16[1024,640]{1,0:T(8,128)(2,1)} %get-tuple-element.89.refs_4_.refs_0_.out_ref, bf16[256,640]{1,0:T(8,128)(2,1)} %get-tuple-element.113.refs_0_, ...), custom_call_target="tpu_custom_call" | custom-call | flops 83999997952 | tf_op jit(solution)/shard_map/attend_back/pallas_call | solution.py:595
  520.0 9.5 %weight_grad.11.refs_1_.refs_0_ = bf16[1152,1920]{1,0:T(8,128)(2,1)} custom-call(bf16[2,1024,1152]{2,1,0:T(8,128)(2,1)} %get-tuple-element.120.left_ref, bf16[1024,1920]{1,0:T(8,128)(2,1)} %attend_back.1.right_ref, bf16[256,2304]{1,0:T(8,128)(2,1)} %copy-done.16, bf16[256,2304]{1,0:T(8,128)(2,1)} %copy-done.13), custom_call_target="tpu_custom_call" | custom-call | flops 24000000000 | tf_op jit(solution)/shard_map/weight_grad/pallas_call | solution.py:142
  538.9 7.9 %fusion.4.one_ref = f32[256,2304]{1,0:T(8,128)} fusion(bf16[2304,1920]{1,0:T(8,128)(2,1)} %all-gather.5.cloned.1.call-done.w_ref, bf16[1024,1920]{1,0:T(8,128)(2,1)} %attend_back.1.right_ref, s32[]{:T(128)S(6)} %select_n.68), kind=kOutput, calls=%fused_computation.4 | convolution fusion | flops 2264924160 | bytes 12189700 | tf_op jit(solution)/shard_map/dot_general | solution.py:39
  563.2 10.9 %scatter_chip.3 = (bf16[2,144,1920]{2,1,0:T(8,128)(2,1)}, bf16[2,144,1920]{2,1,0:T(8,128)(2,1)}, bf16[2,144,1920]{2,1,0:T(8,128)(2,1)}, bf16[2,144,1920]{2,1,0:T(8,128)(2,1)}, s32[1]{0:T(128)}) custom-call(s32[2]{0:T(128)} %pad_add_fusion.5.where_ref, bf16[2,1024,1152]{2,1,0:T(8,128)(2,1)} %get-tuple-element.120.left_ref, ...), custom_call_target="tpu_custom_call" | custom-call | flops 30000001024 | tf_op jit(solution)/shard_map/scatter_chip/pallas_call | solution.py:185
  576.7 7.9 %fusion.2.one_ref = f32[256,2304]{1,0:T(8,128)} fusion(bf16[2304,1920]{1,0:T(8,128)(2,1)} %all-gather.5.cloned.1.call-done.w_ref, bf16[1024,1920]{1,0:T(8,128)(2,1)} %attend_back.1.right_ref, s32[]{:T(128)S(6)} %select_n.70), kind=kOutput, calls=%fused_computation.2 | convolution fusion | flops 2264924160 | bytes 12189700 | tf_op jit(solution)/shard_map/dot_general | solution.py:39
  589.1 8.0 %fusion.refs_3_.term_ref = f32[256,2304]{1,0:T(8,128)} fusion(bf16[2304,1920]{1,0:T(8,128)(2,1)} %all-gather.5.cloned.1.call-done.w_ref, bf16[1024,1920]{1,0:T(8,128)(2,1)} %attend_back.1.right_ref, s32[]{:T(128)S(6)} %select_n.71), kind=kOutput, calls=%fused_computation | convolution fusion | flops 2264924160 | bytes 12189700 | tf_op jit(solution)/shard_map/dot_general | solution.py:39
  615.2 9.3 %collective-permute-done.33.refs_3_ = bf16[144,2560]{1,0:T(8,128)(2,1)S(1)} collective-permute-done((bf16[144,2560]{1,0:T(8,128)(2,1)}, bf16[144,2560]{1,0:T(8,128)(2,1)S(1)}, u32[]{:S(2)}, u32[]{:S(2)}) %collective-permute-start.33) | collective-permute-done | bytes 737312 | tf_op jit(solution)/shard_map/ppermute | solution.py:94
  638.9 18.3 %collective-permute-done.31.refs_2_.arrived_ref = bf16[256,2304]{1,0:T(8,128)(2,1)S(1)} collective-permute-done((bf16[256,2304]{1,0:T(8,128)(2,1)}, bf16[256,2304]{1,0:T(8,128)(2,1)S(1)}, u32[]{:S(2)}, u32[]{:S(2)}) %collective-permute-start.31) | collective-permute-done | bytes 1179680 | tf_op jit(solution)/shard_map/ppermute | solution.py:56
  (240 shorter events, 221.9 us)
Async XLA Ops:
  7.2 65.6 %all-gather.5.cloned.1.call-start = ((), (), s32[]{:S(2)}) async-start(), calls=%async_computation.2 | async-start | bytes 9953280 | tf_op jit(solution)/shard_map/all_gather | solution.py:98
  9.7 160.5 %all-gather.7.cloned.1.call-start = ((), (), s32[]{:S(2)}) async-start(), calls=%async_computation.3 | async-start | bytes 15925248 | tf_op jit(solution)/shard_map/all_gather | solution.py:98
  12.7 227.2 %all-gather.9.cloned.1.call-start = ((), (), s32[]{:S(2)}) async-start(), calls=%async_computation.4 | async-start | bytes 13271040 | tf_op jit(solution)/shard_map/all_gather | solution.py:98
  12.8 31.1 %collective-permute-start = (bf16[256,2304]{1,0:T(8,128)(2,1)S(1)}, bf16[256,2304]{1,0:T(8,128)(2,1)S(1)}, u32[]{:S(2)}, u32[]{:S(2)}) collective-permute-start(bf16[256,2304]{1,0:T(8,128)(2,1)S(1)} %copy-done.8), channel_id=1, source_target_pairs={{0,1},{1,2},{2,3},{3,0},{4,5},{5,6},{6,7},{7,4},{8,9},{9,10},{10,1... | collective-permute-start | bytes 3538952 | tf_op jit(solution)/shard_map/ppermute | solution.py:56
  72.8 29.4 %collective-permute-start.2 = (bf16[256,2304]{1,0:T(8,128)(2,1)S(1)}, bf16[256,2304]{1,0:T(8,128)(2,1)S(1)}, u32[]{:S(2)}, u32[]{:S(2)}) collective-permute-start(bf16[256,2304]{1,0:T(8,128)(2,1)S(1)} %collective-permute-done.1.x_ref.refs_2_), channel_id=1, source_target_pairs={{0,1},{1,2},{2,3},{3,0},{4,5},{5,6},{6,7},{7,4},{8,9},{9,10},{10,1... | collective-permute-start | bytes 3538952 | tf_op jit(solution)/shard_map/ppermute | solution.py:56
  103.1 33.1 %collective-permute-start.5 = (bf16[288,640]{1,0:T(8,128)(2,1)}, bf16[288,640]{1,0:T(8,128)(2,1)S(1)}, u32[]{:S(2)}, u32[]{:S(2)}) collective-permute-start(bf16[288,640]{1,0:T(8,128)(2,1)} %gate.9.refs_0_), channel_id=1, source_target_pairs={{0,3},{1,0},{2,1},{3,2},{4,7},{5,4},{6,5},{7,6},{8,11},{9,8},{10,9... | collective-permute-start | bytes 1105928 | tf_op jit(solution)/shard_map/ppermute | solution.py:80
  106.9 29.3 %collective-permute-start.4 = (bf16[288,640]{1,0:T(8,128)(2,1)}, bf16[288,640]{1,0:T(8,128)(2,1)S(1)}, u32[]{:S(2)}, u32[]{:S(2)}) collective-permute-start(bf16[288,640]{1,0:T(8,128)(2,1)} %gate.9.refs_0_), channel_id=1, source_target_pairs={{0,2},{1,3},{2,0},{3,1},{4,6},{5,7},{6,4},{7,5},{8,10},{9,11},{10,... | collective-permute-start | bytes 1105928 | tf_op jit(solution)/shard_map/ppermute | solution.py:80
  106.9 29.3 %collective-permute-start.3 = (bf16[288,640]{1,0:T(8,128)(2,1)}, bf16[288,640]{1,0:T(8,128)(2,1)S(1)}, u32[]{:S(2)}, u32[]{:S(2)}) collective-permute-start(bf16[288,640]{1,0:T(8,128)(2,1)} %gate.9.refs_0_), channel_id=1, source_target_pairs={{0,1},{1,2},{2,3},{3,0},{4,5},{5,6},{6,7},{7,4},{8,9},{9,10},{10,1... | collective-permute-start | bytes 1105928 | tf_op jit(solution)/shard_map/ppermute | solution.py:80
  139.8 30.4 %collective-permute-start.6 = (bf16[1024,640]{1,0:T(8,128)(2,1)}, bf16[1024,640]{1,0:T(8,128)(2,1)S(1)}, u32[]{:S(2)}, u32[]{:S(2)}) collective-permute-start(bf16[1024,640]{1,0:T(8,128)(2,1)} %gate.10), channel_id=1, source_target_pairs={{0,1},{1,2},{2,3},{3,0},{4,5},{5,6},{6,7},{7,4},{8,9},{9,10},{10,1... | collective-permute-start | bytes 3932168 | tf_op jit(solution)/shard_map/ppermute | solution.py:56
  171.3 133.0 %all-gather.11.cloned.1.call-start = ((), (), s32[]{:S(2)}) async-start(), calls=%async_computation.5 | async-start | bytes 7962624 | tf_op jit(solution)/shard_map/all_gather | solution.py:98
  171.3 29.7 %collective-permute-start.7 = (bf16[1024,640]{1,0:T(8,128)(2,1)}, bf16[1024,640]{1,0:T(8,128)(2,1)S(1)}, u32[]{:S(2)}, u32[]{:S(2)}) collective-permute-start(bf16[1024,640]{1,0:T(8,128)(2,1)} %copy-done), channel_id=1, source_target_pairs={{0,1},{1,2},{2,3},{3,0},{4,5},{5,6},{6,7},{7,4},{8,9},{9,10},{10,1... | collective-permute-start | bytes 3932168 | tf_op jit(solution)/shard_map/ppermute | solution.py:56
  213.9 450.4 %reduce-scatter.5.cloned.1.call-start = ((), (), s32[]{:S(2)}) async-start(), calls=%async_computation.7 | async-start | bytes 4423680 | tf_op jit(solution)/shard_map/reduce_scatter | solution.py:298
  242.4 30.6 %collective-permute-start.9 = (bf16[256,2304]{1,0:T(8,128)(2,1)}, bf16[256,2304]{1,0:T(8,128)(2,1)S(1)}, u32[]{:S(2)}, u32[]{:S(2)}) collective-permute-start(bf16[256,2304]{1,0:T(8,128)(2,1)} %scaled.1.grad_ref), channel_id=1, source_target_pairs={{0,1},{1,2},{2,3},{3,0},{4,5},{5,6},{6,7},{7,4},{8,9},{9,10},{10,1... | collective-permute-start | bytes 3538952 | tf_op jit(solution)/shard_map/ppermute | solution.py:56
  274.3 29.9 %collective-permute-start.10 = (bf16[256,2304]{1,0:T(8,128)(2,1)}, bf16[256,2304]{1,0:T(8,128)(2,1)S(1)}, u32[]{:S(2)}, u32[]{:S(2)}) collective-permute-start(bf16[256,2304]{1,0:T(8,128)(2,1)} %gate.12), channel_id=1, source_target_pairs={{0,1},{1,2},{2,3},{3,0},{4,5},{5,6},{6,7},{7,4},{8,9},{9,10},{10,1... | collective-permute-start | bytes 3538952 | tf_op jit(solution)/shard_map/ppermute | solution.py:56
  304.2 30.7 %collective-permute-start.11 = (bf16[256,2304]{1,0:T(8,128)(2,1)S(1)}, bf16[256,2304]{1,0:T(8,128)(2,1)S(1)}, u32[]{:S(2)}, u32[]{:S(2)}) collective-permute-start(bf16[256,2304]{1,0:T(8,128)(2,1)S(1)} %collective-permute-done.10.refs_0_.grad_ref), channel_id=1, source_target_pairs={{0,1},{1,2},{2,3},{3,0},{4,5},{5,6},{6,7},{7,4},{8,9},{9,10},{10,1... | collective-permute-start | bytes 3538952 | tf_op jit(solution)/shard_map/ppermute | solution.py:56
  320.9 46.4 %collective-permute-start.12 = (bf16[256,2304]{1,0:T(8,128)(2,1)}, bf16[256,2304]{1,0:T(8,128)(2,1)S(1)}, u32[]{:S(2)}, u32[]{:S(2)}) collective-permute-start(bf16[256,2304]{1,0:T(8,128)(2,1)} %get-tuple-element.104), channel_id=1, source_target_pairs={{0,1},{1,2},{2,3},{3,0},{4,5},{5,6},{6,7},{7,4},{8,9},{9,10},{10,1... | collective-permute-start | bytes 3538952 | tf_op jit(solution)/shard_map/ppermute | solution.py:56
  447.5 246.7 %reduce-scatter.3.cloned.1.call-start = ((), (), s32[]{:S(2)}) async-start(), calls=%async_computation.6 | async-start | bytes 8847360 | tf_op jit(solution)/shard_map/reduce_scatter | solution.py:298
  449.7 29.1 %collective-permute-start.17 = (bf16[256,640]{1,0:T(8,128)(2,1)S(1)}, bf16[256,640]{1,0:T(8,128)(2,1)S(1)}, u32[]{:S(2)}, u32[]{:S(2)}) collective-permute-start(bf16[256,640]{1,0:T(8,128)(2,1)S(1)} %copy-done.36), channel_id=1, source_target_pairs={{0,2},{1,3},{2,0},{3,1},{4,6},{5,7},{6,4},{7,5},{8,10},{9,11},{10,... | collective-permute-start | bytes 983048 | tf_op jit(solution)/shard_map/ppermute | solution.py:80
  463.0 66.4 %collective-permute-start.22 = (bf16[1152,2560]{1,0:T(8,128)(2,1)}, bf16[1152,2560]{1,0:T(8,128)(2,1)}, u32[]{:S(2)}, u32[]{:S(2)}) collective-permute-start(bf16[1152,2560]{1,0:T(8,128)(2,1)} %weight_grad.10.refs_8_), channel_id=1, source_target_pairs={{0,4},{4,0},{8,12},{12,8},{16,20},{20,16},{24,28},{28,24},{1,5},{5... | collective-permute-start | bytes 17694728 | tf_op jit(solution)/shard_map/ppermute | solution.py:94
  480.3 38.7 %collective-permute-start.20 = (bf16[256,2304]{1,0:T(8,128)(2,1)}, bf16[256,2304]{1,0:T(8,128)(2,1)S(1)}, u32[]{:S(2)}, u32[]{:S(2)}) collective-permute-start(bf16[256,2304]{1,0:T(8,128)(2,1)} %gate.15), channel_id=1, source_target_pairs={{0,1},{1,2},{2,3},{3,0},{4,5},{5,6},{6,7},{7,4},{8,9},{9,10},{10,1... | collective-permute-start | bytes 3538952 | tf_op jit(solution)/shard_map/ppermute | solution.py:56
  516.1 30.8 %collective-permute-start.23 = (bf16[256,2304]{1,0:T(8,128)(2,1)S(1)}, bf16[256,2304]{1,0:T(8,128)(2,1)S(1)}, u32[]{:S(2)}, u32[]{:S(2)}) collective-permute-start(bf16[256,2304]{1,0:T(8,128)(2,1)S(1)} %fusion.6.refs_0_), channel_id=1, source_target_pairs={{0,1},{1,2},{2,3},{3,0},{4,5},{5,6},{6,7},{7,4},{8,9},{9,10},{10,1... | collective-permute-start | bytes 3538952 | tf_op jit(solution)/shard_map/ppermute | solution.py:56
  529.5 33.7 %collective-permute-start.21 = (bf16[1152,1920]{1,0:T(8,128)(2,1)}, bf16[1152,1920]{1,0:T(8,128)(2,1)}, u32[]{:S(2)}, u32[]{:S(2)}) collective-permute-start(bf16[1152,1920]{1,0:T(8,128)(2,1)} %weight_grad.11.refs_1_.refs_0_), channel_id=1, source_target_pairs={{0,4},{4,0},{8,12},{12,8},{16,20},{20,16},{24,28},{28,24},{1,5},{5... | collective-permute-start | bytes 13271048 | tf_op jit(solution)/shard_map/ppermute | solution.py:94
  536.9 70.2 %collective-permute-start.28 = (bf16[2,144,2560]{2,1,0:T(8,128)(2,1)}, bf16[2,144,2560]{2,1,0:T(8,128)(2,1)}, u32[]{:S(2)}, u32[]{:S(2)}) collective-permute-start(bf16[2,144,2560]{2,1,0:T(8,128)(2,1)} %get-tuple-element.122.refs_1_), channel_id=1, source_target_pairs={{0,16},{4,20},{8,24},{12,28},{16,0},{20,4},{24,8},{28,12},{1,17},{... | collective-permute-start | bytes 4423688 | tf_op jit(solution)/shard_map/ppermute | solution.py:94
  538.2 59.6 %collective-permute-start.29 = (bf16[2,144,2560]{2,1,0:T(8,128)(2,1)}, bf16[2,144,2560]{2,1,0:T(8,128)(2,1)}, u32[]{:S(2)}, u32[]{:S(2)}) collective-permute-start(bf16[2,144,2560]{2,1,0:T(8,128)(2,1)} %get-tuple-element.123.refs_2_), channel_id=1, source_target_pairs={{0,8},{4,12},{8,0},{12,4},{16,24},{20,28},{24,16},{28,20},{1,9},{5... | collective-permute-start | bytes 4423688 | tf_op jit(solution)/shard_map/ppermute | solution.py:94
  551.4 33.2 %collective-permute-start.24 = (bf16[256,2304]{1,0:T(8,128)(2,1)}, bf16[256,2304]{1,0:T(8,128)(2,1)S(1)}, u32[]{:S(2)}, u32[]{:S(2)}) collective-permute-start(bf16[256,2304]{1,0:T(8,128)(2,1)} %get-tuple-element.124.refs_0_), channel_id=1, source_target_pairs={{0,1},{1,2},{2,3},{3,0},{4,5},{5,6},{6,7},{7,4},{8,9},{9,10},{10,1... | collective-permute-start | bytes 3538952 | tf_op jit(solution)/shard_map/ppermute | solution.py:56
  561.2 50.1 %collective-permute-start.27 = (bf16[256,2304]{1,0:T(8,128)(2,1)}, bf16[256,2304]{1,0:T(8,128)(2,1)}, u32[]{:S(2)}, u32[]{:S(2)}) collective-permute-start(bf16[256,2304]{1,0:T(8,128)(2,1)} %get-tuple-element.126.refs_1_), channel_id=1, source_target_pairs={{0,1},{1,2},{2,3},{3,0},{4,5},{5,6},{6,7},{7,4},{8,9},{9,10},{10,1... | collective-permute-start | bytes 3538952 | tf_op jit(solution)/shard_map/ppermute | solution.py:56
  574.7 61.0 %collective-permute-start.26 = (bf16[2,144,1920]{2,1,0:T(8,128)(2,1)}, bf16[2,144,1920]{2,1,0:T(8,128)(2,1)}, u32[]{:S(2)}, u32[]{:S(2)}) collective-permute-start(bf16[2,144,1920]{2,1,0:T(8,128)(2,1)} %get-tuple-element.128.refs_0_), channel_id=1, source_target_pairs={{0,16},{4,20},{8,24},{12,28},{16,0},{20,4},{24,8},{28,12},{1,17},{... | collective-permute-start | bytes 3317768 | tf_op jit(solution)/shard_map/ppermute | solution.py:94
  584.5 48.0 %collective-permute-start.30 = (bf16[2,144,1920]{2,1,0:T(8,128)(2,1)}, bf16[2,144,1920]{2,1,0:T(8,128)(2,1)}, u32[]{:S(2)}, u32[]{:S(2)}) collective-permute-start(bf16[2,144,1920]{2,1,0:T(8,128)(2,1)} %get-tuple-element.129.refs_1_), channel_id=1, source_target_pairs={{0,8},{4,12},{8,0},{12,4},{16,24},{20,28},{24,16},{28,20},{1,9},{5... | collective-permute-start | bytes 3317768 | tf_op jit(solution)/shard_map/ppermute | solution.py:94
  597.8 41.1 %collective-permute-start.25 = (bf16[256,2304]{1,0:T(8,128)(2,1)}, bf16[256,2304]{1,0:T(8,128)(2,1)}, u32[]{:S(2)}, u32[]{:S(2)}) collective-permute-start(bf16[256,2304]{1,0:T(8,128)(2,1)} %get-tuple-element.131.refs_0_), channel_id=1, source_target_pairs={{0,1},{1,2},{2,3},{3,0},{4,5},{5,6},{6,7},{7,4},{8,9},{9,10},{10,1... | collective-permute-start | bytes 3538952 | tf_op jit(solution)/shard_map/ppermute | solution.py:56
  624.5 32.7 %collective-permute-start.31 = (bf16[256,2304]{1,0:T(8,128)(2,1)}, bf16[256,2304]{1,0:T(8,128)(2,1)S(1)}, u32[]{:S(2)}, u32[]{:S(2)}) collective-permute-start(bf16[256,2304]{1,0:T(8,128)(2,1)} %get-tuple-element.138.refs_0_), channel_id=1, source_target_pairs={{0,1},{1,2},{2,3},{3,0},{4,5},{5,6},{6,7},{7,4},{8,9},{9,10},{10,1... | collective-permute-start | bytes 3538952 | tf_op jit(solution)/shard_map/ppermute | solution.py:56
  667.0 30.7 %collective-permute-start.36 = (bf16[288,640]{1,0:T(8,128)(2,1)S(1)}, bf16[288,640]{1,0:T(8,128)(2,1)}, u32[]{:S(2)}, u32[]{:S(2)}) collective-permute-start(bf16[288,640]{1,0:T(8,128)(2,1)S(1)} %copy-done.31), channel_id=1, source_target_pairs={{0,3},{1,0},{2,1},{3,2},{4,7},{5,4},{6,5},{7,6},{8,11},{9,8},{10,9... | collective-permute-start | bytes 1105928 | tf_op jit(solution)/shard_map/ppermute | solution.py:80
  667.0 30.7 %collective-permute-start.37 = (bf16[288,640]{1,0:T(8,128)(2,1)S(1)}, bf16[288,640]{1,0:T(8,128)(2,1)}, u32[]{:S(2)}, u32[]{:S(2)}) collective-permute-start(bf16[288,640]{1,0:T(8,128)(2,1)S(1)} %copy-done.30), channel_id=1, source_target_pairs={{0,2},{1,3},{2,0},{3,1},{4,6},{5,7},{6,4},{7,5},{8,10},{9,11},{10,... | collective-permute-start | bytes 1105928 | tf_op jit(solution)/shard_map/ppermute | solution.py:80
  (61 other events, 481.5 us)
Sparse Core Ops, SparseCore 0:
  10.5 59.0 all-gather.4
  72.0 78.7 all-gather.6
  171.4 68.4 all-gather.8
  241.6 48.8 all-gather.10
  447.6 35.5 reduce-scatter.4
  485.4 76.5 reduce-scatter.2
